TPU v7x, 256 devices: a whole 4x4x8 slice. The times are simulated.
256 devices in a mesh: group: 8 (over x, core), tensor: 32 (over y, z).
Axes of the slice: x: 4, y: 4, z: 8, core: 2. Of those that a mesh axis runs over, the one named last changes fastest.
Arguments:
- tokens: bfloat16 [8192, 8192], P(('group', 'tensor')), parts along dimension 0, may hold values from -6 to 6
- base_weight: bfloat16 [8192, 8192], P(None, 'tensor'), may hold values from -0.0625 to 0.0625
- down_pool: bfloat16 [512, 64, 8192], P(('group', 'tensor')), parts along dimension 0, may hold values from -0.0625 to 0.0625
- up_pool: bfloat16 [512, 64, 8192], P(('group', 'tensor')), parts along dimension 0, may hold values from -0.75 to 0.75
- slot_of: int32 [512], P('group'), parts along dimension 0, may hold values from 0 to 63, each once
- requested: int32 [32], P('group'), parts along dimension 0, may hold values from 0 to 63, as said below
- row_adapter: int32 [8192], P(('group', 'tensor')), parts along dimension 0, may hold values from 0 to 3
Outputs:
- projected: bfloat16 [8192, 8192], P('group', 'tensor'), parts along dimension 0
There are 8 independent parts, one for each index of `group`. A program takes and returns all parts, laid end to end along the dimension named above; an argument that names none is the same for every part. Nothing has to cross between parts.
Inputs may be any that keep to these rules, and one draw needn't show every extreme that they name: `requested`: the 4 ids are distinct. `slot_of`: A permutation of the adapter ids.
All inputs are finite; a program needn't handle non-finite values.
Results may differ from a plain program's by a relative error of at most 0.0046.
Values may be sent and summed in bfloat16 or wider, within the bound.
No kernel may reach another device: no remote copies, remote signals or barrier semaphores. Data moves between devices by JAX's collectives and lax.ppermute only.
A program may use at most 128 MiB of HBM per device.

v0:
```python
import jax
import jax.numpy as jnp
from jax import lax
from jax.sharding import PartitionSpec as P

adapter_scale = 2.0


def from_root(value, axis, root):
    mine = lax.axis_index(axis) == root
    return lax.psum(jnp.where(mine, value, jnp.zeros_like(value)), axis)


def select_rows(products, adapter_ids, count_new, low_rank):
    onehot = (adapter_ids[:, None] == jnp.arange(count_new, dtype=jnp.int32)[None, :]).astype(
        jnp.float32
    )
    shaped = products.reshape(products.shape[0], count_new, low_rank) * onehot[:, :, None]
    return shaped.reshape(products.shape[0], count_new * low_rank).astype(jnp.bfloat16)


def per_device(tokens, base_weight, down_pool, up_pool, slot_of, requested, row_adapter):
    width_out = base_weight.shape[1]
    low_rank = down_pool.shape[1]
    total_width = down_pool.shape[2]
    held_slots = down_pool.shape[0]
    count_new = requested.shape[0]
    pool_rows = slot_of[requested]
    device_index = lax.axis_index("tensor")
    down_list = []
    up_list = []
    for request in range(count_new):
        home_device = pool_rows[request] // held_slots
        local_slot = pool_rows[request] % held_slots
        down_piece = lax.dynamic_index_in_dim(down_pool, local_slot, 0, keepdims=False)
        up_piece = lax.dynamic_index_in_dim(up_pool, local_slot, 0, keepdims=False)
        down_got, up_got = (
            from_root(down_piece, "tensor", home_device),
            from_root(up_piece, "tensor", home_device),
        )
        offset = device_index * width_out
        up_list.append(lax.dynamic_slice_in_dim(up_got, offset, width_out, 1))
        down_list.append(down_got)
    down_cat = jnp.stack(down_list).reshape(count_new * low_rank, total_width)
    up_cat = jnp.stack(up_list).reshape(count_new * low_rank, width_out)
    piece = lax.all_gather(tokens, "tensor", axis=0, tiled=True)
    base_part = jnp.dot(piece, base_weight, preferred_element_type=jnp.float32)
    down_section = lax.dot_general(
        piece, down_cat, (((1,), (1,)), ((), ())), preferred_element_type=jnp.float32
    )
    joined = jnp.concatenate([base_part, down_section], axis=1)
    frozen_output = joined[:, :width_out]
    adapter_ids = lax.all_gather(row_adapter, "tensor", axis=0, tiled=True)
    reduced_rows = select_rows(joined[:, width_out:], adapter_ids, count_new, low_rank)
    adapter_update = jnp.dot(reduced_rows, up_cat, preferred_element_type=jnp.float32)
    return (frozen_output + adapter_scale * adapter_update).astype(jnp.bfloat16)


def solution(mesh):
    placed = (
        P(("group", "tensor"), None),
        P(None, "tensor"),
        P(("group", "tensor"), None, None),
        P(("group", "tensor"), None, None),
        P("group"),
        P("group"),
        P(("group", "tensor")),
    )
    return jax.shard_map(
        per_device, mesh=mesh, in_specs=placed, out_specs=P("group", "tensor"), check_vma=False
    )
```

profile of v0, /device:TPU:1, one launch (start us, length us, event | category | flops | bytes accessed | tf_op | source)
XLA Modules:
  0.0 413.9 jit_solution(13324159906297187354)
XLA Ops:
  6.5 0.0 copy-start
  6.5 0.0 all-reduce.4.cloned.1.call-start
  6.5 0.7 compare_select_fusion
  7.2 0.0 copy-done
  7.2 0.6 gather_fusion
  7.9 0.7 fusion.5
  18.5 0.0 copy-start.1
  18.5 4.6 %dynamic-slice_select_fusion.3 = (bf16[1,64,8192]{2,1,0:T(8,128)(2,1)}, bf16[1,64,8192]{2,1,0:T(8,128)(2,1)}, bf16[1,64,8192]{2,1,0:T(8,128)(2,1)}, bf16[1,64,8192]{2,1,0:T(8,128)(2,1)}) fusion(bf16[2,64,8192]{2,1,0:T(8,128)(2,1)} %param.9, s32[]{:T(128)S(6)} %select_n.128, pred[]{:T(512)S(6)} %eq.38, s32[]{:T(128)S(6)} %select_n.134, pred[]{:T(512)S(6)} %eq.39, ...), kind=kLoop, calls=%fused_computation.15 | loop fusion | flops 2097152 | bytes 8388628 | tf_op jit(solution)/shard_map/jit(_where)/select_n | solution.py:11
  23.1 0.0 copy-done.1
  23.1 2.0 select_bitcast_fusion.3
  25.1 0.0 copy-start.3
  25.1 0.0 copy-start.2
  25.1 0.0 all-reduce.4.cloned.1.call-update
  25.1 0.0 all-gather.2.cloned.1.call-start
  25.2 0.7 all-gather.2.cloned.1.call-update
  25.9 0.0 copy-done.3
  25.9 0.6 dynamic-slice
  27.1 0.0 copy-done.2
  27.2 0.2 dynamic-update-slice
  27.4 20.5 %all-reduce = s32[1024]{0:T(1024)S(1)} all-reduce(s32[1024]{0:T(1024)S(1)} %dynamic-update-slice), channel_id=1, replica_groups=mesh['group'=8,'tensor'=32] {'tensor'}, use_global_device_ids=true, to_apply=%add | all-reduce | flops 1024 | bytes 8192
  48.0 195.4 %all-reduce.4.cloned.1.call-done = (bf16[64,8192]{1,0:T(8,128)(2,1)}, bf16[64,8192]{1,0:T(8,128)(2,1)}, bf16[64,8192]{1,0:T(8,128)(2,1)}, bf16[64,8192]{1,0:T(8,...) async-done(((bf16[64,8192]{1,0:T(8,128)(2,1)}, ...) | async-done | bytes 8388624 | tf_op jit(solution)/shard_map/psum | solution.py:11
  243.3 0.8 dynamic-slice_bitcast_fusion.2
  244.1 0.8 dynamic-slice_bitcast_fusion
  244.9 3.7 pad_maximum_fusion
  248.6 136.3 %all-gather.2.cloned.1.call-done = bf16[1024,8192]{1,0:T(8,128)(2,1)} async-done(((bf16[32,8192]{1,0:T(8,128)(2,1)}), bf16[1024,8192]{1,0:T(8,128)(2,1)}) %all-gather.2.cloned.1.call-update) | async-done | bytes 16777232 | tf_op jit(solution)/shard_map/all_gather | solution.py:46
  384.9 9.3 %fusion.6 = f32[1024,256]{1,0:T(8,128)S(1)} fusion(bf16[1024,8192]{1,0:T(8,128)(2,1)} %all-gather.2.cloned.1.call-done, bf16[8192,256]{1,0:T(8,128)(2,1)} %param.8), kind=kOutput, calls=%fused_computation.26 | convolution fusion | flops 4294967296 | bytes 22020096 | tf_op jit(solution)/shard_map/dot_general | solution.py:47
  394.3 0.1 mul.23
  394.4 12.7 %fusion.2 = bf16[1024,256]{1,0:T(8,128)(2,1)} fusion(f32[1024,256]{1,0:T(8,128)S(1)} %fusion.6, bf16[256,256]{1,0:T(8,128)(2,1)S(1)} %bitcast.39, f32[1024,256]{0,1:T(8,128)S(1)} %bitcast.38, bf16[256,8192]{1,0:T(8,128)(2,1)} %bitcast.37, bf16[1024,8192]{1,0:T(8,128)(2,1)} %all-gather.2.cloned.1.call-done), kind=kOutput, calls=%fused_computation.6 | convolution fusion | flops 4430495744 | bytes 23724032 | tf_op jit(solution)/shard_map/dot_general | solution.py:55
  (4 shorter events, 0.0 us)
Async XLA Ops:
  6.5 0.7 copy-start
  6.5 236.8 %all-reduce.4.cloned.1.call-start = ((), (), s32[]{:S(2)}) async-start(), calls=%async_computation.1 | async-start | bytes 16777216 | tf_op jit(solution)/shard_map/psum | solution.py:11
  18.5 4.6 %copy-start.1 = (bf16[2,64,8192]{2,1,0:T(8,128)(2,1)S(1)}, bf16[2,64,8192]{2,1,0:T(8,128)(2,1)}, u32[]{:S(2)}) copy-start(bf16[2,64,8192]{2,1,0:T(8,128)(2,1)} %param.10) | copy-start | bytes 6291460
  25.1 0.8 copy-start.3
  25.1 2.0 copy-start.2
  25.1 359.8 %all-gather.2.cloned.1.call-start = ((), (), s32[]{:S(2)}) async-start(), calls=%async_computation | async-start | bytes 17301504 | tf_op jit(solution)/shard_map/all_gather | solution.py:46
Sparse Core Ops, SparseCore 0:
  25.2 218.0 all-reduce.3
  245.9 138.9 all-gather.1
where the time goes:
time: 414 us
  waiting for transfers between devices  332 us (80%)
  between operations  24.1 us (6%)
  matrix products  22 us (5%)
  blocking collectives  20.5 us (5%)
  other arithmetic  11 us (3%)
    psum x1, waiting for transfers between devices, from_root(): return lax.psum(jnp.where(mine, value, jnp.zeros_like(value)), axis)  195 us
    all_gather x1, waiting for transfers between devices, per_device(): piece = lax.all_gather(tokens, 'tensor', axis=0, tiled=True)  136 us
    unnamed x1, blocking collectives  20.5 us
    dot_general x1, matrix products, per_device(): jnp.dot(reduced_rows, up_cat, preferred_element_type=jnp.float32)  12.7 us
    dot_general x1, matrix products, per_device(): base_part = jnp.dot(piece, base_weight, preferred_element_type=jnp.float32)  9.31 us
  transfers between devices with their start and end apart: 2, of which 2 were waited for; matrix products, arithmetic and copies ran while one was open for 1% of the time, Pallas kernels for 0%

commit v1 on v0

v1 whole, which is shorter than its diff:
```python
import jax
import jax.numpy as jnp
from jax import lax
from jax.sharding import Mesh, PartitionSpec as P

adapter_scale = 2.0


def swap(value, axis):
    return lax.all_to_all(value, axis, split_axis=0, concat_axis=0, tiled=True)


def spread(value, axis, count):
    return swap(jnp.broadcast_to(value[None], (count,) + value.shape), axis)


def after(value, *earlier):
    return lax.optimization_barrier((value,) + earlier)[0]


def per_device(nx, nc, ny, nz, tokens, base_weight, down_pool, up_pool, slot_of, requested, row_adapter):
    rows, width = tokens.shape
    width_out = base_weight.shape[1]
    held, rank, _ = down_pool.shape
    count_new = requested.shape[0]
    part = width // ny
    sub = part // (nx * nc)
    nt = ny * nz
    x, core, z = lax.axis_index("x"), lax.axis_index("core"), lax.axis_index("z")

    pool_rows = slot_of[requested]
    home, local = pool_rows // held, pool_rows % held
    home_y, home_z = home // nz, home % nz

    mine = swap(tokens.reshape(rows, ny, part).transpose(1, 0, 2), "y")
    gathered = lax.all_gather(mine.reshape(ny * rows, part), "z", axis=0, tiled=True)

    ids = spread(row_adapter, ("y", "z"), nt).reshape(ny, nz, rows)

    piece = base_weight.reshape(ny, nc * nx, sub, width_out)
    piece = lax.dynamic_index_in_dim(piece, core * nx + x, 1, keepdims=False)
    piece = swap(piece, "y").transpose(1, 0, 2).reshape(sub, ny * width_out)
    piece = spread(piece, "x", nx).reshape(nx * sub, ny * width_out)
    weight = spread(piece, "core", nc).reshape(part, ny * width_out)

    down = swap(down_pool.reshape(held, rank, ny, part).transpose(2, 0, 1, 3), "y")
    down = down.reshape(ny * held, rank, part)
    down_cat = jnp.concatenate(
        [lax.dynamic_index_in_dim(down, home_y[s] * held + local[s], 0, keepdims=False) for s in range(count_new)]
    )

    up = swap(up_pool.reshape(held, rank, ny, part).transpose(2, 0, 1, 3), "y")
    up = up.reshape(ny * held, rank, nz, width_out)
    up = jnp.stack(
        [lax.dynamic_index_in_dim(up, home_y[s] * held + local[s], 0, keepdims=False) for s in range(count_new)]
    )
    up = swap(up.transpose(2, 0, 1, 3), "z")
    up_cat = jnp.concatenate(
        [lax.dynamic_index_in_dim(up[:, s], home_z[s], 0, keepdims=False) for s in range(count_new)]
    )

    base = jnp.stack(
        [
            jnp.dot(gathered, weight[:, k * width_out : (k + 1) * width_out], preferred_element_type=jnp.float32).astype(
                jnp.bfloat16
            )
            for k in range(ny)
        ]
    )
    base = swap(base, "y")

    products = lax.dot_general(gathered, down_cat, (((1,), (1,)), ((), ())), preferred_element_type=jnp.float32)
    products = products.reshape(nz, ny, rows, count_new, rank).transpose(1, 0, 2, 3, 4)
    wanted = (ids[..., None] == jnp.arange(count_new, dtype=jnp.int32)) & (home_z == z)
    chosen = jnp.sum(jnp.where(wanted[..., None], products, 0.0), axis=3)
    chosen = swap(chosen.reshape(nt, rows, rank), ("y", "z"))
    lowered = jnp.sum(chosen, axis=0).astype(jnp.bfloat16)
    lowered = spread(lowered, ("y", "z"), nt)
    onehot = ids.reshape(nt, rows)[..., None] == jnp.arange(count_new, dtype=jnp.int32)
    lowered = jnp.where(onehot[..., None], lowered[:, :, None, :], jnp.zeros((), jnp.bfloat16))
    lowered = lowered.reshape(nt * rows, count_new * rank)
    update = jnp.dot(lowered, up_cat, preferred_element_type=jnp.float32)

    total = jnp.sum(base.astype(jnp.float32), axis=0).reshape(nz, ny, rows, width_out).transpose(1, 0, 2, 3)
    return (total.reshape(nt * rows, width_out) + adapter_scale * update).astype(jnp.bfloat16)


def solution(mesh):
    nx, nc, ny, nz = 4, 2, 4, 8
    fine = Mesh(mesh.devices.reshape(nx, nc, ny, nz), ("x", "core", "y", "z"))
    group, tensor = ("x", "core"), ("y", "z")
    both = group + tensor
    placed = (
        P(both, None),
        P(None, tensor),
        P(both, None, None),
        P(both, None, None),
        P(group),
        P(group),
        P(both),
    )

    def step(*args):
        return per_device(nx, nc, ny, nz, *args)

    return jax.shard_map(step, mesh=fine, in_specs=placed, out_specs=P(group, tensor), check_vma=False)
```

time: 414 us -> 246 us (0.59)
  waiting for transfers between devices: 332 us -> 82 us
  starting transfers between devices: 0.04 us -> 40.9 us
  local copies, waits for them, and re-layouts: 3.81 us -> 35.4 us
  blocking collectives: 20.5 us -> 27.5 us
    psum x1 -> x0, waiting for transfers between devices: 195 us -> none  [from_root(): return lax.psum(jnp.where(mine, value, jnp.zeros_like(value)), axis)]
    all_gather x1, waiting for transfers between devices: 136 us -> 0.02 us  [per_device(): lax.all_gather(mine.reshape(ny * rows, part), 'z', axis=0, tiled=True)]
    all_to_all x0 -> x9, waiting for transfers between devices: none -> 82 us  [swap(): return lax.all_to_all(value, axis, split_axis=0, concat_axis=0, tiled=True)]
    all_to_all x0 -> x9, starting transfers between devices: none -> 40.9 us  [swap(): return lax.all_to_all(value, axis, split_axis=0, concat_axis=0, tiled=True)]
    all_to_all x0 -> x2, blocking collectives: none -> 27.5 us  [swap(): return lax.all_to_all(value, axis, split_axis=0, concat_axis=0, tiled=True)]
    unnamed x1 -> x0, blocking collectives: 20.5 us -> none
    reshape x0 -> x4, local copies, waits for them, and re-layouts: none -> 10.3 us  [the longest x1 3.34 us: per_device(): down_pool.reshape(held, rank, ny, part).transpose(2, 0, 1, 3)]
    unnamed x11 -> x40, local copies, waits for them, and re-layouts: 0.85 us -> 6.26 us
  transfers between devices with their start and end apart: 2 -> 10, of which waited for: 2 -> 8; matrix products, arithmetic and copies ran while one was open for 1% -> 24% of each run, Pallas kernels for 0% -> 0%
where the time goes in v1:
time: 246 us; the launch traced here: 243 us
  waiting for transfers between devices  82 us (33%)
  starting transfers between devices  40.9 us (17%)
  local copies, waits for them, and re-layouts  35.4 us (14%)
  blocking collectives  27.5 us (11%)
  between operations  26.9 us (11%)
  matrix products  19.2 us (8%)
  other arithmetic  10.7 us (4%)
    all_to_all x9, waiting for transfers between devices, swap(): return lax.all_to_all(value, axis, split_axis=0, concat_axis=0, tiled=True)  82 us
    all_to_all x9, starting transfers between devices, swap(): return lax.all_to_all(value, axis, split_axis=0, concat_axis=0, tiled=True)  40.9 us
    all_to_all x2, blocking collectives, swap(): return lax.all_to_all(value, axis, split_axis=0, concat_axis=0, tiled=True)  27.5 us
    dot_general x4, matrix products, per_device(): jnp.dot(gathered, weight[:, k * width_out:(k + 1) * width_out], preferred...  13.6 us
    unnamed x40, local copies, waits for them, and re-layouts  6.26 us
  transfers between devices with their start and end apart: 10, of which 8 were waited for; matrix products, arithmetic and copies ran while one was open for 24% of the time, Pallas kernels for 0%

profile of v1, /device:TPU:1, one launch (start us, length us, event | category | flops | bytes accessed | tf_op | source)
XLA Modules:
  0.0 242.6 jit_solution(5205335532297725720)
XLA Ops:
  6.5 1.5 reshape.115
  8.0 0.3 copy.34
  8.3 12.7 %all_to_all.56 = bf16[4,32,2048]{2,1,0:T(8,128)(2,1)} all-to-all(bf16[4,32,2048]{2,1,0:T(8,128)(2,1)S(1)} %copy.34), channel_id=1, replica_groups=mesh['x'=4,'core'=2,'y'=4,'z'=8] {'y'}, dimensions={0} | all-to-all | bytes 1048576 | tf_op jit(solution)/shard_map/all_to_all | solution.py:10
  21.0 0.6 broadcast_in_dim.71
  21.7 10.0 %all-to-all-start.5 = ((s32[32,1,32]{2,1,0:T(1,128)}), s32[32,1,32]{2,1,0:T(1,128)S(1)}, u32[]{:S(2)}, u32[]{:S(2)}) async-start(s32[32,1,32]{2,1,0:T(1,128)} %broadcast_in_dim.71), calls=%async_computation.5 | async-start | bytes 32768 | tf_op jit(solution)/shard_map/all_to_all | solution.py:10
  31.6 1.1 constant_dynamic-slice_fusion.4
  32.7 1.0 copy.43
  33.7 6.5 %all-to-all-done.5 = s32[32,1,32]{2,1,0:T(1,128)S(1)} async-done(((s32[32,1,32]{2,1,0:T(1,128)}), s32[32,1,32]{2,1,0:T(1,128)S(1)}, u32[]{:S(2)}, u32[]{:S(2)}) %all-to-all-start.5) | async-done | bytes 4128 | tf_op jit(solution)/shard_map/all_to_all | solution.py:10
  40.3 3.5 %all-to-all-start = ((bf16[4,256,256]{1,2,0:T(8,128)(2,1)}), bf16[4,256,256]{1,2,0:T(8,128)(2,1)S(1)}, u32[]{:S(2)}, u32[]{:S(2)}) async-start(bf16[4,256,256]{1,2,0:T(8,128)(2,1)} %bitcast.1), calls=%async_computation | async-start | bytes 1048576 | tf_op jit(solution)/shard_map/all_to_all | solution.py:10
  43.7 3.3 %reshape.119 = bf16[2,64,4,2048]{3,2,1,0:T(4,128)(2,1)S(1)} reshape(bf16[2,64,8192]{2,1,0:T(8,128)(2,1)} %param.9) | data formatting | bytes 4194304 | tf_op jit(solution)/shard_map/reshape | solution.py:46
  47.1 2.5 %copy.38 = bf16[4,2,64,2048]{3,2,1,0:T(8,128)(2,1)} copy(bf16[4,2,64,2048]{3,0,2,1:T(4,128)(2,1)S(1)} %bitcast.87) | data formatting | bytes 4194304 | tf_op jit(solution)/shard_map/transpose | solution.py:46
  49.6 1.0 all-to-all-done
  50.7 3.6 %all-to-all-start.6 = ((bf16[4,2,64,2048]{3,2,1,0:T(8,128)(2,1)}), bf16[4,2,64,2048]{3,2,1,0:T(8,128)(2,1)S(1)}, u32[]{:S(2)}, u32[]{:S(2)}) async-start(bf16[4,2,64,2048]{3,2,1,0:T(8,128)(2,1)} %copy.38), calls=%async_computation.6 | async-start | bytes 4194304 | tf_op jit(solution)/shard_map/all_to_all | solution.py:10
  54.3 3.2 %copy.47 = bf16[2,8,4,8,2048]{4,3,1,0,2:T(8,128)(2,1)} copy(bf16[2,8,4,8,2048]{4,3,2,1,0:T(8,128)(2,1)} %bitcast.96) | data formatting | bytes 4194304 | tf_op jit(solution)/shard_map/reshape | solution.py:52
  57.5 18.7 %all-to-all-done.6 = bf16[4,2,64,2048]{3,2,1,0:T(8,128)(2,1)S(1)} async-done(((bf16[4,2,64,2048]{3,2,1,0:T(8,128)(2,1)}), bf16[4,2,64,2048]{3,2,1,0:T(8,128)(2,1)S(1)}, u32[]{:S(2)}, u32[]{:S(2)}) %all-to-all-start.6) | async-done | bytes 2097184 | tf_op jit(solution)/shard_map/all_to_all | solution.py:10
  76.3 1.4 copy-done.4
  77.6 3.6 %all-to-all-start.9 = ((bf16[4,2,64,2048]{3,2,1,0:T(8,128)(2,1)}), bf16[4,2,64,2048]{3,2,1,0:T(8,128)(2,1)S(1)}, u32[]{:S(2)}, u32[]{:S(2)}) async-start(bf16[4,2,64,2048]{3,2,1,0:T(8,128)(2,1)} %bitcast.86), calls=%async_computation.9 | async-start | bytes 4194304 | tf_op jit(solution)/shard_map/all_to_all | solution.py:10
  81.3 0.6 gather_fusion
  82.2 19.8 %all-to-all-done.9 = bf16[4,2,64,2048]{3,2,1,0:T(8,128)(2,1)S(1)} async-done(((bf16[4,2,64,2048]{3,2,1,0:T(8,128)(2,1)}), bf16[4,2,64,2048]{3,2,1,0:T(8,128)(2,1)S(1)}, u32[]{:S(2)}, u32[]{:S(2)}) %all-to-all-start.9) | async-done | bytes 2097184 | tf_op jit(solution)/shard_map/all_to_all | solution.py:10
  102.0 1.8 broadcast_in_dim.68
  103.8 0.3 copy-done.2
  104.1 4.0 %all-to-all-start.1 = ((bf16[4,256,1024]{2,1,0:T(8,128)(2,1)}), bf16[4,256,1024]{2,1,0:T(8,128)(2,1)S(1)}, u32[]{:S(2)}, u32[]{:S(2)}) async-start(bf16[4,256,1024]{2,1,0:T(8,128)(2,1)} %broadcast_in_dim.68), calls=%async_computation.1 | async-start | bytes 4194304 | tf_op jit(solution)/shard_map/all_to_all | solution.py:10
  108.1 0.6 fusion.31
  109.3 0.7 fusion.30
  114.6 1.3 dynamic-slice_bitcast_fusion.3
  115.9 4.4 %convolution_bitcast_fusion = f32[1024,256]{0,1:T(8,128)} fusion(bf16[1024,2048]{1,0:T(8,128)(2,1)} %all-gather.2.cloned.1.call-done, bf16[64,2048]{1,0:T(8,128)(2,1)S(1)} %get-tuple-element.13, bf16[64,2048]{1,0:T(8,128)(2,1)S(1)} %get-tuple-element.14, bf16[64,2048]{1,0:T(8,128)(2,1)S(1)} %get-tuple-element.15, bf16[64,2048]{1,0:T(8,128)(2,1)S(1)} %get-tuple-element.12), kind=kOutput, calls=%fused_computation.8 | convolution fusion | flops 1077936128 | bytes 6291456 | tf_op jit(solution)/shard_map/dot_general | solution.py:72
  120.3 1.6 copy.39
  121.9 2.3 reshape.121
  124.2 3.7 %fusion = f32[4,8,32,64]{3,2,0,1:T(8,128)S(1)} fusion(f32[8,4,32,4,64]{4,3,2,1,0:T(4,128)} %reshape.121, pred[4,8,32,4]{3,2,0,1:T(8,128)(4,1)S(1)} %fusion.18), kind=kLoop, calls=%fused_computation.5 | loop fusion | flops 458752 | bytes 1314816 | tf_op jit(solution)/shard_map/reduce_sum | solution.py:75
  127.9 1.0 reshape.134
  128.9 0.5 broadcast_in_dim.70
  129.5 14.8 %all_to_all.57 = bf16[2,1024,1024]{2,1,0:T(8,128)(2,1)} all-to-all(bf16[2,1024,1024]{2,1,0:T(8,128)(2,1)S(1)} %broadcast_in_dim.70), channel_id=1, replica_groups=mesh['x'=4,'core'=2,'y'=4,'z'=8] {'core'}, dimensions={0} | all-to-all | bytes 8388608 | tf_op jit(solution)/shard_map/all_to_all | solution.py:10
  144.2 3.9 %all-to-all-start.7 = ((f32[32,1,2048]{2,1,0:T(1,128)}), f32[32,1,2048]{2,1,0:T(1,128)S(1)}, u32[]{:S(2)}, u32[]{:S(2)}) async-start(f32[32,1,2048]{2,1,0:T(1,128)} %reshape.134), calls=%async_computation.7 | async-start | bytes 524288 | tf_op jit(solution)/shard_map/all_to_all | solution.py:10
  148.1 0.7 copy.45
  149.0 1.3 copy.42
  150.3 8.0 %all-to-all-done.7 = f32[32,1,2048]{2,1,0:T(1,128)S(1)} async-done(((f32[32,1,2048]{2,1,0:T(1,128)}), f32[32,1,2048]{2,1,0:T(1,128)S(1)}, u32[]{:S(2)}, u32[]{:S(2)}) %all-to-all-start.7) | async-done | bytes 262176 | tf_op jit(solution)/shard_map/all_to_all | solution.py:10
  158.3 4.9 %all-to-all-start.10 = ((bf16[8,4,64,256]{3,2,1,0:T(8,128)(2,1)}), bf16[8,4,64,256]{3,2,1,0:T(8,128)(2,1)S(1)}, u32[]{:S(2)}, u32[]{:S(2)}) async-start(bf16[8,4,64,256]{3,2,1,0:T(8,128)(2,1)} %copy.42), calls=%async_computation.10 | async-start | bytes 2097152 | tf_op jit(solution)/shard_map/all_to_all | solution.py:10
  163.2 4.0 %fusion.6 = bf16[1,1024,256]{1,2,0:T(8,128)(2,1)S(1)} fusion(bf16[1024,2048]{1,0:T(8,128)(2,1)} %all-gather.2.cloned.1.call-done, bf16[2048,1024]{1,0:T(8,128)(2,1)} %bitcast.90), kind=kOutput, calls=%fused_computation.17 | convolution fusion | flops 1074003968 | bytes 5767168 | tf_op jit(solution)/shard_map/dot_general | solution.py:64
  167.2 3.7 %fusion.5 = bf16[1,1024,256]{1,2,0:T(8,128)(2,1)S(1)} fusion(bf16[1024,2048]{1,0:T(8,128)(2,1)} %all-gather.2.cloned.1.call-done, bf16[2048,1024]{1,0:T(8,128)(2,1)S(1)} %bitcast.92), kind=kOutput, calls=%fused_computation.16 | convolution fusion | flops 1074003968 | bytes 5767168 | tf_op jit(solution)/shard_map/dot_general | solution.py:64
  170.9 2.1 fusion.4
  173.0 0.5 broadcast.137
  173.5 1.2 reduce
  174.7 0.2 reshape.135
  175.1 0.9 reshape.136
  175.9 16.5 %all-to-all-done.10 = bf16[8,4,64,256]{3,2,1,0:T(8,128)(2,1)S(1)} async-done(((bf16[8,4,64,256]{3,2,1,0:T(8,128)(2,1)}), bf16[8,4,64,256]{3,2,1,0:T(8,128)(2,1)S(1)}, u32[]{:S(2)}, u32[]{:S(2)}) %all-to-all-start.10) | async-done | bytes 1048608 | tf_op jit(solution)/shard_map/all_to_all | solution.py:10
  192.4 3.8 %all-to-all-start.8 = ((bf16[32,2,1024]{2,1,0:T(2,128)(2,1)}), bf16[32,2,1024]{2,1,0:T(2,128)(2,1)S(1)}, u32[]{:S(2)}, u32[]{:S(2)}) async-start(bf16[32,2,1024]{2,1,0:T(2,128)(2,1)} %reshape.136), calls=%async_computation.8 | async-start | bytes 262144 | tf_op jit(solution)/shard_map/all_to_all | solution.py:10
  196.3 3.9 %fusion.3 = bf16[1,1024,256]{1,2,0:T(8,128)(2,1)S(1)} fusion(bf16[1024,2048]{1,0:T(8,128)(2,1)} %all-gather.2.cloned.1.call-done, bf16[2048,1024]{1,0:T(8,128)(2,1)} %bitcast.91), kind=kOutput, calls=%fused_computation.14 | convolution fusion | flops 1074003968 | bytes 5767168 | tf_op jit(solution)/shard_map/dot_general | solution.py:64
  200.2 1.6 pad_maximum_fusion
  201.8 3.6 %all-to-all-done.8 = bf16[32,2,1024]{2,1,0:T(2,128)(2,1)S(1)} async-done(((bf16[32,2,1024]{2,1,0:T(2,128)(2,1)}), bf16[32,2,1024]{2,1,0:T(2,128)(2,1)S(1)}, u32[]{:S(2)}, u32[]{:S(2)}) %all-to-all-start.8) | async-done | bytes 131104 | tf_op jit(solution)/shard_map/all_to_all | solution.py:10
  205.4 3.6 %all-to-all-start.4 = ((bf16[4,1024,256]{1,2,0:T(8,128)(2,1)}), bf16[4,1024,256]{1,2,0:T(8,128)(2,1)S(1)}, u32[]{:S(2)}, u32[]{:S(2)}) async-start(bf16[4,1024,256]{1,2,0:T(8,128)(2,1)} %pad_maximum_fusion), calls=%async_computation.4 | async-start | bytes 4194304 | tf_op jit(solution)/shard_map/all_to_all | solution.py:10
  209.0 0.7 fusion.29
  217.8 0.9 iota_compare_fusion.1
  218.7 0.6 dynamic-slice_bitcast_fusion.4
  219.4 0.6 dynamic-slice_bitcast_fusion.5
  220.0 0.6 dynamic-slice_bitcast_fusion.6
  220.6 0.6 dynamic-slice_bitcast_fusion.7
  221.2 0.2 reshape.137
  221.4 2.6 %broadcast_select_fusion = bf16[32,32,4,64]{3,2,1,0:T(4,128)(2,1)S(1)} fusion(pred[32,32,4]{2,1,0:T(8,128)(4,1)} %iota_compare_fusion.1, bf16[32,32,64]{2,1,0:T(8,128)(2,1)S(1)} %reshape.137), kind=kLoop, calls=%fused_computation.30 | loop fusion | flops 262144 | bytes 659456 | tf_op jit(solution)/shard_map/jit(_where)/select_n | solution.py:80
  224.0 1.5 select_n.89
  225.5 7.7 %all-to-all-done.4 = bf16[4,1024,256]{1,2,0:T(8,128)(2,1)S(1)} async-done(((bf16[4,1024,256]{1,2,0:T(8,128)(2,1)}), bf16[4,1024,256]{1,2,0:T(8,128)(2,1)S(1)}, u32[]{:S(2)}, u32[]{:S(2)}) %all-to-all-start.4) | async-done | bytes 2097184 | tf_op jit(solution)/shard_map/all_to_all | solution.py:10
  233.2 0.4 convert_reduce_fusion
  233.7 0.3 copy.35
  234.1 0.6 copy-done.6
  234.7 1.1 fusion.2
  (49 shorter events, 1.1 us)
Async XLA Ops:
  6.5 74.8 %copy-start = (s32[64]{0:T(128)S(1)}, s32[64]{0:T(128)}, u32[]{:S(2)}) copy-start(s32[64]{0:T(128)} %param.11) | copy-start | bytes 772
  6.5 14.5 %copy-start.14 = (s32[32]{0:T(128)S(1)}, s32[32]{0:T(128)}, u32[]{:S(2)}) copy-start(s32[32]{0:T(128)} %param.13) | copy-start | bytes 388
  6.5 109.3 %all-gather.2.cloned.1.call-start = ((), (), s32[]{:S(2)}) async-start(), calls=%async_computation.11 | async-start | bytes 4718592 | tf_op jit(solution)/shard_map/all_gather | solution.py:36
  21.7 18.6 %all-to-all-start.5 = ((s32[32,1,32]{2,1,0:T(1,128)}), s32[32,1,32]{2,1,0:T(1,128)S(1)}, u32[]{:S(2)}, u32[]{:S(2)}) async-start(s32[32,1,32]{2,1,0:T(1,128)} %broadcast_in_dim.71), calls=%async_computation.5 | async-start | bytes 32768 | tf_op jit(solution)/shard_map/all_to_all | solution.py:10
  40.3 74.1 %copy-start.8 = (s32[32,1,32]{2,1,0:T(1,128)}, s32[32,1,32]{2,1,0:T(1,128)S(1)}, u32[]{:S(2)}) copy-start(s32[32,1,32]{2,1,0:T(1,128)S(1)} %all-to-all-done.5) | copy-start | bytes 12292
  40.3 10.4 %all-to-all-start = ((bf16[4,256,256]{1,2,0:T(8,128)(2,1)}), bf16[4,256,256]{1,2,0:T(8,128)(2,1)S(1)}, u32[]{:S(2)}, u32[]{:S(2)}) async-start(bf16[4,256,256]{1,2,0:T(8,128)(2,1)} %bitcast.1), calls=%async_computation | async-start | bytes 1048576 | tf_op jit(solution)/shard_map/all_to_all | solution.py:10
  50.7 25.6 %all-to-all-start.6 = ((bf16[4,2,64,2048]{3,2,1,0:T(8,128)(2,1)}), bf16[4,2,64,2048]{3,2,1,0:T(8,128)(2,1)S(1)}, u32[]{:S(2)}, u32[]{:S(2)}) async-start(bf16[4,2,64,2048]{3,2,1,0:T(8,128)(2,1)} %copy.38), calls=%async_computation.6 | async-start | bytes 4194304 | tf_op jit(solution)/shard_map/all_to_all | solution.py:10
  76.3 1.4 copy-start.4
  76.3 5.0 %copy-start.16 = (s32[4]{0:T(128)S(1)}, s32[4]{0:T(128)}, u32[]{:S(2)}) copy-start(s32[4]{0:T(128)} %param.12) | copy-start | bytes 52
  77.6 24.4 %all-to-all-start.9 = ((bf16[4,2,64,2048]{3,2,1,0:T(8,128)(2,1)}), bf16[4,2,64,2048]{3,2,1,0:T(8,128)(2,1)S(1)}, u32[]{:S(2)}, u32[]{:S(2)}) async-start(bf16[4,2,64,2048]{3,2,1,0:T(8,128)(2,1)} %bitcast.86), calls=%async_computation.9 | async-start | bytes 4194304 | tf_op jit(solution)/shard_map/all_to_all | solution.py:10
  102.0 2.1 copy-start.2
  104.1 24.9 %all-to-all-start.1 = ((bf16[4,256,1024]{2,1,0:T(8,128)(2,1)}), bf16[4,256,1024]{2,1,0:T(8,128)(2,1)S(1)}, u32[]{:S(2)}, u32[]{:S(2)}) async-start(bf16[4,256,1024]{2,1,0:T(8,128)(2,1)} %broadcast_in_dim.68), calls=%async_computation.1 | async-start | bytes 4194304 | tf_op jit(solution)/shard_map/all_to_all | solution.py:10
  129.5 18.6 %copy-start.3 = (bf16[4,2,64,2048]{3,2,1,0:T(8,128)(2,1)S(1)}, bf16[4,2,64,2048]{3,2,1,0:T(8,128)(2,1)}, u32[]{:S(2)}) copy-start(bf16[4,2,64,2048]{3,2,1,0:T(8,128)(2,1)} %copy-done.2) | copy-start | bytes 6291460
  144.2 14.1 %all-to-all-start.7 = ((f32[32,1,2048]{2,1,0:T(1,128)}), f32[32,1,2048]{2,1,0:T(1,128)S(1)}, u32[]{:S(2)}, u32[]{:S(2)}) async-start(f32[32,1,2048]{2,1,0:T(1,128)} %reshape.134), calls=%async_computation.7 | async-start | bytes 524288 | tf_op jit(solution)/shard_map/all_to_all | solution.py:10
  158.3 34.1 %all-to-all-start.10 = ((bf16[8,4,64,256]{3,2,1,0:T(8,128)(2,1)}), bf16[8,4,64,256]{3,2,1,0:T(8,128)(2,1)S(1)}, u32[]{:S(2)}, u32[]{:S(2)}) async-start(bf16[8,4,64,256]{3,2,1,0:T(8,128)(2,1)} %copy.42), calls=%async_computation.10 | async-start | bytes 2097152 | tf_op jit(solution)/shard_map/all_to_all | solution.py:10
  163.2 4.0 %copy-start.5 = (bf16[2,1024,1024]{2,1,0:T(8,128)(2,1)S(1)}, bf16[2,1024,1024]{2,1,0:T(8,128)(2,1)}, u32[]{:S(2)}) copy-start(bf16[2,1024,1024]{2,1,0:T(8,128)(2,1)} %all_to_all.57) | copy-start | bytes 12582916
  167.2 3.7 %copy-start.15 = (bf16[1024,2048]{1,0:T(8,128)(2,1)S(1)}, bf16[1024,2048]{1,0:T(8,128)(2,1)}, u32[]{:S(2)}) copy-start(bf16[1024,2048]{1,0:T(8,128)(2,1)} %all-gather.2.cloned.1.call-done) | copy-start | bytes 12582916
  192.4 13.0 %all-to-all-start.8 = ((bf16[32,2,1024]{2,1,0:T(2,128)(2,1)}), bf16[32,2,1024]{2,1,0:T(2,128)(2,1)S(1)}, u32[]{:S(2)}, u32[]{:S(2)}) async-start(bf16[32,2,1024]{2,1,0:T(2,128)(2,1)} %reshape.136), calls=%async_computation.8 | async-start | bytes 262144 | tf_op jit(solution)/shard_map/all_to_all | solution.py:10
  196.3 3.9 %copy-start.7 = (bf16[1,1024,256]{1,2,0:T(8,128)(2,1)S(1)}, bf16[1,1024,256]{1,2,0:T(8,128)(2,1)}, u32[]{:S(2)}) copy-start(bf16[1,1024,256]{1,2,0:T(8,128)(2,1)} %fusion.4) | copy-start | bytes 1572868
  201.8 16.0 %copy-start.9 = (s32[32,1,32]{2,1,0:T(1,128)S(1)}, s32[32,1,32]{2,1,0:T(1,128)}, u32[]{:S(2)}) copy-start(s32[32,1,32]{2,1,0:T(1,128)} %copy-done.8) | copy-start | bytes 12292
  205.4 27.8 %all-to-all-start.4 = ((bf16[4,1024,256]{1,2,0:T(8,128)(2,1)}), bf16[4,1024,256]{1,2,0:T(8,128)(2,1)S(1)}, u32[]{:S(2)}, u32[]{:S(2)}) async-start(bf16[4,1024,256]{1,2,0:T(8,128)(2,1)} %pad_maximum_fusion), calls=%async_computation.4 | async-start | bytes 4194304 | tf_op jit(solution)/shard_map/all_to_all | solution.py:10
  233.6 1.0 copy-start.6
  233.6 1.0 copy-start.10
  233.6 1.0 copy-start.11
  233.6 1.0 copy-start.12
  233.7 1.0 copy-start.13
  234.0 1.8 copy-start.1
Sparse Core Ops, SparseCore 0:
  21.2 57.7 all-gather.1

commit v2 on v1

v2 whole, which is shorter than its diff:
```python
import functools

import jax
import jax.numpy as jnp
from jax import lax
from jax.experimental import pallas as pl
from jax.experimental.pallas import tpu as pltpu
from jax.sharding import Mesh, PartitionSpec as P

adapter_scale = 2.0
vmem_bytes = 48 * 1024 * 1024


def swap(value, axis):
    return lax.all_to_all(value, axis, split_axis=0, concat_axis=0, tiled=True)


def spread(value, axis, count):
    return swap(jnp.broadcast_to(value[None], (count,) + value.shape), axis)


def after(value, *earlier):
    return lax.optimization_barrier((value,) + earlier)[0]


def shift(value, axis, size, by):
    return lax.ppermute(value, axis, [(i, (i + by) % size) for i in range(size)])


def doubled(value, axis, size, place):
    bit = 1
    while bit < size:
        other = lax.ppermute(value, axis, [(i, i ^ bit) for i in range(size)])
        high = (place & bit) != 0
        value = jnp.concatenate([jnp.where(high, other, value), jnp.where(high, value, other)])
        bit *= 2
    return value


def base_kernel(core_ref, rows_ref, mine_ref, other_ref, out_ref):
    half = mine_ref.shape[0]
    rows = rows_ref.shape[0] * rows_ref.shape[2]
    core = core_ref[0]
    first = rows_ref[:, 0, :, pl.ds(pl.multiple_of(core * half, half), half)].reshape(rows, half)
    second = rows_ref[:, 0, :, pl.ds(pl.multiple_of((1 - core) * half, half), half)].reshape(rows, half)
    total = jnp.dot(first, mine_ref[...], preferred_element_type=jnp.float32)
    total += jnp.dot(second, other_ref[...], preferred_element_type=jnp.float32)
    width = out_ref.shape[2]
    for k in range(out_ref.shape[0]):
        out_ref[k] = total[:, k * width : (k + 1) * width].astype(out_ref.dtype)


def base_parts(core, gathered, mine, other, ny, nz, rows, width_out):
    part = gathered.shape[1]
    whole = pl.BlockSpec(mine.shape, lambda i, c: (0, 0))
    return pl.pallas_call(
        base_kernel,
        out_shape=jax.ShapeDtypeStruct((ny, ny * nz * rows, width_out), jnp.bfloat16),
        grid_spec=pltpu.PrefetchScalarGridSpec(
            num_scalar_prefetch=1,
            grid=(ny,),
            in_specs=[pl.BlockSpec((nz, 1, rows, part), lambda i, c: (0, i, 0, 0)), whole, whole],
            out_specs=pl.BlockSpec((ny, nz * rows, width_out), lambda i, c: (0, i, 0)),
        ),
        compiler_params=pltpu.CompilerParams(vmem_limit_bytes=vmem_bytes),
        cost_estimate=pl.CostEstimate(
            flops=2 * ny * nz * rows * part * ny * width_out, bytes_accessed=10 * 1024 * 1024, transcendentals=0
        ),
        name="base_parts",
    )(core, gathered.reshape(nz, ny, rows, part), mine, other)


def chosen_kernel(count, wanted_ref, slot_ref, rows_ref, ids_ref, *rest):
    downs, out_ref = rest[:count], rest[count]
    nz, _, rows, part = rows_ref.shape
    rank = downs[0].shape[1]
    lines = rows_ref[:, 0].reshape(nz * rows, part)
    lane = lax.broadcasted_iota(jnp.int32, (nz * rows, 2 * rank), 1)
    total = jnp.zeros((nz * rows, 2 * rank), jnp.float32)
    for s in range(0, count, 2):
        both = jnp.concatenate([downs[s][0], downs[s + 1][0]], axis=0)
        product = lax.dot_general(lines, both, (((1,), (1,)), ((), ())), preferred_element_type=jnp.float32)
        target = jnp.where(lane < rank, wanted_ref[s], wanted_ref[s + 1])
        total += jnp.where(ids_ref[...] == target, product, 0.0)
    total = total[:, :rank] + total[:, rank:]
    for k in range(nz):
        piece = total[k * rows : (k + 1) * rows]
        out_ref[k] = jnp.concatenate([piece[: rows // 2], piece[rows // 2 :]], axis=1)


def chosen_parts(wanted, slots, gathered, ids, down, count, ny, nz, rows):
    part = gathered.shape[1]
    _, rank, _ = down.shape

    def slot_spec(s):
        return pl.BlockSpec((1, rank, part), lambda i, w, p: (p[s], 0, 0))

    return pl.pallas_call(
        functools.partial(chosen_kernel, count),
        out_shape=jax.ShapeDtypeStruct((ny * nz, rows // 2, 2 * rank), jnp.float32),
        grid_spec=pltpu.PrefetchScalarGridSpec(
            num_scalar_prefetch=2,
            grid=(ny,),
            in_specs=[
                pl.BlockSpec((nz, 1, rows, part), lambda i, w, p: (0, i, 0, 0)),
                pl.BlockSpec((nz * rows, 2 * rank), lambda i, w, p: (i, 0)),
            ]
            + [slot_spec(s) for s in range(count)],
            out_specs=pl.BlockSpec((nz, rows // 2, 2 * rank), lambda i, w, p: (i, 0, 0)),
        ),
        compiler_params=pltpu.CompilerParams(vmem_limit_bytes=vmem_bytes),
        cost_estimate=pl.CostEstimate(
            flops=2 * ny * nz * rows * part * count * rank, bytes_accessed=6 * 1024 * 1024, transcendentals=0
        ),
        name="chosen_parts",
    )(wanted, slots, gathered.reshape(nz, ny, rows, part), ids, *([down] * count))


def final_kernel(count, base_ref, low_ref, ids_ref, up_ref, out_ref):
    nz, half, both = low_ref.shape
    rank = both // 2
    low = jnp.concatenate(
        [low_ref[k][:, h * rank : (h + 1) * rank] for k in range(nz) for h in range(2)], axis=0
    ).astype(jnp.float32)
    low = jnp.concatenate([low, low], axis=1)
    lane = lax.broadcasted_iota(jnp.int32, low.shape, 1)
    update = jnp.zeros(out_ref.shape, jnp.float32)
    for s in range(0, count, 2):
        target = jnp.where(lane < rank, s, s + 1)
        kept = jnp.where(ids_ref[...] == target, low, 0.0).astype(jnp.bfloat16)
        update += jnp.dot(kept, up_ref[s * rank : (s + 2) * rank], preferred_element_type=jnp.float32)
    out_ref[...] = (base_ref[...].astype(jnp.float32) + adapter_scale * update).astype(out_ref.dtype)


def final_rows(base, low, ids, up_cat, count, ny, nz):
    tall, width_out = base.shape
    block = tall // ny
    return pl.pallas_call(
        functools.partial(final_kernel, count),
        out_shape=jax.ShapeDtypeStruct((tall, width_out), jnp.bfloat16),
        grid=(ny,),
        in_specs=[
            pl.BlockSpec((block, width_out), lambda i: (i, 0)),
            pl.BlockSpec((nz,) + low.shape[1:], lambda i: (i, 0, 0)),
            pl.BlockSpec((block, ids.shape[1]), lambda i: (i, 0)),
            pl.BlockSpec(up_cat.shape, lambda i: (0, 0)),
        ],
        out_specs=pl.BlockSpec((block, width_out), lambda i: (i, 0)),
        compiler_params=pltpu.CompilerParams(vmem_limit_bytes=vmem_bytes),
        cost_estimate=pl.CostEstimate(
            flops=2 * tall * up_cat.shape[0] * width_out, bytes_accessed=2 * 1024 * 1024, transcendentals=0
        ),
        name="final_rows",
    )(base, low, ids, up_cat)


def per_device(nx, nc, ny, nz, tokens, base_weight, down_pool, up_pool, slot_of, requested, row_adapter):
    rows, width = tokens.shape
    width_out = base_weight.shape[1]
    held, rank, _ = down_pool.shape
    count_new = requested.shape[0]
    part = width // ny
    sub = part // (nx * nc)
    nt = ny * nz
    x, core, y, z = [lax.axis_index(a) for a in ("x", "core", "y", "z")]

    blocks = jnp.stack([tokens[:, k * part : (k + 1) * part] for k in range(ny)])
    mine = swap(blocks, "y")
    gathered = lax.all_gather(mine.reshape(ny * rows, part), "z", axis=0, tiled=True)

    pool_rows = slot_of[requested]
    home, local = pool_rows // held, pool_rows % held
    home_y, home_z = home // nz, home % nz

    ids = doubled(row_adapter.reshape(1, rows), "z", nz, z)
    ids = doubled(ids, "y", ny, y)
    ids = jnp.broadcast_to(ids.reshape(nt * rows, 1), (nt * rows, 2 * rank))

    piece = base_weight.reshape(ny, nc * nx, sub, width_out)
    piece = lax.dynamic_index_in_dim(piece, core * nx + x, 1, keepdims=False)
    piece = swap(after(piece, mine), "y").transpose(1, 0, 2).reshape(sub, ny * width_out)
    piece = spread(piece, "x", nx).reshape(nx * sub, ny * width_out)
    other = shift(piece, "core", nc, 1)

    down = jnp.stack([down_pool[:, :, k * part : (k + 1) * part] for k in range(ny)])
    down = swap(after(down, piece), "y").reshape(ny * held, rank, part)

    ups = []
    for d in range(ny):
        block = lax.dynamic_slice_in_dim(up_pool, ((y + d) % ny) * part, part, 2)
        ups.append(shift(after(block, mine), "y", ny, d) if d else block)
    ups = jnp.stack(ups)
    ups = jnp.stack([ups[(y - home_y[s]) % ny, local[s]] for s in range(count_new)])
    cols = []
    for d in range(nz):
        block = lax.dynamic_slice_in_dim(ups, ((z + d) % nz) * width_out, width_out, 2)
        cols.append(shift(block, "z", nz, d) if d else block)
    cols = jnp.stack(cols)
    up_cat = jnp.concatenate([cols[(z - home_z[s]) % nz, s] for s in range(count_new)])

    base = base_parts(core.astype(jnp.int32).reshape(1), gathered, piece, other, ny, nz, rows, width_out)
    base = lax.psum_scatter(base, "y", scatter_dimension=0, tiled=True)[0]

    wanted = jnp.where(home_z == z, jnp.arange(count_new, dtype=jnp.int32), -1)
    slots = home_y * held + local
    chosen = swap(chosen_parts(wanted, slots, gathered, ids, down, count_new, ny, nz, rows), ("y", "z"))
    lowered = jnp.sum(chosen, axis=0).astype(jnp.bfloat16)
    lowered = spread(lowered, ("y", "z"), nt)
    return final_rows(base, lowered, ids, up_cat, count_new, ny, nz)


def solution(mesh):
    nx, nc, ny, nz = 4, 2, 4, 8
    fine = Mesh(mesh.devices.reshape(nx, nc, ny, nz), ("x", "core", "y", "z"))
    group, tensor = ("x", "core"), ("y", "z")
    both = group + tensor
    placed = (
        P(both, None),
        P(None, tensor),
        P(both, None, None),
        P(both, None, None),
        P(group),
        P(group),
        P(both),
    )

    def step(*args):
        return per_device(nx, nc, ny, nz, *args)

    return jax.shard_map(step, mesh=fine, in_specs=placed, out_specs=P(group, tensor), check_vma=False)
```

time: 246 us -> 236 us (0.959)
  matrix products: 19.2 us -> 0 us
  starting transfers between devices: 40.9 us -> 57.2 us
  Pallas kernels: 0 us -> 15.8 us
  local copies, waits for them, and re-layouts: 35.4 us -> 25 us
  other arithmetic: 10.7 us -> 4.87 us
  blocking collectives: 27.5 us -> 22.1 us
    ppermute x0 -> x16, waiting for transfers between devices: none -> 49.5 us  [the longest x5 30.5 us: doubled(): other = lax.ppermute(value, axis, [(i, i ^ bit) for i in range(size)])]
    all_to_all x9 -> x4, waiting for transfers between devices: 82 us -> 33.3 us  [swap(): return lax.all_to_all(value, axis, split_axis=0, concat_axis=0, tiled=True)]
    ppermute x0 -> x16, starting transfers between devices: none -> 34.4 us  [the longest x11 22.8 us: shift(): lax.ppermute(value, axis, [(i, (i + by) % size) for i in range(size)])]
    dot_general x6 -> x0, matrix products: 19.2 us -> none  [the longest x4 13.6 us: per_device(): jnp.dot(gathered, weight[:, k * width_out:(k + 1) * width_out], preferred...]
    all_to_all x9 -> x4, starting transfers between devices: 40.9 us -> 22.8 us  [swap(): return lax.all_to_all(value, axis, split_axis=0, concat_axis=0, tiled=True)]
    pallas_call x0 -> x3, Pallas kernels: none -> 15.8 us  [the longest x1 7.15 us: base_parts(): pl.pallas_call(base_kernel, out_shape=jax.ShapeDtypeStruct((ny, ny * nz *...]
    reshape x4 -> x0, local copies, waits for them, and re-layouts: 10.3 us -> none  [the longest x1 3.34 us: per_device(): down_pool.reshape(held, rank, ny, part).transpose(2, 0, 1, 3)]
    another operation x0 -> x5, local copies, waits for them, and re-layouts: none -> 5.9 us  [the longest x1 2.87 us: per_device(): ups = jnp.stack(ups)]
  transfers between devices with their start and end apart: 10 -> 22, of which waited for: 8 -> 7; matrix products, arithmetic and copies ran while one was open for 24% -> 11% of each run, Pallas kernels for 0% -> 6%
where the time goes in v2:
time: 236 us; the launch traced here: 234 us
  waiting for transfers between devices  82.8 us (35%)
  starting transfers between devices  57.2 us (24%)
  between operations  26.4 us (11%)
  local copies, waits for them, and re-layouts  25 us (11%)
  blocking collectives  22.1 us (9%)
  Pallas kernels  15.8 us (7%)
  other arithmetic  4.87 us (2%)
    all_to_all x4, waiting for transfers between devices, swap(): return lax.all_to_all(value, axis, split_axis=0, concat_axis=0, tiled=True)  33.3 us
    ppermute x5, waiting for transfers between devices, doubled(): other = lax.ppermute(value, axis, [(i, i ^ bit) for i in range(size)])  30.5 us
    all_to_all x4, starting transfers between devices, swap(): return lax.all_to_all(value, axis, split_axis=0, concat_axis=0, tiled=True)  22.8 us
    ppermute x11, starting transfers between devices, shift(): lax.ppermute(value, axis, [(i, (i + by) % size) for i in range(size)])  22.8 us
    all_to_all x2, blocking collectives, swap(): return lax.all_to_all(value, axis, split_axis=0, concat_axis=0, tiled=True)  22.1 us
    ppermute x11, waiting for transfers between devices, shift(): lax.ppermute(value, axis, [(i, (i + by) % size) for i in range(size)])  19 us
    ppermute x5, starting transfers between devices, doubled(): other = lax.ppermute(value, axis, [(i, i ^ bit) for i in range(size)])  11.6 us
    unnamed x23, local copies, waits for them, and re-layouts  10.7 us
  transfers between devices with their start and end apart: 22, of which 7 were waited for; matrix products, arithmetic and copies ran while one was open for 11% of the time, Pallas kernels for 6%

profile of v2, /device:TPU:1, one launch (start us, length us, event | category | flops | bytes accessed | tf_op | source)
XLA Modules:
  0.0 234.1 jit_solution(17176599579615331205)
XLA Ops:
  6.5 1.1 slice_bitcast_fusion.7
  7.7 0.1 pad_maximum_fusion.3
  7.8 12.7 %all_to_all.30 = bf16[4,32,2048]{2,1,0:T(8,128)(2,1)} all-to-all(bf16[4,32,2048]{2,1,0:T(8,128)(2,1)S(1)} %pad_maximum_fusion.3), channel_id=1, replica_groups=mesh['x'=4,'core'=2,'y'=4,'z'=8] {'y'}, dimensions={0} | all-to-all | bytes 1048576 | tf_op jit(solution)/shard_map/all_to_all | solution.py:15
  20.5 0.0 all-gather.2.cloned.1.call-update
  20.5 1.1 dynamic-slice_bitcast_fusion.1
  21.6 9.3 %all_to_all.31 = bf16[4,256,256]{2,1,0:T(8,128)(2,1)S(1)} all-to-all(bf16[4,256,256]{2,1,0:T(8,128)(2,1)S(1)} %dynamic-slice_bitcast_fusion.1), channel_id=1, replica_groups=mesh['x'=4,'core'=2,'y'=4,'z'=8] {'y'}, dimensions={0} | all-to-all | bytes 1048576 | tf_op jit(solution)/shard_map/all_to_all | solution.py:15
  30.9 0.2 copy.8
  31.2 0.2 copy.9
  31.4 1.6 broadcast_in_dim.26
  33.0 5.6 %all-to-all-start.2 = ((bf16[4,256,1024]{2,1,0:T(8,128)(2,1)}), bf16[4,256,1024]{2,1,0:T(8,128)(2,1)S(1)}, u32[]{:S(2)}, u32[]{:S(2)}) async-start(bf16[4,256,1024]{2,1,0:T(8,128)(2,1)} %broadcast_in_dim.26), calls=%async_computation.2 | async-start | bytes 4194304 | tf_op jit(solution)/shard_map/all_to_all | solution.py:15
  38.6 1.7 collective-permute-start.1
  40.4 21.6 %all-to-all-done.2 = bf16[4,256,1024]{2,1,0:T(8,128)(2,1)S(1)} async-done(((bf16[4,256,1024]{2,1,0:T(8,128)(2,1)}), bf16[4,256,1024]{2,1,0:T(8,128)(2,1)S(1)}, u32[]{:S(2)}, u32[]{:S(2)}) %all-to-all-start.2) | async-done | bytes 2097184 | tf_op jit(solution)/shard_map/all_to_all | solution.py:15
  61.9 4.0 %collective-permute-start = (bf16[1024,1024]{1,0:T(8,128)(2,1)S(1)}, bf16[1024,1024]{1,0:T(8,128)(2,1)}, u32[]{:S(2)}, u32[]{:S(2)}) collective-permute-start(bf16[1024,1024]{1,0:T(8,128)(2,1)S(1)} %bitcast.83), channel_id=1, source_target_pairs={{0,32},{32,0},{1,33},{33,1},{2,34},{34,2},{3,35},{35,3},{4,36},{36... | collective-permute-start | bytes 6291464 | tf_op jit(solution)/shard_map/ppermute | solution.py:27
  65.9 0.6 gather_fusion
  66.6 0.7 fusion
  69.8 0.6 fusion.1
  72.5 2.9 %dynamic-slice_bitcast_fusion = (bf16[1,2,64,2048]{3,2,1,0:T(8,128)(2,1)S(1)}, bf16[2,64,2048]{2,1,0:T(8,128)(2,1)S(1)}, bf16[2,64,2048]{2,1,0:T(8,128)(2,1)}, bf16[2,64,2048]{2,1,0:T(8,128)(2,1)}) fusion(bf16[2,64,8192]{2,1,0:T(8,128)(2,1)} %param.10, s32[]{:T(128)S(6)} %select_n.267, s32[]{:T(128)S(6)} %select_n.269, s32[]{:T(128)S(6)} %select_n.273, ...), kind=kLoop, calls=%fused_computation.5 | loop fusion | bytes 4194320 | tf_op jit(solution)/shard_map/stack | solution.py:192
  75.4 0.2 slice_bitcast_fusion.3
  75.6 1.7 pad_maximum_fusion
  77.3 3.0 %collective-permute-start.2 = (s32[2,32]{1,0:T(2,128)S(1)}, s32[2,32]{1,0:T(2,128)S(1)}, u32[]{:S(2)}, u32[]{:S(2)}) collective-permute-start(s32[2,32]{1,0:T(2,128)S(1)} %pad_add_fusion.4), channel_id=1, source_target_pairs={{0,2},{1,3},{2,0},{3,1},{4,6},{5,7},{6,4},{7,5},{8,10},{9,11},{10,... | collective-permute-start | bytes 776 | tf_op jit(solution)/shard_map/ppermute | solution.py:33
  80.3 7.2 %base_parts.1 = bf16[4,1024,256]{2,1,0:T(8,128)(2,1)S(1)} custom-call(s32[1]{0:T(128)} %bitcast.core_ref, bf16[8,4,32,2048]{3,2,1,0:T(8,128)(2,1)} %bitcast.86, bf16[1024,1024]{1,0:T(8,128)(2,1)S(1)} %bitcast.84, bf16[1024,1024]{1,0:T(8,128)(2,1)} %collective-permute-done.other_ref), custom_call_target="tpu_custom_call" | custom-call | flops 4294967296 | bytes 10485760 | tf_op jit(solution)/shard_map/base_parts/pallas_call | solution.py:56
  87.5 1.4 copy-done.1
  88.9 0.0 reduce-scatter.2.cloned.1.call-update
  88.9 5.2 %collective-permute-start.3 = (s32[4,32]{1,0:T(4,128)S(1)}, s32[4,32]{1,0:T(4,128)S(1)}, u32[]{:S(2)}, u32[]{:S(2)}) collective-permute-start(s32[4,32]{1,0:T(4,128)S(1)} %pad_add_fusion.3), channel_id=1, source_target_pairs={{0,4},{1,5},{2,6},{3,7},{4,0},{5,1},{6,2},{7,3},{8,12},{9,13},{10,... | collective-permute-start | bytes 1544 | tf_op jit(solution)/shard_map/ppermute | solution.py:33
  94.8 0.6 collective-permute-done.3
  95.4 0.4 collective-permute-start.4
  95.8 1.8 collective-permute-start.7
  97.6 1.8 collective-permute-start.8
  99.4 1.3 collective-permute-start.5
  108.1 29.9 %collective-permute-done.5 = s32[16,32]{1,0:T(8,128)S(1)} collective-permute-done((s32[16,32]{1,0:T(8,128)S(1)}, s32[16,32]{1,0:T(8,128)S(1)}, u32[]{:S(2)}, u32[]{:S(2)}) %collective-permute-start.5) | collective-permute-done | bytes 2080 | tf_op jit(solution)/shard_map/ppermute | solution.py:33
  138.1 0.6 broadcast_select_fusion.1
  138.7 3.6 %all-to-all-start.3 = ((bf16[4,2,64,2048]{3,2,1,0:T(8,128)(2,1)}), bf16[4,2,64,2048]{3,2,1,0:T(8,128)(2,1)S(1)}, u32[]{:S(2)}, u32[]{:S(2)}) async-start(bf16[4,2,64,2048]{3,2,1,0:T(8,128)(2,1)} %pad_maximum_fusion), calls=%async_computation.4 | async-start | bytes 4194304 | tf_op jit(solution)/shard_map/all_to_all | solution.py:15
  142.3 1.6 pad_maximum_fusion.1
  143.9 0.1 dynamic-slice_bitcast_fusion.5
  144.0 0.1 pad_maximum_fusion.2
  144.2 0.9 constant_dynamic-slice_fusion
  145.1 2.1 collective-permute-start.9
  147.1 0.6 pad_add_fusion
  147.7 0.8 broadcast_in_dim.28
  148.5 2.3 collective-permute-start.15
  150.8 1.7 collective-permute-start.14
  152.5 1.3 collective-permute-start.13
  153.8 3.8 %collective-permute-start.12 = (bf16[4,64,256]{2,1,0:T(8,128)(2,1)}, bf16[4,64,256]{2,1,0:T(8,128)(2,1)}, u32[]{:S(2)}, u32[]{:S(2)}) collective-permute-start(bf16[4,64,256]{2,1,0:T(8,128)(2,1)} %get-tuple-element.40), channel_id=1, source_target_pairs={{0,4},{1,5},{2,6},{3,7},{4,0},{5,1},{6,2},{7,3},{8,12},{9,13},{10,... | collective-permute-start | bytes 393224 | tf_op jit(solution)/shard_map/ppermute | solution.py:27
  157.7 0.7 bitcast_dynamic-update-slice_fusion.7
  158.3 1.6 bitcast_dynamic-update-slice_fusion.6
  159.9 8.3 %collective-permute-done.10 = bf16[4,64,256]{2,1,0:T(8,128)(2,1)S(1)} collective-permute-done((bf16[4,64,256]{2,1,0:T(8,128)(2,1)}, bf16[4,64,256]{2,1,0:T(8,128)(2,1)S(1)}, u32[]{:S(2)}, u32[]{:S(2)}) %collective-permute-start.10) | collective-permute-done | bytes 131104 | tf_op jit(solution)/shard_map/ppermute | solution.py:27
  168.2 4.0 %collective-permute-start.11 = (bf16[4,64,256]{2,1,0:T(8,128)(2,1)}, bf16[4,64,256]{2,1,0:T(8,128)(2,1)S(1)}, u32[]{:S(2)}, u32[]{:S(2)}) collective-permute-start(bf16[4,64,256]{2,1,0:T(8,128)(2,1)} %get-tuple-element.41), channel_id=1, source_target_pairs={{0,3},{1,4},{2,5},{3,6},{4,7},{5,0},{6,1},{7,2},{8,11},{9,12},{10,... | collective-permute-start | bytes 393224 | tf_op jit(solution)/shard_map/ppermute | solution.py:27
  172.2 0.7 bitcast_dynamic-update-slice_fusion.5
  172.9 10.7 %collective-permute-done.11 = bf16[4,64,256]{2,1,0:T(8,128)(2,1)S(1)} collective-permute-done((bf16[4,64,256]{2,1,0:T(8,128)(2,1)}, bf16[4,64,256]{2,1,0:T(8,128)(2,1)S(1)}, u32[]{:S(2)}, u32[]{:S(2)}) %collective-permute-start.11) | collective-permute-done | bytes 131104 | tf_op jit(solution)/shard_map/ppermute | solution.py:27
  183.5 0.7 bitcast_dynamic-update-slice_fusion.4
  184.2 0.2 broadcast_in_dim.29.ids_ref
  184.4 6.3 %chosen_parts.1 = f32[32,16,128]{2,1,0:T(8,128)} custom-call(s32[4]{0:T(128)S(1)} %get-tuple-element.19.wanted_ref, s32[4]{0:T(128)S(1)} %get-tuple-element.15.slot_ref, bf16[8,4,32,2048]{3,2,1,0:T(8,128)(2,1)} %bitcast.87, s32[1024,128]{1,0:T(8,128)S(1)} %broadcast_in_dim.29.ids_ref, bf16[8,64,2048]{2,1,0:T(8,128)(2,1)S(1)} %bitcast.79, ...), custom_call_target="tpu_custom_call" | custom-call | flops 1073741824 | bytes 6291456 | tf_op jit(solution)/shard_map/chosen_parts/pallas_call | solution.py:98
  190.7 7.5 %all-to-all-start.4 = ((f32[32,16,128]{2,1,0:T(8,128)}), f32[32,16,128]{2,1,0:T(8,128)S(1)}, u32[]{:S(2)}, u32[]{:S(2)}) async-start(f32[32,16,128]{2,1,0:T(8,128)} %chosen_parts.1), calls=%async_computation.5 | async-start | bytes 524288 | tf_op jit(solution)/shard_map/all_to_all | solution.py:15
  198.2 1.6 bitcast_dynamic-update-slice_fusion.3
  199.8 1.6 bitcast_dynamic-update-slice_fusion.2
  201.4 1.6 bitcast_dynamic-update-slice_fusion.1
  202.9 5.0 %all-to-all-done.4 = f32[32,16,128]{2,1,0:T(8,128)S(1)} async-done(((f32[32,16,128]{2,1,0:T(8,128)}), f32[32,16,128]{2,1,0:T(8,128)S(1)}, u32[]{:S(2)}, u32[]{:S(2)}) %all-to-all-start.4) | async-done | bytes 262176 | tf_op jit(solution)/shard_map/all_to_all | solution.py:15
  207.9 0.7 broadcast_in_dim.30
  208.6 6.1 %all-to-all-start.5 = ((bf16[32,16,128]{2,1,0:T(8,128)(2,1)}), bf16[32,16,128]{2,1,0:T(8,128)(2,1)S(1)}, u32[]{:S(2)}, u32[]{:S(2)}) async-start(bf16[32,16,128]{2,1,0:T(8,128)(2,1)} %broadcast_in_dim.30), calls=%async_computation.6 | async-start | bytes 262144 | tf_op jit(solution)/shard_map/all_to_all | solution.py:15
  214.7 1.6 bitcast_dynamic-update-slice_fusion
  216.2 0.8 dynamic-slice_bitcast_fusion.9
  217.1 6.7 %all-to-all-done.5.low_ref = bf16[32,16,128]{2,1,0:T(8,128)(2,1)S(1)} async-done(((bf16[32,16,128]{2,1,0:T(8,128)(2,1)}), bf16[32,16,128]{2,1,0:T(8,128)(2,1)S(1)}, u32[]{:S(2)}, u32[]{:S(2)}) %all-to-all-start.5) | async-done | bytes 131104 | tf_op jit(solution)/shard_map/all_to_all | solution.py:15
  223.8 1.0 copy-done.2
  224.9 2.4 %final_rows.1 = bf16[1024,256]{1,0:T(8,128)(2,1)} custom-call(bf16[1024,256]{1,0:T(8,128)(2,1)S(1)} %bitcast.85, bf16[32,16,128]{2,1,0:T(8,128)(2,1)S(1)} %all-to-all-done.5.low_ref, s32[1024,128]{1,0:T(8,128)S(1)} %broadcast_in_dim.29.ids_ref, bf16[256,256]{1,0:T(8,128)(2,1)S(1)} %pad_maximum_fusion.4.up_ref), custom_call_target="tpu_custom_call" | custom-call | flops 134217728 | bytes 2097152 | tf_op jit(solution)/shard_map/final_rows/pallas_call | solution.py:138
  (47 shorter events, 0.2 us)
Async XLA Ops:
  6.5 59.4 %copy-start = (s32[64]{0:T(128)S(1)}, s32[64]{0:T(128)}, u32[]{:S(2)}) copy-start(s32[64]{0:T(128)} %param.11) | copy-start | bytes 772
  6.5 73.8 %all-gather.2.cloned.1.call-start = ((), (), s32[]{:S(2)}) async-start(), calls=%async_computation.7 | async-start | bytes 4718592 | tf_op jit(solution)/shard_map/all_gather | solution.py:169
  33.0 5.6 %copy-start.6 = (s32[32]{0:T(128)S(1)}, s32[32]{0:T(128)}, u32[]{:S(2)}) copy-start(s32[32]{0:T(128)} %param.13) | copy-start | bytes 388
  33.0 7.3 %copy-start.7 = (s32[4]{0:T(128)S(1)}, s32[4]{0:T(128)}, u32[]{:S(2)}) copy-start(s32[4]{0:T(128)} %param.12) | copy-start | bytes 52
  33.0 28.9 %all-to-all-start.2 = ((bf16[4,256,1024]{2,1,0:T(8,128)(2,1)}), bf16[4,256,1024]{2,1,0:T(8,128)(2,1)S(1)}, u32[]{:S(2)}, u32[]{:S(2)}) async-start(bf16[4,256,1024]{2,1,0:T(8,128)(2,1)} %broadcast_in_dim.26), calls=%async_computation.2 | async-start | bytes 4194304 | tf_op jit(solution)/shard_map/all_to_all | solution.py:15
  38.6 185.2 %reduce-scatter.2.cloned.1.call-start = ((), (), s32[]{:S(2)}) async-start(), calls=%async_computation.8 | async-start | bytes 2621440 | tf_op jit(solution)/shard_map/reduce_scatter | solution.py:202
  38.6 38.7 %collective-permute-start.1 = (s32[1,32]{1,0:T(1,128)S(1)}, s32[1,32]{1,0:T(1,128)S(1)}, u32[]{:S(2)}, u32[]{:S(2)}) collective-permute-start(s32[1,32]{1,0:T(1,128)S(1)} %bitcast.92), channel_id=1, source_target_pairs={{0,1},{1,0},{2,3},{3,2},{4,5},{5,4},{6,7},{7,6},{8,9},{9,8},{10,11... | collective-permute-start | bytes 392 | tf_op jit(solution)/shard_map/ppermute | solution.py:33
  61.9 18.4 %collective-permute-start = (bf16[1024,1024]{1,0:T(8,128)(2,1)S(1)}, bf16[1024,1024]{1,0:T(8,128)(2,1)}, u32[]{:S(2)}, u32[]{:S(2)}) collective-permute-start(bf16[1024,1024]{1,0:T(8,128)(2,1)S(1)} %bitcast.83), channel_id=1, source_target_pairs={{0,32},{32,0},{1,33},{33,1},{2,34},{34,2},{3,35},{35,3},{4,36},{36... | collective-permute-start | bytes 6291464 | tf_op jit(solution)/shard_map/ppermute | solution.py:27
  72.5 2.9 %copy-start.3 = (bf16[2,64,8192]{2,1,0:T(8,128)(2,1)S(1)}, bf16[2,64,8192]{2,1,0:T(8,128)(2,1)}, u32[]{:S(2)}) copy-start(bf16[2,64,8192]{2,1,0:T(8,128)(2,1)} %param.9) | copy-start | bytes 6291460
  77.3 11.6 %collective-permute-start.2 = (s32[2,32]{1,0:T(2,128)S(1)}, s32[2,32]{1,0:T(2,128)S(1)}, u32[]{:S(2)}, u32[]{:S(2)}) collective-permute-start(s32[2,32]{1,0:T(2,128)S(1)} %pad_add_fusion.4), channel_id=1, source_target_pairs={{0,2},{1,3},{2,0},{3,1},{4,6},{5,7},{6,4},{7,5},{8,10},{9,11},{10,... | collective-permute-start | bytes 776 | tf_op jit(solution)/shard_map/ppermute | solution.py:33
  87.5 1.4 copy-start.1
  88.9 6.4 %collective-permute-start.3 = (s32[4,32]{1,0:T(4,128)S(1)}, s32[4,32]{1,0:T(4,128)S(1)}, u32[]{:S(2)}, u32[]{:S(2)}) collective-permute-start(s32[4,32]{1,0:T(4,128)S(1)} %pad_add_fusion.3), channel_id=1, source_target_pairs={{0,4},{1,5},{2,6},{3,7},{4,0},{5,1},{6,2},{7,3},{8,12},{9,13},{10,... | collective-permute-start | bytes 1544 | tf_op jit(solution)/shard_map/ppermute | solution.py:33
  95.4 4.0 %collective-permute-start.4 = (s32[8,32]{1,0:T(8,128)S(1)}, s32[8,32]{1,0:T(8,128)S(1)}, u32[]{:S(2)}, u32[]{:S(2)}) collective-permute-start(s32[8,32]{1,0:T(8,128)S(1)} %pad_add_fusion.2), channel_id=1, source_target_pairs={{0,8},{8,0},{16,24},{24,16},{1,9},{9,1},{17,25},{25,17},{2,10},{10... | collective-permute-start | bytes 3080 | tf_op jit(solution)/shard_map/ppermute | solution.py:33
  95.8 46.5 %collective-permute-start.7 = (bf16[2,64,2048]{2,1,0:T(8,128)(2,1)}, bf16[2,64,2048]{2,1,0:T(8,128)(2,1)}, u32[]{:S(2)}, u32[]{:S(2)}) collective-permute-start(bf16[2,64,2048]{2,1,0:T(8,128)(2,1)} %get-tuple-element.13), channel_id=1, source_target_pairs={{0,16},{8,24},{16,0},{24,8},{1,17},{9,25},{17,1},{25,9},{2,18},{10... | collective-permute-start | bytes 1572872 | tf_op jit(solution)/shard_map/ppermute | solution.py:27
  97.6 44.7 %collective-permute-start.8 = (bf16[2,64,2048]{2,1,0:T(8,128)(2,1)}, bf16[2,64,2048]{2,1,0:T(8,128)(2,1)}, u32[]{:S(2)}, u32[]{:S(2)}) collective-permute-start(bf16[2,64,2048]{2,1,0:T(8,128)(2,1)} %get-tuple-element.14), channel_id=1, source_target_pairs={{0,24},{8,0},{16,8},{24,16},{1,25},{9,1},{17,9},{25,17},{2,26},{10... | collective-permute-start | bytes 1572872 | tf_op jit(solution)/shard_map/ppermute | solution.py:27
  99.3 43.0 %collective-permute-start.6 = (bf16[2,64,2048]{2,1,0:T(8,128)(2,1)S(1)}, bf16[2,64,2048]{2,1,0:T(8,128)(2,1)}, u32[]{:S(2)}, u32[]{:S(2)}) collective-permute-start(bf16[2,64,2048]{2,1,0:T(8,128)(2,1)S(1)} %get-tuple-element.12), channel_id=1, source_target_pairs={{0,8},{8,16},{16,24},{24,0},{1,9},{9,17},{17,25},{25,1},{2,10},{10... | collective-permute-start | bytes 1572872 | tf_op jit(solution)/shard_map/ppermute | solution.py:27
  99.4 38.7 %collective-permute-start.5 = (s32[16,32]{1,0:T(8,128)S(1)}, s32[16,32]{1,0:T(8,128)S(1)}, u32[]{:S(2)}, u32[]{:S(2)}) collective-permute-start(s32[16,32]{1,0:T(8,128)S(1)} %pad_add_fusion.1), channel_id=1, source_target_pairs={{0,16},{8,24},{16,0},{24,8},{1,17},{9,25},{17,1},{25,9},{2,18},{10... | collective-permute-start | bytes 6152 | tf_op jit(solution)/shard_map/ppermute | solution.py:33
  138.7 45.5 %all-to-all-start.3 = ((bf16[4,2,64,2048]{3,2,1,0:T(8,128)(2,1)}), bf16[4,2,64,2048]{3,2,1,0:T(8,128)(2,1)S(1)}, u32[]{:S(2)}, u32[]{:S(2)}) async-start(bf16[4,2,64,2048]{3,2,1,0:T(8,128)(2,1)} %pad_maximum_fusion), calls=%async_computation.4 | async-start | bytes 4194304 | tf_op jit(solution)/shard_map/all_to_all | solution.py:15
  144.0 3.1 %copy-start.4 = (s32[16,32]{1,0:T(8,128)S(1)}, s32[16,32]{1,0:T(8,128)}, u32[]{:S(2)}) copy-start(s32[16,32]{1,0:T(8,128)} %get-tuple-element.48) | copy-start | bytes 6148
  144.0 3.1 %copy-start.5 = (s32[16,32]{1,0:T(8,128)S(1)}, s32[16,32]{1,0:T(8,128)}, u32[]{:S(2)}) copy-start(s32[16,32]{1,0:T(8,128)} %get-tuple-element.49) | copy-start | bytes 6148
  145.1 13.3 %collective-permute-start.9 = (bf16[4,64,256]{2,1,0:T(8,128)(2,1)}, bf16[4,64,256]{2,1,0:T(8,128)(2,1)}, u32[]{:S(2)}, u32[]{:S(2)}) collective-permute-start(bf16[4,64,256]{2,1,0:T(8,128)(2,1)} %get-tuple-element.43), channel_id=1, source_target_pairs={{0,1},{1,2},{2,3},{3,4},{4,5},{5,6},{6,7},{7,0},{8,9},{9,10},{10,1... | collective-permute-start | bytes 393224 | tf_op jit(solution)/shard_map/ppermute | solution.py:27
  148.5 66.1 %collective-permute-start.15 = (bf16[4,64,256]{2,1,0:T(8,128)(2,1)S(1)}, bf16[4,64,256]{2,1,0:T(8,128)(2,1)}, u32[]{:S(2)}, u32[]{:S(2)}) collective-permute-start(bf16[4,64,256]{2,1,0:T(8,128)(2,1)S(1)} %get-tuple-element.37), channel_id=1, source_target_pairs={{0,7},{1,0},{2,1},{3,2},{4,3},{5,4},{6,5},{7,6},{8,15},{9,8},{10,9... | collective-permute-start | bytes 393224 | tf_op jit(solution)/shard_map/ppermute | solution.py:27
  150.8 50.6 %collective-permute-start.14 = (bf16[4,64,256]{2,1,0:T(8,128)(2,1)S(1)}, bf16[4,64,256]{2,1,0:T(8,128)(2,1)}, u32[]{:S(2)}, u32[]{:S(2)}) collective-permute-start(bf16[4,64,256]{2,1,0:T(8,128)(2,1)S(1)} %get-tuple-element.38), channel_id=1, source_target_pairs={{0,6},{1,7},{2,0},{3,1},{4,2},{5,3},{6,4},{7,5},{8,14},{9,15},{10,... | collective-permute-start | bytes 393224 | tf_op jit(solution)/shard_map/ppermute | solution.py:27
  152.5 47.3 %collective-permute-start.13 = (bf16[4,64,256]{2,1,0:T(8,128)(2,1)S(1)}, bf16[4,64,256]{2,1,0:T(8,128)(2,1)}, u32[]{:S(2)}, u32[]{:S(2)}) collective-permute-start(bf16[4,64,256]{2,1,0:T(8,128)(2,1)S(1)} %get-tuple-element.39), channel_id=1, source_target_pairs={{0,5},{1,6},{2,7},{3,0},{4,1},{5,2},{6,3},{7,4},{8,13},{9,14},{10,... | collective-permute-start | bytes 393224 | tf_op jit(solution)/shard_map/ppermute | solution.py:27
  153.8 44.4 %collective-permute-start.12 = (bf16[4,64,256]{2,1,0:T(8,128)(2,1)}, bf16[4,64,256]{2,1,0:T(8,128)(2,1)}, u32[]{:S(2)}, u32[]{:S(2)}) collective-permute-start(bf16[4,64,256]{2,1,0:T(8,128)(2,1)} %get-tuple-element.40), channel_id=1, source_target_pairs={{0,4},{1,5},{2,6},{3,7},{4,0},{5,1},{6,2},{7,3},{8,12},{9,13},{10,... | collective-permute-start | bytes 393224 | tf_op jit(solution)/shard_map/ppermute | solution.py:27
  158.3 9.9 %collective-permute-start.10 = (bf16[4,64,256]{2,1,0:T(8,128)(2,1)}, bf16[4,64,256]{2,1,0:T(8,128)(2,1)S(1)}, u32[]{:S(2)}, u32[]{:S(2)}) collective-permute-start(bf16[4,64,256]{2,1,0:T(8,128)(2,1)} %get-tuple-element.42), channel_id=1, source_target_pairs={{0,2},{1,3},{2,4},{3,5},{4,6},{5,7},{6,0},{7,1},{8,10},{9,11},{10,... | collective-permute-start | bytes 393224 | tf_op jit(solution)/shard_map/ppermute | solution.py:27
  168.2 15.3 %collective-permute-start.11 = (bf16[4,64,256]{2,1,0:T(8,128)(2,1)}, bf16[4,64,256]{2,1,0:T(8,128)(2,1)S(1)}, u32[]{:S(2)}, u32[]{:S(2)}) collective-permute-start(bf16[4,64,256]{2,1,0:T(8,128)(2,1)} %get-tuple-element.41), channel_id=1, source_target_pairs={{0,3},{1,4},{2,5},{3,6},{4,7},{5,0},{6,1},{7,2},{8,11},{9,12},{10,... | collective-permute-start | bytes 393224 | tf_op jit(solution)/shard_map/ppermute | solution.py:27
  190.7 17.2 %all-to-all-start.4 = ((f32[32,16,128]{2,1,0:T(8,128)}), f32[32,16,128]{2,1,0:T(8,128)S(1)}, u32[]{:S(2)}, u32[]{:S(2)}) async-start(f32[32,16,128]{2,1,0:T(8,128)} %chosen_parts.1), calls=%async_computation.5 | async-start | bytes 524288 | tf_op jit(solution)/shard_map/all_to_all | solution.py:15
  208.6 15.2 %all-to-all-start.5 = ((bf16[32,16,128]{2,1,0:T(8,128)(2,1)}), bf16[32,16,128]{2,1,0:T(8,128)(2,1)S(1)}, u32[]{:S(2)}, u32[]{:S(2)}) async-start(bf16[32,16,128]{2,1,0:T(8,128)(2,1)} %broadcast_in_dim.30), calls=%async_computation.6 | async-start | bytes 262144 | tf_op jit(solution)/shard_map/all_to_all | solution.py:15
  223.8 1.0 copy-start.2
Sparse Core Ops, SparseCore 0:
  20.6 57.7 all-gather.1
  89.0 51.6 reduce-scatter.1

commit v3 on v1

v3 whole, which is shorter than its diff:
```python
import functools

import jax
import jax.numpy as jnp
from jax import lax
from jax.experimental import pallas as pl
from jax.experimental.pallas import tpu as pltpu
from jax.sharding import Mesh, PartitionSpec as P

adapter_scale = 2.0
mebibyte = 1024 * 1024


def swap(value, axis):
    return lax.all_to_all(value, axis, split_axis=0, concat_axis=0, tiled=True)


def after(value, *earlier):
    return lax.optimization_barrier((value,) + earlier)[0]


def shift(value, axis, size, by):
    return lax.ppermute(value, axis, [(i, (i + by) % size) for i in range(size)])


def doubled(value, axis, size, place):
    bit = 1
    while bit < size:
        other = lax.ppermute(value, axis, [(i, i ^ bit) for i in range(size)])
        high = (place & bit) != 0
        value = jnp.concatenate([jnp.where(high, other, value), jnp.where(high, value, other)])
        bit *= 2
    return value


def send_kernel(place_ref, tokens_ref, *rest):
    half = len(rest) // 2
    rows = tokens_ref.shape[0]
    for d in range(half):
        block_ref, out_ref = rest[d], rest[half + d]
        part, width = out_ref.shape[1], block_ref.shape[2]
        short = out_ref.shape[0] - rows
        first = (place_ref[2] + d) % half * part
        out_ref[:rows] = tokens_ref[:, pl.ds(pl.multiple_of(first, part), part)]
        for k in range(part // width):
            out_ref[rows:, k * width : (k + 1) * width] = block_ref[0, k * short : (k + 1) * short]


def send_parts(place, tokens, weights, ny, group):
    rows, width = tokens.shape
    _, sub, width_out = weights.shape
    part = width // ny
    short = sub * width_out // part

    def block_spec(d):
        return pl.BlockSpec(
            (1, sub, width_out), lambda i, p: ((p[2] + d) % ny * group + p[1] * (group // 2) + p[0], 0, 0)
        )

    return pl.pallas_call(
        send_kernel,
        out_shape=[jax.ShapeDtypeStruct((rows + short, part), tokens.dtype)] * ny,
        grid_spec=pltpu.PrefetchScalarGridSpec(
            num_scalar_prefetch=1,
            grid=(1,),
            in_specs=[pl.BlockSpec(tokens.shape, lambda i, p: (0, 0))] + [block_spec(d) for d in range(ny)],
            out_specs=[pl.BlockSpec((rows + short, part), lambda i, p: (0, 0))] * ny,
        ),
        compiler_params=pltpu.CompilerParams(vmem_limit_bytes=60 * mebibyte),
        cost_estimate=pl.CostEstimate(flops=0, bytes_accessed=2 * mebibyte, transcendentals=0),
        name="send_parts",
    )(place, tokens, *([weights] * ny))


def arrive_kernel(*refs):
    arrived, far_ref, piece_ref = refs[:-2], refs[-2], refs[-1]
    rows = far_ref.shape[0] // len(arrived)
    width = piece_ref.shape[1] // len(arrived)
    short = arrived[0].shape[0] - rows
    for d, ref in enumerate(arrived):
        far_ref[d * rows : (d + 1) * rows] = ref[:rows]
        for k in range(ref.shape[1] // width):
            piece_ref[k * short : (k + 1) * short, d * width : (d + 1) * width] = ref[
                rows:, k * width : (k + 1) * width
            ]


def arrive_parts(arrived, rows, sub, width_out):
    count = len(arrived)
    part = arrived[0].shape[1]
    return pl.pallas_call(
        arrive_kernel,
        out_shape=[
            jax.ShapeDtypeStruct((count * rows, part), arrived[0].dtype),
            jax.ShapeDtypeStruct((sub, count * width_out), arrived[0].dtype),
        ],
        compiler_params=pltpu.CompilerParams(vmem_limit_bytes=8 * mebibyte),
        cost_estimate=pl.CostEstimate(flops=0, bytes_accessed=2 * mebibyte, transcendentals=0),
        name="arrive_parts",
    )(*arrived)


def cut_kernel(*refs):
    count = (len(refs) - 2) // 3
    pools, outs, held, arrived, left = refs[:count], refs[count : 2 * count], refs[2 * count : -2], refs[-2], refs[-1]

    def pool_of(j):
        return pltpu.make_async_copy(pools[j], held[j], arrived.at[j])

    def piece_of(j, k):
        part = outs[j].shape[3]
        return pltpu.make_async_copy(held[j].at[:, :, pl.ds(k * part, part)], outs[j].at[k], left.at[j, k])

    for j in range(count):
        pool_of(j).start()
    for j in range(count):
        pool_of(j).wait()
        for k in range(outs[j].shape[0]):
            piece_of(j, k).start()
    for j in range(count):
        for k in range(outs[j].shape[0]):
            piece_of(j, k).wait()


def cut_parts(pools, count):
    held, rank, width = pools[0].shape
    where = pl.BlockSpec(memory_space=pl.ANY)
    return pl.pallas_call(
        cut_kernel,
        out_shape=[jax.ShapeDtypeStruct((count, held, rank, width // count), p.dtype) for p in pools],
        in_specs=[where] * len(pools),
        out_specs=[where] * len(pools),
        scratch_shapes=[pltpu.VMEM(p.shape, p.dtype) for p in pools]
        + [pltpu.SemaphoreType.DMA((len(pools),)), pltpu.SemaphoreType.DMA((len(pools), count))],
        compiler_params=pltpu.CompilerParams(vmem_limit_bytes=60 * mebibyte),
        cost_estimate=pl.CostEstimate(flops=0, bytes_accessed=8 * mebibyte, transcendentals=0),
        name="cut_parts",
    )(*pools)


def pick_kernel(slot_ref, wanted_ref, pool_ref, out_ref):
    width = out_ref.shape[3]
    wanted = wanted_ref[pl.program_id(0)] != 0
    for k in range(out_ref.shape[0]):
        piece = pool_ref[0, :, k * width : (k + 1) * width]
        out_ref[k, 0] = jnp.where(wanted, piece, jnp.zeros_like(piece))


def pick_parts(slots, wanted, pool, pieces):
    _, rank, part = pool.shape
    count = slots.shape[0]
    width = part // pieces
    return pl.pallas_call(
        pick_kernel,
        out_shape=jax.ShapeDtypeStruct((pieces, count, rank, width), pool.dtype),
        grid_spec=pltpu.PrefetchScalarGridSpec(
            num_scalar_prefetch=2,
            grid=(count,),
            in_specs=[pl.BlockSpec((1, rank, part), lambda i, s, w: (s[i], 0, 0))],
            out_specs=pl.BlockSpec((pieces, 1, rank, width), lambda i, s, w: (0, i, 0, 0)),
        ),
        compiler_params=pltpu.CompilerParams(vmem_limit_bytes=12 * mebibyte),
        cost_estimate=pl.CostEstimate(flops=0, bytes_accessed=4 * count * rank * part, transcendentals=0),
        name="pick_parts",
    )(slots, wanted, pool)


def order_kernel(place_ref, *refs):
    out_ref = refs[-1]
    count = len(refs) - 1
    sub = refs[0].shape[0]
    for e in range(count):
        first = (place_ref[0] + count - e) % count * sub
        out_ref[pl.ds(pl.multiple_of(first, sub), sub)] = refs[e][...]


def order_parts(place, pieces):
    sub, wide = pieces[0].shape
    near = pl.BlockSpec(memory_space=pltpu.VMEM)
    return pl.pallas_call(
        order_kernel,
        out_shape=jax.ShapeDtypeStruct((len(pieces) * sub, wide), pieces[0].dtype),
        in_specs=[pl.BlockSpec(memory_space=pltpu.SMEM)] + [near] * len(pieces),
        out_specs=near,
        compiler_params=pltpu.CompilerParams(vmem_limit_bytes=8 * mebibyte),
        cost_estimate=pl.CostEstimate(flops=0, bytes_accessed=4 * mebibyte, transcendentals=0),
        name="order_parts",
    )(place, *pieces)


def part_kernel(place_ref, wanted_ref, slot_ref, gathered_ref, mine_ref, other_ref, pool_ref, ids_ref, *rest):
    ny = gathered_ref.shape[1]
    outs, chosen_ref = rest[:ny], rest[ny]
    rows_ref, weight_ref, down_ref, held_ref, arrived, weighed, downed, left = rest[ny + 1 :]
    half = mine_ref.shape[0]
    _, nz, rows, part = rows_ref.shape
    width = outs[0].shape[1]
    rank = pool_ref.shape[1]
    count = slot_ref.shape[0]
    block = nz * rows
    blocks = 2

    def owner_of(k):
        return (place_ref[2] + ny - k) % ny

    def owned(k):
        return pl.ds(pl.multiple_of(owner_of(k) * block, block), block)

    def lines_of(k):
        return pltpu.make_async_copy(gathered_ref.at[:, k], rows_ref.at[k], arrived.at[k])

    def weight_of(j, ref):
        return pltpu.make_async_copy(ref, weight_ref.at[j], weighed.at[j])

    def down_of(s):
        return pltpu.make_async_copy(pool_ref.at[slot_ref[s]], down_ref.at[pl.ds(s * rank, rank)], downed.at[s])

    def result_of(d, k):
        return pltpu.make_async_copy(held_ref.at[d, k], outs[d].at[owned(k)], left.at[d, k])

    weight_of(0, mine_ref).start()
    for k in range(blocks):
        lines_of(k).start()
    weight_of(1, other_ref).start()
    for k in range(blocks, ny):
        lines_of(k).start()
    for s in range(count):
        down_of(s).start()

    for step in range(ny // blocks):
        for k in range(blocks):
            lines_of(step * blocks + k).wait()
        here = pl.ds(step * blocks, blocks)
        total = None
        for j, (ref, core) in enumerate(((mine_ref, place_ref[1]), (other_ref, 1 - place_ref[1]))):
            if step == 0:
                weight_of(j, ref).wait()
            lines = rows_ref[here, :, :, pl.ds(pl.multiple_of(core * half, half), half)].reshape(blocks * block, half)
            product = jnp.dot(lines, weight_ref[j], preferred_element_type=jnp.float32)
            total = product if total is None else total + product
        for k in range(blocks):
            for d in range(ny):
                piece = total[k * block : (k + 1) * block, d * width : (d + 1) * width]
                held_ref[d, step * blocks + k] = piece.astype(held_ref.dtype)
                result_of(d, step * blocks + k).start()

    for s in range(count):
        down_of(s).wait()
    lane = lax.broadcasted_iota(jnp.int32, (block, 2 * rank), 1)
    targets = [jnp.where(lane < rank, wanted_ref[s], wanted_ref[s + 1]) for s in range(0, count, 2)]
    for k in range(ny):
        product = lax.dot_general(
            rows_ref[k].reshape(block, part),
            down_ref[...],
            (((1,), (1,)), ((), ())),
            preferred_element_type=jnp.float32,
        )
        ids = ids_ref[owned(k)]
        chosen = jnp.zeros((block, 2 * rank), jnp.float32)
        for j, target in enumerate(targets):
            chosen += jnp.where(ids == target, product[:, 2 * j * rank : 2 * (j + 1) * rank], 0.0)
        chosen = chosen[:, :rank] + chosen[:, rank:]
        for j in range(nz):
            piece = chosen[j * rows : (j + 1) * rows]
            chosen_ref[owner_of(k) * nz + j] = jnp.concatenate([piece[: rows // 2], piece[rows // 2 :]], axis=1)
    for k in range(ny):
        for d in range(ny):
            result_of(d, k).wait()


def part_products(place, wanted, slots, gathered, mine, other, down, ids, width_out):
    nz, ny, rows, part = gathered.shape
    _, rank, _ = down.shape
    count = slots.shape[0]
    scalars = pl.BlockSpec(memory_space=pltpu.SMEM)
    where = pl.BlockSpec(memory_space=pl.ANY)
    near = pl.BlockSpec(memory_space=pltpu.VMEM)
    kind = gathered.dtype
    *base, chosen = pl.pallas_call(
        part_kernel,
        out_shape=[jax.ShapeDtypeStruct((ny * nz * rows, width_out), kind)] * ny
        + [jax.ShapeDtypeStruct((ny * nz, rows // 2, 2 * rank), jnp.float32)],
        in_specs=[scalars, scalars, scalars, where, where, where, where, near],
        out_specs=[where] * ny + [near],
        scratch_shapes=[
            pltpu.VMEM((ny, nz, rows, part), kind),
            pltpu.VMEM((2,) + mine.shape, kind),
            pltpu.VMEM((count * rank, part), kind),
            pltpu.VMEM((ny, ny, nz * rows, width_out), kind),
            pltpu.SemaphoreType.DMA((ny,)),
            pltpu.SemaphoreType.DMA((2,)),
            pltpu.SemaphoreType.DMA((count,)),
            pltpu.SemaphoreType.DMA((ny, ny)),
        ],
        compiler_params=pltpu.CompilerParams(vmem_limit_bytes=50 * mebibyte),
        cost_estimate=pl.CostEstimate(
            flops=2 * ny * nz * rows * part * (ny * width_out + count * rank),
            bytes_accessed=12 * mebibyte,
            transcendentals=0,
        ),
        name="part_products",
    )(place, wanted, slots, gathered, mine, other, down, ids)
    return base, chosen


def lower_kernel(parts_ref, out_ref):
    low = jnp.sum(parts_ref[...], axis=0).astype(out_ref.dtype)
    for k in range(out_ref.shape[0]):
        out_ref[k] = low


def lower_parts(parts):
    near = pl.BlockSpec(memory_space=pltpu.VMEM)
    return pl.pallas_call(
        lower_kernel,
        out_shape=jax.ShapeDtypeStruct(parts.shape, jnp.bfloat16),
        in_specs=[near],
        out_specs=near,
        compiler_params=pltpu.CompilerParams(vmem_limit_bytes=8 * mebibyte),
        cost_estimate=pl.CostEstimate(flops=0, bytes_accessed=mebibyte, transcendentals=0),
        name="lower_parts",
    )(parts)


def final_kernel(low_ref, ids_ref, up_ref, *rest):
    base, out_ref = rest[:-1], rest[-1]
    count, rank, width = up_ref.shape
    low = jnp.concatenate(
        [low_ref[k][:, h * rank : (h + 1) * rank] for k in range(low_ref.shape[0]) for h in range(2)], axis=0
    )
    low = jnp.concatenate([low, low], axis=1).astype(jnp.float32)
    lane = lax.broadcasted_iota(jnp.int32, low.shape, 1)
    kept = [
        jnp.where(ids_ref[...] == jnp.where(lane < rank, s, s + 1), low, 0.0).astype(jnp.bfloat16)
        for s in range(0, count, 2)
    ]
    up = up_ref[...].reshape(count * rank, width)
    update = jnp.dot(jnp.concatenate(kept, axis=1), up, preferred_element_type=jnp.float32)
    total = base[0][...].astype(jnp.float32)
    for ref in base[1:]:
        total += ref[...].astype(jnp.float32)
    out_ref[...] = (total + adapter_scale * update).astype(out_ref.dtype)


def final_rows(low, ids, ups, base):
    tall, width_out = base[0].shape
    count, rank, _ = ups.shape
    near = pl.BlockSpec(memory_space=pltpu.VMEM)
    return pl.pallas_call(
        final_kernel,
        out_shape=jax.ShapeDtypeStruct((tall, width_out), jnp.bfloat16),
        in_specs=[near] * (3 + len(base)),
        out_specs=near,
        compiler_params=pltpu.CompilerParams(vmem_limit_bytes=16 * mebibyte),
        cost_estimate=pl.CostEstimate(
            flops=2 * tall * count * rank * width_out, bytes_accessed=4 * mebibyte, transcendentals=0
        ),
        name="final_rows",
    )(low, ids, ups, *base)


def per_device(nx, nc, ny, nz, tokens, base_weight, down_pool, up_pool, slot_of, requested, row_adapter):
    rows, width = tokens.shape
    width_out = base_weight.shape[1]
    held, rank, _ = down_pool.shape
    count_new = requested.shape[0]
    part = width // ny
    sub = part // (nx * nc)
    nt = ny * nz
    x, core, y, z = [lax.axis_index(a).astype(jnp.int32) for a in ("x", "core", "y", "z")]
    place = jnp.stack([x, core, y, z])

    weights = base_weight.reshape(ny * nc * nx, sub, width_out)
    sent = send_parts(place, tokens, weights, ny, nc * nx)
    down, up = cut_parts([down_pool, after(up_pool, sent[1])], ny)
    arrived = [after(sent[0], down, up)] + [shift(sent[d], "y", ny, d) for d in range(1, ny)]
    far, piece = arrive_parts(arrived, rows, sub, width_out)
    gathered = lax.all_gather(far, "z", axis=0, tiled=True).reshape(nz, ny, rows, part)

    pool_rows = slot_of[requested]
    home, local = pool_rows // held, pool_rows % held
    home_y, home_z = home // nz, home % nz
    slots = home_y * held + local

    down = swap(down, "y").reshape(ny * held, rank, part)

    ids = doubled(after(row_adapter, sent[1]).reshape(1, rows), "z", nz, z)
    ids = doubled(ids, "y", ny, y)

    piece = order_parts(place, [shift(piece, "x", nx, e) if e else piece for e in range(nx)])
    other = shift(piece, "core", nc, 1)

    ups = swap(after(up, down, ids), "y").reshape(ny * held, rank, part)
    ups = pick_parts(slots, (home_z == z).astype(jnp.int32), ups, nz)
    other = after(other, ups)
    ups = lax.psum_scatter(ups, "z", scatter_dimension=0, tiled=True)[0]

    wanted = jnp.where(home_z == z, jnp.arange(count_new, dtype=jnp.int32), -1)
    ids = jnp.broadcast_to(ids.reshape(nt * rows, 1), (nt * rows, 2 * rank))
    base, chosen = part_products(place, wanted, slots, gathered, piece, other, down, ids, width_out)
    base = [shift(part, "y", ny, ny - d) if d else part for d, part in enumerate(base)]
    lowered = swap(lower_parts(swap(chosen, ("y", "z"))), ("y", "z"))
    return final_rows(lowered, ids, ups, base)


def solution(mesh):
    nx, nc, ny, nz = 4, 2, 4, 8
    fine = Mesh(mesh.devices.reshape(nx, nc, ny, nz), ("x", "core", "y", "z"))
    group, tensor = ("x", "core"), ("y", "z")
    both = group + tensor
    placed = (
        P(both, None),
        P(None, tensor),
        P(both, None, None),
        P(both, None, None),
        P(group),
        P(group),
        P(both),
    )

    def step(*args):
        return per_device(nx, nc, ny, nz, *args)

    return jax.shard_map(step, mesh=fine, in_specs=placed, out_specs=P(group, tensor), check_vma=False)
```

time: 246 us -> 160 us (0.65); the launches traced: 243 us -> 159 us
  local copies, waits for them, and re-layouts: 35.4 us -> 3.99 us
  blocking collectives: 27.5 us -> 0 us
  Pallas kernels: 0 us -> 27 us
  matrix products: 19.2 us -> 0 us
  waiting for transfers between devices: 82 us -> 63 us
  between operations: 26.9 us -> 13.6 us
  other arithmetic: 10.7 us -> 0.7 us
  starting transfers between devices: 40.9 us -> 50.9 us
    all_to_all x9 -> x4, waiting for transfers between devices: 82 us -> 8.49 us  [swap(): return lax.all_to_all(value, axis, split_axis=0, concat_axis=0, tiled=True)]
    ppermute x0 -> x15, waiting for transfers between devices: none -> 54.4 us  [the longest x10 42.6 us: shift(): lax.ppermute(value, axis, [(i, (i + by) % size) for i in range(size)])]
    ppermute x0 -> x15, starting transfers between devices: none -> 27.9 us  [the longest x5 14.9 us: doubled(): other = lax.ppermute(value, axis, [(i, i ^ bit) for i in range(size)])]
    all_to_all x2 -> x0, blocking collectives: 27.5 us -> none  [swap(): return lax.all_to_all(value, axis, split_axis=0, concat_axis=0, tiled=True)]
    pallas_call x0 -> x8, Pallas kernels: none -> 27 us  [the longest x1 12.6 us: part_products(): pl.pallas_call(part_kernel, out_shape=[jax.ShapeDtypeStruct((ny * nz * ro...]
    dot_general x6 -> x0, matrix products: 19.2 us -> none  [the longest x4 13.6 us: per_device(): jnp.dot(gathered, weight[:, k * width_out:(k + 1) * width_out], preferred...]
    all_to_all x9 -> x4, starting transfers between devices: 40.9 us -> 23 us  [swap(): return lax.all_to_all(value, axis, split_axis=0, concat_axis=0, tiled=True)]
    reshape x4 -> x0, local copies, waits for them, and re-layouts: 10.3 us -> none  [the longest x1 3.34 us: per_device(): down_pool.reshape(held, rank, ny, part).transpose(2, 0, 1, 3)]
  transfers between devices with their start and end apart: 10 -> 21, of which waited for: 8 -> 14; matrix products, arithmetic and copies ran while one was open for 24% -> 1% of each run, Pallas kernels for 0% -> 14%
where the time goes in v3:
time: 160 us; the launch traced here: 159 us
  waiting for transfers between devices  63 us (39%)
  starting transfers between devices  50.9 us (32%)
  Pallas kernels  27 us (17%)
  between operations  13.6 us (8%)
  local copies, waits for them, and re-layouts  3.99 us (2%)
    ppermute x10, waiting for transfers between devices, shift(): lax.ppermute(value, axis, [(i, (i + by) % size) for i in range(size)])  42.6 us
    all_to_all x4, starting transfers between devices, swap(): return lax.all_to_all(value, axis, split_axis=0, concat_axis=0, tiled=True)  23 us
    ppermute x5, starting transfers between devices, doubled(): other = lax.ppermute(value, axis, [(i, i ^ bit) for i in range(size)])  14.9 us
    ppermute x10, starting transfers between devices, shift(): lax.ppermute(value, axis, [(i, (i + by) % size) for i in range(size)])  13 us
    pallas_call x1, Pallas kernels, part_products(): pl.pallas_call(part_kernel, out_shape=[jax.ShapeDtypeStruct((ny * nz * ro...  12.6 us
    ppermute x5, waiting for transfers between devices, doubled(): other = lax.ppermute(value, axis, [(i, i ^ bit) for i in range(size)])  11.8 us
    all_to_all x4, waiting for transfers between devices, swap(): return lax.all_to_all(value, axis, split_axis=0, concat_axis=0, tiled=True)  8.49 us
    pallas_call x1, Pallas kernels, cut_parts(): pl.pallas_call(cut_kernel, out_shape=[jax.ShapeDtypeStruct((count, held,...  3.72 us
  transfers between devices with their start and end apart: 21, of which 14 were waited for; matrix products, arithmetic and copies ran while one was open for 1% of the time, Pallas kernels for 14%

profile of v3, /device:TPU:1, one launch (start us, length us, event | category | flops | bytes accessed | tf_op | source)
XLA Modules:
  0.0 159.2 jit_solution(7525366815041541410)
XLA Ops:
  6.5 0.0 copy-start
  6.5 0.0 all-gather.2.cloned.1.call-start
  6.5 0.6 pad_add_fusion.5.place_ref
  7.1 2.9 %send_parts.1 = (bf16[64,2048]{1,0:T(8,128)(2,1)}, bf16[64,2048]{1,0:T(8,128)(2,1)}, bf16[64,2048]{1,0:T(8,128)(2,1)}, bf16[64,2048]{1,0:T(8,128)(2,1)}) custom-call(s32[4]{0:T(128)} %pad_add_fusion.5.place_ref, bf16[32,8192]{1,0:T(8,128)(2,1)} %tokens_ref.1, bf16[32,256,256]{2,1,0:T(8,128)(2,1)} %bitcast.14, bf16[32,256,256]{2,1,0:T(8,128)(2,1)} %bitcast.15, ...), custom_call_target="tpu_custom_call" | custom-call | bytes 2097152 | tf_op jit(solution)/shard_map/send_parts/pallas_call | solution.py:60
  10.0 3.7 %collective-permute-start.1 = (bf16[64,2048]{1,0:T(8,128)(2,1)}, bf16[64,2048]{1,0:T(8,128)(2,1)S(1)}, u32[]{:S(2)}, u32[]{:S(2)}) collective-permute-start(bf16[64,2048]{1,0:T(8,128)(2,1)} %get-tuple-element.29), channel_id=1, source_target_pairs={{0,16},{8,24},{16,0},{24,8},{1,17},{9,25},{17,1},{25,9},{2,18},{10... | collective-permute-start | bytes 786440 | tf_op jit(solution)/shard_map/ppermute | solution.py:23
  13.8 0.8 collective-permute-start.2
  14.5 0.7 collective-permute-start
  15.2 3.7 %cut_parts.1 = (bf16[4,2,64,2048]{3,2,1,0:T(8,128)(2,1)}, bf16[4,2,64,2048]{3,2,1,0:T(8,128)(2,1)}) custom-call(bf16[2,64,8192]{2,1,0:T(8,128)(2,1)} %refs_0_.1, bf16[2,64,8192]{2,1,0:T(8,128)(2,1)} %refs_1_), custom_call_target="tpu_custom_call" | custom-call | bytes 8388608 | tf_op jit(solution)/shard_map/cut_parts/pallas_call | solution.py:128
  19.0 0.1 collective-permute-done.1.refs_2_
  19.1 6.7 %collective-permute-done.2.refs_3_ = bf16[64,2048]{1,0:T(8,128)(2,1)S(1)} collective-permute-done((bf16[64,2048]{1,0:T(8,128)(2,1)}, bf16[64,2048]{1,0:T(8,128)(2,1)S(1)}, u32[]{:S(2)}, u32[]{:S(2)}) %collective-permute-start.2) | collective-permute-done | bytes 262176 | tf_op jit(solution)/shard_map/ppermute | solution.py:23
  25.8 0.1 collective-permute-done.refs_1_
  25.9 0.0 copy-done.1
  25.9 0.9 arrive_parts.1
  26.8 0.0 all-gather.2.cloned.1.call-update
  26.9 0.0 copy-start.6
  26.9 4.7 %all-to-all-start = ((bf16[4,2,64,2048]{3,2,1,0:T(8,128)(2,1)}), bf16[4,2,64,2048]{3,2,1,0:T(8,128)(2,1)S(1)}, u32[]{:S(2)}, u32[]{:S(2)}) async-start(bf16[4,2,64,2048]{3,2,1,0:T(8,128)(2,1)} %get-tuple-element.26), calls=%async_computation | async-start | bytes 4194304 | tf_op jit(solution)/shard_map/all_to_all | solution.py:15
  31.5 0.0 copy-done.6
  31.5 1.6 %collective-permute-start.7 = (s32[1,32]{1,0:T(1,128)S(1)}, s32[1,32]{1,0:T(1,128)S(1)}, u32[]{:S(2)}, u32[]{:S(2)}) collective-permute-start(s32[1,32]{1,0:T(1,128)S(1)} %bitcast.19), channel_id=1, source_target_pairs={{0,1},{1,0},{2,3},{3,2},{4,5},{5,4},{6,7},{7,6},{8,9},{9,8},{10,11... | collective-permute-start | bytes 392 | tf_op jit(solution)/shard_map/ppermute | solution.py:29
  33.2 0.9 collective-permute-done.7
  34.1 3.1 %collective-permute-start.8 = (s32[2,32]{1,0:T(2,128)S(1)}, s32[2,32]{1,0:T(2,128)S(1)}, u32[]{:S(2)}, u32[]{:S(2)}) collective-permute-start(s32[2,32]{1,0:T(2,128)S(1)} %pad_add_fusion.4), channel_id=1, source_target_pairs={{0,2},{1,3},{2,0},{3,1},{4,6},{5,7},{6,4},{7,5},{8,10},{9,11},{10,... | collective-permute-start | bytes 776 | tf_op jit(solution)/shard_map/ppermute | solution.py:29
  37.2 1.3 collective-permute-done.8
  38.5 6.2 %collective-permute-start.9 = (s32[4,32]{1,0:T(4,128)S(1)}, s32[4,32]{1,0:T(4,128)S(1)}, u32[]{:S(2)}, u32[]{:S(2)}) collective-permute-start(s32[4,32]{1,0:T(4,128)S(1)} %pad_add_fusion.3), channel_id=1, source_target_pairs={{0,4},{1,5},{2,6},{3,7},{4,0},{5,1},{6,2},{7,3},{8,12},{9,13},{10,... | collective-permute-start | bytes 1544 | tf_op jit(solution)/shard_map/ppermute | solution.py:29
  44.7 1.0 collective-permute-done.9
  45.7 1.6 collective-permute-start.10
  47.2 8.6 %collective-permute-done.10 = s32[8,32]{1,0:T(8,128)S(1)} collective-permute-done((s32[8,32]{1,0:T(8,128)S(1)}, s32[8,32]{1,0:T(8,128)S(1)}, u32[]{:S(2)}, u32[]{:S(2)}) %collective-permute-start.10) | collective-permute-done | bytes 1056 | tf_op jit(solution)/shard_map/ppermute | solution.py:29
  55.9 2.5 %collective-permute-start.11 = (s32[16,32]{1,0:T(8,128)S(1)}, s32[16,32]{1,0:T(8,128)S(1)}, u32[]{:S(2)}, u32[]{:S(2)}) collective-permute-start(s32[16,32]{1,0:T(8,128)S(1)} %pad_add_fusion.1), channel_id=1, source_target_pairs={{0,16},{8,24},{16,0},{24,8},{1,17},{9,25},{17,1},{25,9},{2,18},{10... | collective-permute-start | bytes 6152 | tf_op jit(solution)/shard_map/ppermute | solution.py:29
  58.3 2.5 %collective-permute-start.5 = (bf16[256,1024]{1,0:T(8,128)(2,1)S(1)}, bf16[256,1024]{1,0:T(8,128)(2,1)S(1)}, u32[]{:S(2)}, u32[]{:S(2)}) collective-permute-start(bf16[256,1024]{1,0:T(8,128)(2,1)S(1)} %get-tuple-element.32.refs_0_), channel_id=1, source_target_pairs={{0,192},{64,0},{128,64},{192,128},{1,193},{65,1},{129,65},{193,129... | collective-permute-start | bytes 1572872 | tf_op jit(solution)/shard_map/ppermute | solution.py:23
  60.8 0.5 collective-permute-start.4
  61.3 0.6 collective-permute-start.3
  61.9 0.0 collective-permute-done.11
  62.0 0.0 all-to-all-done
  62.0 1.4 copy-done.5
  63.4 3.6 %all-to-all-start.1 = ((bf16[4,2,64,2048]{3,2,1,0:T(8,128)(2,1)}), bf16[4,2,64,2048]{3,2,1,0:T(8,128)(2,1)S(1)}, u32[]{:S(2)}, u32[]{:S(2)}) async-start(bf16[4,2,64,2048]{3,2,1,0:T(8,128)(2,1)} %get-tuple-element.34), calls=%async_computation.1 | async-start | bytes 4194304 | tf_op jit(solution)/shard_map/all_to_all | solution.py:15
  67.0 0.0 copy-start.7
  67.0 0.0 reduce-scatter.2.cloned.1.call-start
  67.1 3.9 %collective-permute-done.5.refs_3_ = bf16[256,1024]{1,0:T(8,128)(2,1)S(1)} collective-permute-done((bf16[256,1024]{1,0:T(8,128)(2,1)S(1)}, bf16[256,1024]{1,0:T(8,128)(2,1)S(1)}, u32[]{:S(2)}, u32[]{:S(2)}) %collective-permute-start.5) | collective-permute-done | bytes 524320 | tf_op jit(solution)/shard_map/ppermute | solution.py:23
  71.0 2.8 %collective-permute-done.4.refs_2_ = bf16[256,1024]{1,0:T(8,128)(2,1)} collective-permute-done((bf16[256,1024]{1,0:T(8,128)(2,1)S(1)}, bf16[256,1024]{1,0:T(8,128)(2,1)}, u32[]{:S(2)}, u32[]{:S(2)}) %collective-permute-start.4) | collective-permute-done | bytes 524320 | tf_op jit(solution)/shard_map/ppermute | solution.py:23
  73.8 13.7 %collective-permute-done.3.refs_1_ = bf16[256,1024]{1,0:T(8,128)(2,1)} collective-permute-done((bf16[256,1024]{1,0:T(8,128)(2,1)S(1)}, bf16[256,1024]{1,0:T(8,128)(2,1)}, u32[]{:S(2)}, u32[]{:S(2)}) %collective-permute-start.3) | collective-permute-done | bytes 524320 | tf_op jit(solution)/shard_map/ppermute | solution.py:23
  87.5 2.7 %order_parts.1.mine_ref = bf16[1024,1024]{1,0:T(8,128)(2,1)} custom-call(s32[4]{0:T(128)S(1)} %copy-done.3, bf16[256,1024]{1,0:T(8,128)(2,1)S(1)} %get-tuple-element.32.refs_0_, bf16[256,1024]{1,0:T(8,128)(2,1)} %collective-permute-done.3.refs_1_, bf16[256,1024]{1,0:T(8,128)(2,1)} %collective-permute-done.4.refs_2_, ...), custom_call_target="tpu_custom_call" | custom-call | bytes 4194304 | tf_op jit(solution)/shard_map/order_parts/pallas_call | solution.py:180
  90.2 0.5 collective-permute-start.6
  90.7 0.6 gather_fusion
  91.4 0.0 all-to-all-done.1
  91.4 2.2 %pick_parts.1 = bf16[8,4,64,256]{3,2,1,0:T(8,128)(2,1)} custom-call(s32[4]{0:T(128)S(1)} %get-tuple-element.54.slot_ref, s32[4]{0:T(128)S(1)} %get-tuple-element.41.wanted_ref, bf16[8,64,2048]{2,1,0:T(8,128)(2,1)S(1)} %bitcast.12), custom_call_target="tpu_custom_call" | custom-call | bytes 2097152 | tf_op jit(solution)/shard_map/pick_parts/pallas_call | solution.py:153
  93.6 0.0 reduce-scatter.2.cloned.1.call-update
  93.6 0.1 broadcast_in_dim.13
  93.7 1.2 collective-permute-done.6.other_ref
  94.8 0.2 broadcast_in_dim.14.ids_ref
  95.0 12.6 %part_products.1 = (bf16[1024,256]{1,0:T(8,128)(2,1)S(1)}, bf16[1024,256]{1,0:T(8,128)(2,1)}, bf16[1024,256]{1,0:T(8,128)(2,1)}, bf16[1024,256]{1,0:T(8,128)(2,1)S(1)}, f32[32,16,128]{2,1,0:T(8,128)}) custom-call(s32[4]{0:T(128)S(1)} %copy-done.3, s32[4]{0:T(128)S(1)} %get-tuple-element.55.wanted_ref, s32[4]{0:T(128)S(1)} %get-tuple-element.54.slot_ref, ...), custom_call_target="tpu_custom_call" | custom-call | flops 5368709120 | bytes 12582912 | tf_op jit(solution)/shard_map/part_products/pallas_call | solution.py:279
  107.6 0.0 copy-start.4
  107.6 0.8 copy-done.4
  108.4 8.9 %all-to-all-start.2 = ((f32[32,16,128]{2,1,0:T(8,128)}), f32[32,16,128]{2,1,0:T(8,128)S(1)}, u32[]{:S(2)}, u32[]{:S(2)}) async-start(f32[32,16,128]{2,1,0:T(8,128)} %get-tuple-element.36), calls=%async_computation.2 | async-start | bytes 524288 | tf_op jit(solution)/shard_map/all_to_all | solution.py:15
  117.3 2.6 %collective-permute-start.12 = (bf16[1024,256]{1,0:T(8,128)(2,1)}, bf16[1024,256]{1,0:T(8,128)(2,1)S(1)}, u32[]{:S(2)}, u32[]{:S(2)}) collective-permute-start(bf16[1024,256]{1,0:T(8,128)(2,1)} %get-tuple-element.38), channel_id=1, source_target_pairs={{0,24},{8,0},{16,8},{24,16},{1,25},{9,1},{17,9},{25,17},{2,26},{10... | collective-permute-start | bytes 1572872 | tf_op jit(solution)/shard_map/ppermute | solution.py:23
  119.8 0.5 collective-permute-start.13
  120.4 0.6 collective-permute-start.14
  121.0 8.4 %all-to-all-done.2.parts_ref = f32[32,16,128]{2,1,0:T(8,128)S(1)} async-done(((f32[32,16,128]{2,1,0:T(8,128)}), f32[32,16,128]{2,1,0:T(8,128)S(1)}, u32[]{:S(2)}, u32[]{:S(2)}) %all-to-all-start.2) | async-done | bytes 262176 | tf_op jit(solution)/shard_map/all_to_all | solution.py:15
  129.4 0.7 lower_parts.1
  130.0 5.8 %all-to-all-start.3 = ((bf16[32,16,128]{2,1,0:T(8,128)(2,1)}), bf16[32,16,128]{2,1,0:T(8,128)(2,1)S(1)}, u32[]{:S(2)}, u32[]{:S(2)}) async-start(bf16[32,16,128]{2,1,0:T(8,128)(2,1)} %lower_parts.1), calls=%async_computation.3 | async-start | bytes 262144 | tf_op jit(solution)/shard_map/all_to_all | solution.py:15
  135.9 0.0 reduce-scatter.2.cloned.1.call-done
  135.9 0.0 collective-permute-done.12.rest_1_
  135.9 0.0 collective-permute-done.13.rest_2_
  135.9 14.0 %collective-permute-done.14.rest_3_ = bf16[1024,256]{1,0:T(8,128)(2,1)S(1)} collective-permute-done((bf16[1024,256]{1,0:T(8,128)(2,1)}, bf16[1024,256]{1,0:T(8,128)(2,1)S(1)}, u32[]{:S(2)}, u32[]{:S(2)}) %collective-permute-start.14) | collective-permute-done | bytes 524320 | tf_op jit(solution)/shard_map/ppermute | solution.py:23
  150.0 0.1 all-to-all-done.3.low_ref
  150.0 0.9 copy-done.2
  150.9 1.4 final_rows.1
  (22 shorter events, 0.1 us)
Async XLA Ops:
  6.5 84.2 %copy-start = (s32[64]{0:T(128)S(1)}, s32[64]{0:T(128)}, u32[]{:S(2)}) copy-start(s32[64]{0:T(128)} %param.11) | copy-start | bytes 772
  6.5 88.3 %all-gather.2.cloned.1.call-start = ((), (), s32[]{:S(2)}) async-start(), calls=%async_computation.5 | async-start | bytes 4718592 | tf_op jit(solution)/shard_map/all_gather | solution.py:378
  10.0 9.1 %collective-permute-start.1 = (bf16[64,2048]{1,0:T(8,128)(2,1)}, bf16[64,2048]{1,0:T(8,128)(2,1)S(1)}, u32[]{:S(2)}, u32[]{:S(2)}) collective-permute-start(bf16[64,2048]{1,0:T(8,128)(2,1)} %get-tuple-element.29), channel_id=1, source_target_pairs={{0,16},{8,24},{16,0},{24,8},{1,17},{9,25},{17,1},{25,9},{2,18},{10... | collective-permute-start | bytes 786440 | tf_op jit(solution)/shard_map/ppermute | solution.py:23
  13.8 12.1 %collective-permute-start.2 = (bf16[64,2048]{1,0:T(8,128)(2,1)}, bf16[64,2048]{1,0:T(8,128)(2,1)S(1)}, u32[]{:S(2)}, u32[]{:S(2)}) collective-permute-start(bf16[64,2048]{1,0:T(8,128)(2,1)} %get-tuple-element.30), channel_id=1, source_target_pairs={{0,24},{8,0},{16,8},{24,16},{1,25},{9,1},{17,9},{25,17},{2,26},{10... | collective-permute-start | bytes 786440 | tf_op jit(solution)/shard_map/ppermute | solution.py:23
  14.5 11.4 %copy-start.1 = (bf16[64,2048]{1,0:T(8,128)(2,1)S(1)}, bf16[64,2048]{1,0:T(8,128)(2,1)}, u32[]{:S(2)}) copy-start(bf16[64,2048]{1,0:T(8,128)(2,1)} %get-tuple-element.28.refs_0_) | copy-start | bytes 786436
  14.5 11.4 %collective-permute-start = (bf16[64,2048]{1,0:T(8,128)(2,1)}, bf16[64,2048]{1,0:T(8,128)(2,1)S(1)}, u32[]{:S(2)}, u32[]{:S(2)}) collective-permute-start(bf16[64,2048]{1,0:T(8,128)(2,1)} %get-tuple-element.24), channel_id=1, source_target_pairs={{0,8},{8,16},{16,24},{24,0},{1,9},{9,17},{17,25},{25,1},{2,10},{10... | collective-permute-start | bytes 786440 | tf_op jit(solution)/shard_map/ppermute | solution.py:23
  26.9 4.7 %copy-start.6 = (s32[32]{0:T(128)S(1)}, s32[32]{0:T(128)}, u32[]{:S(2)}) copy-start(s32[32]{0:T(128)} %param.13) | copy-start | bytes 388
  26.9 35.1 %all-to-all-start = ((bf16[4,2,64,2048]{3,2,1,0:T(8,128)(2,1)}), bf16[4,2,64,2048]{3,2,1,0:T(8,128)(2,1)S(1)}, u32[]{:S(2)}, u32[]{:S(2)}) async-start(bf16[4,2,64,2048]{3,2,1,0:T(8,128)(2,1)} %get-tuple-element.26), calls=%async_computation | async-start | bytes 4194304 | tf_op jit(solution)/shard_map/all_to_all | solution.py:15
  31.5 2.6 %collective-permute-start.7 = (s32[1,32]{1,0:T(1,128)S(1)}, s32[1,32]{1,0:T(1,128)S(1)}, u32[]{:S(2)}, u32[]{:S(2)}) collective-permute-start(s32[1,32]{1,0:T(1,128)S(1)} %bitcast.19), channel_id=1, source_target_pairs={{0,1},{1,0},{2,3},{3,2},{4,5},{5,4},{6,7},{7,6},{8,9},{9,8},{10,11... | collective-permute-start | bytes 392 | tf_op jit(solution)/shard_map/ppermute | solution.py:29
  34.1 4.3 %collective-permute-start.8 = (s32[2,32]{1,0:T(2,128)S(1)}, s32[2,32]{1,0:T(2,128)S(1)}, u32[]{:S(2)}, u32[]{:S(2)}) collective-permute-start(s32[2,32]{1,0:T(2,128)S(1)} %pad_add_fusion.4), channel_id=1, source_target_pairs={{0,2},{1,3},{2,0},{3,1},{4,6},{5,7},{6,4},{7,5},{8,10},{9,11},{10,... | collective-permute-start | bytes 776 | tf_op jit(solution)/shard_map/ppermute | solution.py:29
  38.5 7.2 %collective-permute-start.9 = (s32[4,32]{1,0:T(4,128)S(1)}, s32[4,32]{1,0:T(4,128)S(1)}, u32[]{:S(2)}, u32[]{:S(2)}) collective-permute-start(s32[4,32]{1,0:T(4,128)S(1)} %pad_add_fusion.3), channel_id=1, source_target_pairs={{0,4},{1,5},{2,6},{3,7},{4,0},{5,1},{6,2},{7,3},{8,12},{9,13},{10,... | collective-permute-start | bytes 1544 | tf_op jit(solution)/shard_map/ppermute | solution.py:29
  45.7 10.2 %collective-permute-start.10 = (s32[8,32]{1,0:T(8,128)S(1)}, s32[8,32]{1,0:T(8,128)S(1)}, u32[]{:S(2)}, u32[]{:S(2)}) collective-permute-start(s32[8,32]{1,0:T(8,128)S(1)} %pad_add_fusion.2), channel_id=1, source_target_pairs={{0,8},{8,0},{16,24},{24,16},{1,9},{9,1},{17,25},{25,17},{2,10},{10... | collective-permute-start | bytes 3080 | tf_op jit(solution)/shard_map/ppermute | solution.py:29
  55.9 6.1 %collective-permute-start.11 = (s32[16,32]{1,0:T(8,128)S(1)}, s32[16,32]{1,0:T(8,128)S(1)}, u32[]{:S(2)}, u32[]{:S(2)}) collective-permute-start(s32[16,32]{1,0:T(8,128)S(1)} %pad_add_fusion.1), channel_id=1, source_target_pairs={{0,16},{8,24},{16,0},{24,8},{1,17},{9,25},{17,1},{25,9},{2,18},{10... | collective-permute-start | bytes 6152 | tf_op jit(solution)/shard_map/ppermute | solution.py:29
  58.3 12.7 %collective-permute-start.5 = (bf16[256,1024]{1,0:T(8,128)(2,1)S(1)}, bf16[256,1024]{1,0:T(8,128)(2,1)S(1)}, u32[]{:S(2)}, u32[]{:S(2)}) collective-permute-start(bf16[256,1024]{1,0:T(8,128)(2,1)S(1)} %get-tuple-element.32.refs_0_), channel_id=1, source_target_pairs={{0,192},{64,0},{128,64},{192,128},{1,193},{65,1},{129,65},{193,129... | collective-permute-start | bytes 1572872 | tf_op jit(solution)/shard_map/ppermute | solution.py:23
  60.8 13.0 %collective-permute-start.4 = (bf16[256,1024]{1,0:T(8,128)(2,1)S(1)}, bf16[256,1024]{1,0:T(8,128)(2,1)}, u32[]{:S(2)}, u32[]{:S(2)}) collective-permute-start(bf16[256,1024]{1,0:T(8,128)(2,1)S(1)} %get-tuple-element.32.refs_0_), channel_id=1, source_target_pairs={{0,128},{64,192},{128,0},{192,64},{1,129},{65,193},{129,1},{193,65... | collective-permute-start | bytes 1572872 | tf_op jit(solution)/shard_map/ppermute | solution.py:23
  61.3 26.2 %collective-permute-start.3 = (bf16[256,1024]{1,0:T(8,128)(2,1)S(1)}, bf16[256,1024]{1,0:T(8,128)(2,1)}, u32[]{:S(2)}, u32[]{:S(2)}) collective-permute-start(bf16[256,1024]{1,0:T(8,128)(2,1)S(1)} %get-tuple-element.32.refs_0_), channel_id=1, source_target_pairs={{0,64},{64,128},{128,192},{192,0},{1,65},{65,129},{129,193},{193,1... | collective-permute-start | bytes 1572872 | tf_op jit(solution)/shard_map/ppermute | solution.py:23
  62.0 1.4 copy-start.5
  62.0 25.5 %copy-start.3 = (s32[4]{0:T(128)S(1)}, s32[4]{0:T(128)}, u32[]{:S(2)}) copy-start(s32[4]{0:T(128)} %pad_add_fusion.5.place_ref) | copy-start | bytes 52
  63.4 28.0 %all-to-all-start.1 = ((bf16[4,2,64,2048]{3,2,1,0:T(8,128)(2,1)}), bf16[4,2,64,2048]{3,2,1,0:T(8,128)(2,1)S(1)}, u32[]{:S(2)}, u32[]{:S(2)}) async-start(bf16[4,2,64,2048]{3,2,1,0:T(8,128)(2,1)} %get-tuple-element.34), calls=%async_computation.1 | async-start | bytes 4194304 | tf_op jit(solution)/shard_map/all_to_all | solution.py:15
  67.0 23.7 %copy-start.7 = (s32[4]{0:T(128)S(1)}, s32[4]{0:T(128)}, u32[]{:S(2)}) copy-start(s32[4]{0:T(128)} %param.12) | copy-start | bytes 52
  67.0 68.9 %reduce-scatter.2.cloned.1.call-start = ((), (), s32[]{:S(2)}) async-start(), calls=%async_computation.6 | async-start | bytes 1179648 | tf_op jit(solution)/shard_map/reduce_scatter | solution.py:396
  90.2 4.6 %collective-permute-start.6 = (bf16[1024,1024]{1,0:T(8,128)(2,1)}, bf16[1024,1024]{1,0:T(8,128)(2,1)}, u32[]{:S(2)}, u32[]{:S(2)}) collective-permute-start(bf16[1024,1024]{1,0:T(8,128)(2,1)} %order_parts.1.mine_ref), channel_id=1, source_target_pairs={{0,32},{32,0},{1,33},{33,1},{2,34},{34,2},{3,35},{35,3},{4,36},{36... | collective-permute-start | bytes 6291464 | tf_op jit(solution)/shard_map/ppermute | solution.py:23
  107.6 0.8 copy-start.4
  108.4 21.0 %all-to-all-start.2 = ((f32[32,16,128]{2,1,0:T(8,128)}), f32[32,16,128]{2,1,0:T(8,128)S(1)}, u32[]{:S(2)}, u32[]{:S(2)}) async-start(f32[32,16,128]{2,1,0:T(8,128)} %get-tuple-element.36), calls=%async_computation.2 | async-start | bytes 524288 | tf_op jit(solution)/shard_map/all_to_all | solution.py:15
  117.3 18.6 %collective-permute-start.12 = (bf16[1024,256]{1,0:T(8,128)(2,1)}, bf16[1024,256]{1,0:T(8,128)(2,1)S(1)}, u32[]{:S(2)}, u32[]{:S(2)}) collective-permute-start(bf16[1024,256]{1,0:T(8,128)(2,1)} %get-tuple-element.38), channel_id=1, source_target_pairs={{0,24},{8,0},{16,8},{24,16},{1,25},{9,1},{17,9},{25,17},{2,26},{10... | collective-permute-start | bytes 1572872 | tf_op jit(solution)/shard_map/ppermute | solution.py:23
  119.8 16.1 %collective-permute-start.13 = (bf16[1024,256]{1,0:T(8,128)(2,1)}, bf16[1024,256]{1,0:T(8,128)(2,1)S(1)}, u32[]{:S(2)}, u32[]{:S(2)}) collective-permute-start(bf16[1024,256]{1,0:T(8,128)(2,1)} %get-tuple-element.39), channel_id=1, source_target_pairs={{0,16},{8,24},{16,0},{24,8},{1,17},{9,25},{17,1},{25,9},{2,18},{10... | collective-permute-start | bytes 1572872 | tf_op jit(solution)/shard_map/ppermute | solution.py:23
  120.4 29.6 %collective-permute-start.14 = (bf16[1024,256]{1,0:T(8,128)(2,1)}, bf16[1024,256]{1,0:T(8,128)(2,1)S(1)}, u32[]{:S(2)}, u32[]{:S(2)}) collective-permute-start(bf16[1024,256]{1,0:T(8,128)(2,1)} %copy-done.4), channel_id=1, source_target_pairs={{0,8},{8,16},{16,24},{24,0},{1,9},{9,17},{17,25},{25,1},{2,10},{10... | collective-permute-start | bytes 1572872 | tf_op jit(solution)/shard_map/ppermute | solution.py:23
  130.0 20.0 %all-to-all-start.3 = ((bf16[32,16,128]{2,1,0:T(8,128)(2,1)}), bf16[32,16,128]{2,1,0:T(8,128)(2,1)S(1)}, u32[]{:S(2)}, u32[]{:S(2)}) async-start(bf16[32,16,128]{2,1,0:T(8,128)(2,1)} %lower_parts.1), calls=%async_computation.3 | async-start | bytes 262144 | tf_op jit(solution)/shard_map/all_to_all | solution.py:15
  150.0 0.9 copy-start.2
Sparse Core Ops, SparseCore 0:
  27.0 58.1 all-gather.1
  93.7 38.2 reduce-scatter.1

commit v4 on v1

v4 whole, which is shorter than its diff:
```python
import functools

import jax
import jax.numpy as jnp
from jax import lax
from jax.experimental import pallas as pl
from jax.experimental.pallas import tpu as pltpu
from jax.sharding import Mesh, PartitionSpec as P

adapter_scale = 2.0
mebibyte = 1024 * 1024


def swap(value, axis):
    return lax.all_to_all(value, axis, split_axis=0, concat_axis=0, tiled=True)


def after(value, *earlier):
    return lax.optimization_barrier((value,) + earlier)[0]


def shift(value, axis, size, by):
    return lax.ppermute(value, axis, [(i, (i + by) % size) for i in range(size)])


def send_kernel(place_ref, tokens_ref, *outs):
    part = outs[0].shape[1]
    for d, out_ref in enumerate(outs):
        first = (place_ref[2] + d) % len(outs) * part
        out_ref[...] = tokens_ref[:, pl.ds(pl.multiple_of(first, part), part)]


def send_parts(place, tokens, count):
    rows, width = tokens.shape
    near = pl.BlockSpec(memory_space=pltpu.VMEM)
    return pl.pallas_call(
        send_kernel,
        out_shape=[jax.ShapeDtypeStruct((rows, width // count), tokens.dtype)] * count,
        in_specs=[pl.BlockSpec(memory_space=pltpu.SMEM), near],
        out_specs=[near] * count,
        compiler_params=pltpu.CompilerParams(vmem_limit_bytes=8 * mebibyte),
        cost_estimate=pl.CostEstimate(flops=0, bytes_accessed=mebibyte, transcendentals=0),
        name="send_parts",
    )(place, tokens)


def cut_kernel(*refs):
    count = len(refs) // 2 - 1
    pools, out, held, arrived, left = refs[:count], refs[count], refs[count + 1 : -2], refs[-2], refs[-1]
    slots = pools[0].shape[0]
    part = out.shape[3]

    def pool_of(j):
        return pltpu.make_async_copy(pools[j], held[j], arrived.at[j])

    def piece_of(j, k):
        source = held[j].at[:, :, pl.ds(k * part, part)]
        return pltpu.make_async_copy(source, out.at[k, pl.ds(j * slots, slots)], left.at[j, k])

    for j in range(count):
        pool_of(j).start()
    for j in range(count):
        pool_of(j).wait()
        for k in range(out.shape[0]):
            piece_of(j, k).start()
    for j in range(count):
        for k in range(out.shape[0]):
            piece_of(j, k).wait()


def cut_parts(pools, count):
    held, rank, width = pools[0].shape
    where = pl.BlockSpec(memory_space=pl.ANY)
    return pl.pallas_call(
        cut_kernel,
        out_shape=jax.ShapeDtypeStruct((count, len(pools) * held, rank, width // count), pools[0].dtype),
        in_specs=[where] * len(pools),
        out_specs=where,
        scratch_shapes=[pltpu.VMEM(p.shape, p.dtype) for p in pools]
        + [pltpu.SemaphoreType.DMA((len(pools),)), pltpu.SemaphoreType.DMA((len(pools), count))],
        compiler_params=pltpu.CompilerParams(vmem_limit_bytes=60 * mebibyte),
        cost_estimate=pl.CostEstimate(flops=0, bytes_accessed=8 * mebibyte, transcendentals=0),
        name="cut_parts",
    )(*pools)


def order_kernel(place_ref, *refs):
    out_ref = refs[-1]
    count = len(refs) - 1
    sub = refs[0].shape[0]
    for e in range(count):
        first = (place_ref[0] + count - e) % count * sub
        out_ref[pl.ds(pl.multiple_of(first, sub), sub)] = refs[e][...]


def order_parts(place, pieces):
    sub, wide = pieces[0].shape
    near = pl.BlockSpec(memory_space=pltpu.VMEM)
    return pl.pallas_call(
        order_kernel,
        out_shape=jax.ShapeDtypeStruct((len(pieces) * sub, wide), pieces[0].dtype),
        in_specs=[pl.BlockSpec(memory_space=pltpu.SMEM)] + [near] * len(pieces),
        out_specs=near,
        compiler_params=pltpu.CompilerParams(vmem_limit_bytes=8 * mebibyte),
        cost_estimate=pl.CostEstimate(flops=0, bytes_accessed=4 * mebibyte, transcendentals=0),
        name="order_parts",
    )(place, *pieces)


def local_kernel(
    place_ref, wanted_ref, slot_ref, rows_ref, pool_ref, out_ref, ups_ref, down_ref, up_ref, downed, upped
):
    nz, ny, rows, part = rows_ref.shape
    rank = pool_ref.shape[1]
    count = slot_ref.shape[0] // 2
    width = ups_ref.shape[3]
    steps = 2
    share = nz // steps

    def up_of(s):
        return pltpu.make_async_copy(pool_ref.at[slot_ref[s]], up_ref.at[s], upped.at[s])

    def down_of(s):
        lines = pl.ds(s * rank, rank)
        return pltpu.make_async_copy(pool_ref.at[slot_ref[count + s]], down_ref.at[lines], downed.at[s])

    for s in range(count):
        down_of(s).start()
    for s in range(count):
        up_of(s).start()
    for s in range(count):
        down_of(s).wait()

    lane = lax.broadcasted_iota(jnp.int32, (rows, count * rank), 1) // rank
    wanted = lane < 0
    for s in range(count):
        wanted = wanted | ((lane == s) & (wanted_ref[s] != 0))
    for i in range(steps):
        product = lax.dot_general(
            rows_ref[i * share : (i + 1) * share].reshape(share * ny * rows, part),
            down_ref[...],
            (((1,), (1,)), ((), ())),
            preferred_element_type=jnp.float32,
        )
        for j in range(share):
            for k in range(ny):
                first = (j * ny + k) * rows
                piece = jnp.where(wanted, product[first : first + rows], 0.0)
                out_ref[(place_ref[2] + ny - k) % ny * nz + i * share + j] = piece.astype(out_ref.dtype)
    for s in range(count):
        up_of(s).wait()
        for k in range(nz):
            piece = up_ref[s, :, k * width : (k + 1) * width]
            ups_ref[k, s] = jnp.where(wanted_ref[s] != 0, piece, jnp.zeros_like(piece))


def local_parts(place, wanted, slots, gathered, pools, width_out):
    nz, ny, rows, part = gathered.shape
    _, rank, _ = pools.shape
    count = wanted.shape[0]
    kind = gathered.dtype
    scalars = pl.BlockSpec(memory_space=pltpu.SMEM)
    where = pl.BlockSpec(memory_space=pl.ANY)
    near = pl.BlockSpec(memory_space=pltpu.VMEM)
    return pl.pallas_call(
        local_kernel,
        out_shape=[
            jax.ShapeDtypeStruct((ny * nz, rows, count * rank), kind),
            jax.ShapeDtypeStruct((nz, count, rank, width_out), kind),
        ],
        in_specs=[scalars, scalars, scalars, near, where],
        out_specs=[near, near],
        scratch_shapes=[
            pltpu.VMEM((count * rank, part), kind),
            pltpu.VMEM((count, rank, part), kind),
            pltpu.SemaphoreType.DMA((count,)),
            pltpu.SemaphoreType.DMA((count,)),
        ],
        compiler_params=pltpu.CompilerParams(vmem_limit_bytes=14 * mebibyte),
        cost_estimate=pl.CostEstimate(
            flops=2 * ny * nz * rows * part * count * rank, bytes_accessed=8 * mebibyte, transcendentals=0
        ),
        name="local_parts",
    )(place, wanted, slots, gathered, pools)


def base_kernel(place_ref, rows_ref, mine_ref, other_ref, *outs):
    nz, ny, rows, part = rows_ref.shape
    half = mine_ref.shape[0]
    width = outs[0].shape[1]
    steps = 2
    tall = nz // steps * ny * rows
    for step in range(steps):
        here = pl.ds(step * (nz // steps), nz // steps)
        total = None
        for ref, core in ((mine_ref, place_ref[1]), (other_ref, 1 - place_ref[1])):
            lines = rows_ref[here, :, :, pl.ds(pl.multiple_of(core * half, half), half)].reshape(tall, half)
            product = jnp.dot(lines, ref[...], preferred_element_type=jnp.float32)
            total = product if total is None else total + product
        for d, out_ref in enumerate(outs):
            out_ref[step * tall : (step + 1) * tall] = total[:, d * width : (d + 1) * width].astype(out_ref.dtype)


def base_parts(place, gathered, mine, other, width_out):
    nz, ny, rows, part = gathered.shape
    near = pl.BlockSpec(memory_space=pltpu.VMEM)
    return pl.pallas_call(
        base_kernel,
        out_shape=[jax.ShapeDtypeStruct((ny * nz * rows, width_out), gathered.dtype)] * ny,
        in_specs=[pl.BlockSpec(memory_space=pltpu.SMEM), near, near, near],
        out_specs=[near] * ny,
        compiler_params=pltpu.CompilerParams(vmem_limit_bytes=14 * mebibyte),
        cost_estimate=pl.CostEstimate(
            flops=2 * ny * nz * rows * part * ny * width_out, bytes_accessed=10 * mebibyte, transcendentals=0
        ),
        name="base_parts",
    )(place, gathered, mine, other)


def lower_kernel(count, parts_ref, ids_ref, out_ref):
    total = jnp.sum(parts_ref[...].astype(jnp.float32), axis=0)
    rank = total.shape[1] // count
    ids = ids_ref[:, :rank]
    low = jnp.zeros((total.shape[0], rank), jnp.float32)
    for s in range(count):
        low += jnp.where(ids == s, total[:, s * rank : (s + 1) * rank], 0.0)
    low = jnp.concatenate([low, ids.astype(jnp.float32)], axis=1).astype(out_ref.dtype)
    for k in range(out_ref.shape[0]):
        out_ref[k] = low


def lower_parts(parts, ids, count):
    pieces, rows, wide = parts.shape
    near = pl.BlockSpec(memory_space=pltpu.VMEM)
    return pl.pallas_call(
        functools.partial(lower_kernel, count),
        out_shape=jax.ShapeDtypeStruct((pieces, rows, 2 * wide // count), parts.dtype),
        in_specs=[near, near],
        out_specs=near,
        compiler_params=pltpu.CompilerParams(vmem_limit_bytes=8 * mebibyte),
        cost_estimate=pl.CostEstimate(flops=0, bytes_accessed=mebibyte, transcendentals=0),
        name="lower_parts",
    )(parts, ids)


def final_kernel(place_ref, low_ref, up_ref, *rest):
    base, out_ref = rest[:-1], rest[-1]
    ny = len(base)
    nz, _, rows, width = base[0].shape
    count, rank, _ = up_ref.shape
    block = nz * rows
    low = low_ref[...].reshape(ny * block, 2 * rank).astype(jnp.float32)
    low, ids = low[:, :rank], low[:, rank:]
    low = jnp.concatenate([low, low], axis=1)
    ids = jnp.concatenate([ids, ids], axis=1)
    lane = lax.broadcasted_iota(jnp.int32, low.shape, 1)
    kept = [
        jnp.where(ids == jnp.where(lane < rank, float(s), float(s + 1)), low, 0.0).astype(jnp.bfloat16)
        for s in range(0, count, 2)
    ]
    up = up_ref[...].reshape(count * rank, width)
    update = jnp.dot(jnp.concatenate(kept, axis=1), up, preferred_element_type=jnp.float32)
    for owner in range(ny):
        total = adapter_scale * update[owner * block : (owner + 1) * block]
        for d, ref in enumerate(base):
            back = (place_ref[2] + d + ny - owner) % ny
            total += ref[:, pl.ds(back, 1)].reshape(block, width).astype(jnp.float32)
        out_ref[owner * block : (owner + 1) * block] = total.astype(out_ref.dtype)


def final_rows(place, low, ups, base, ny, nz):
    tall, width_out = base[0].shape
    count, rank, _ = ups.shape
    near = pl.BlockSpec(memory_space=pltpu.VMEM)
    return pl.pallas_call(
        final_kernel,
        out_shape=jax.ShapeDtypeStruct((tall, width_out), jnp.bfloat16),
        in_specs=[pl.BlockSpec(memory_space=pltpu.SMEM)] + [near] * (2 + len(base)),
        out_specs=near,
        compiler_params=pltpu.CompilerParams(vmem_limit_bytes=16 * mebibyte),
        cost_estimate=pl.CostEstimate(
            flops=2 * tall * count * rank * width_out, bytes_accessed=4 * mebibyte, transcendentals=0
        ),
        name="final_rows",
    )(place, low, ups, *[part.reshape(nz, ny, tall // (ny * nz), width_out) for part in base])


def per_device(nx, nc, ny, nz, tokens, base_weight, down_pool, up_pool, slot_of, requested, row_adapter):
    rows, width = tokens.shape
    width_out = base_weight.shape[1]
    held, rank, _ = down_pool.shape
    count_new = requested.shape[0]
    part = width // ny
    sub = part // (nx * nc)
    nt = ny * nz
    x, core, y, z = [lax.axis_index(a).astype(jnp.int32) for a in ("x", "core", "y", "z")]
    place = jnp.stack([x, core, y, z])

    sent = send_parts(place, tokens, ny)
    pools = cut_parts([up_pool, after(down_pool, sent[1])], ny)
    arrived = [after(sent[0], pools)] + [shift(sent[d], "y", ny, d) for d in range(1, ny)]
    far = jnp.concatenate(arrived)
    gathered = lax.all_gather(far, "z", axis=0, tiled=True).reshape(nz, ny, rows, part)

    weights = base_weight.reshape(ny * nc * nx, sub, width_out)
    piece = [
        lax.dynamic_index_in_dim(weights, (y + d) % ny * (nc * nx) + core * nx + x, 0, keepdims=False)
        for d in range(ny)
    ]
    piece = [shift(after(block, sent[1]), "y", ny, d) if d else block for d, block in enumerate(piece)]

    pools = swap(after(pools, far, *piece), "y").reshape(ny * 2 * held, rank, part)
    piece = jnp.concatenate(piece, axis=1)

    pool_rows = slot_of[requested]
    home, local = pool_rows // held, pool_rows % held
    home_y, home_z = home // nz, home % nz
    slots = home_y * (2 * held) + local

    piece = order_parts(place, [shift(piece, "x", nx, e) if e else piece for e in range(nx)])
    other = shift(piece, "core", nc, 1)

    wanted = (home_z == z).astype(jnp.int32)
    slots = jnp.concatenate([slots, slots + held])
    chosen, ups = local_parts(place, wanted, slots, gathered, pools, width_out)
    ups = lax.psum_scatter(ups, "z", scatter_dimension=0, tiled=True)[0]
    base = base_parts(after(place, chosen), gathered, piece, other, width_out)
    base = [shift(part, "y", ny, ny - d) if d else part for d, part in enumerate(base)]
    ids = jnp.broadcast_to(row_adapter[:, None], (rows, 2 * rank))
    lowered = swap(lower_parts(swap(chosen, ("y", "z")), ids, count_new), ("y", "z"))
    return final_rows(place, lowered, ups, base, ny, nz)


def solution(mesh):
    nx, nc, ny, nz = 4, 2, 4, 8
    fine = Mesh(mesh.devices.reshape(nx, nc, ny, nz), ("x", "core", "y", "z"))
    group, tensor = ("x", "core"), ("y", "z")
    both = group + tensor
    placed = (
        P(both, None),
        P(None, tensor),
        P(both, None, None),
        P(both, None, None),
        P(group),
        P(group),
        P(both),
    )

    def step(*args):
        return per_device(nx, nc, ny, nz, *args)

    return jax.shard_map(step, mesh=fine, in_specs=placed, out_specs=P(group, tensor), check_vma=False)
```

time: 246 us -> 150 us (0.61); the launches traced: 243 us -> 149 us
  blocking collectives: 27.5 us -> 0 us
  local copies, waits for them, and re-layouts: 35.4 us -> 9 us
  waiting for transfers between devices: 82 us -> 61.4 us
  Pallas kernels: 0 us -> 19.5 us
  matrix products: 19.2 us -> 0 us
  between operations: 26.9 us -> 13.6 us
  other arithmetic: 10.7 us -> 0.91 us
  starting transfers between devices: 40.9 us -> 44.8 us
    all_to_all x9 -> x3, waiting for transfers between devices: 82 us -> 15.9 us  [swap(): return lax.all_to_all(value, axis, split_axis=0, concat_axis=0, tiled=True)]
    ppermute x0 -> x13, waiting for transfers between devices: none -> 45.5 us  [shift(): lax.ppermute(value, axis, [(i, (i + by) % size) for i in range(size)])]
    all_to_all x2 -> x0, blocking collectives: 27.5 us -> none  [swap(): return lax.all_to_all(value, axis, split_axis=0, concat_axis=0, tiled=True)]
    ppermute x0 -> x13, starting transfers between devices: none -> 20.9 us  [shift(): lax.ppermute(value, axis, [(i, (i + by) % size) for i in range(size)])]
    pallas_call x0 -> x7, Pallas kernels: none -> 19.5 us  [the longest x1 7.15 us: base_parts(): pl.pallas_call(base_kernel, out_shape=[jax.ShapeDtypeStruct((ny * nz * ro...]
    dot_general x6 -> x0, matrix products: 19.2 us -> none  [the longest x4 13.6 us: per_device(): jnp.dot(gathered, weight[:, k * width_out:(k + 1) * width_out], preferred...]
    all_to_all x9 -> x3, starting transfers between devices: 40.9 us -> 23.8 us  [swap(): return lax.all_to_all(value, axis, split_axis=0, concat_axis=0, tiled=True)]
    reshape x4 -> x0, local copies, waits for them, and re-layouts: 10.3 us -> none  [the longest x1 3.34 us: per_device(): down_pool.reshape(held, rank, ny, part).transpose(2, 0, 1, 3)]
  transfers between devices with their start and end apart: 10 -> 18, of which waited for: 8 -> 10; matrix products, arithmetic and copies ran while one was open for 24% -> 1% of each run, Pallas kernels for 0% -> 11%
where the time goes in v4:
time: 150 us; the launch traced here: 149 us
  waiting for transfers between devices  61.4 us (41%)
  starting transfers between devices  44.8 us (30%)
  Pallas kernels  19.5 us (13%)
  between operations  13.6 us (9%)
  local copies, waits for them, and re-layouts  9 us (6%)
    ppermute x13, waiting for transfers between devices, shift(): lax.ppermute(value, axis, [(i, (i + by) % size) for i in range(size)])  45.5 us
    all_to_all x3, starting transfers between devices, swap(): return lax.all_to_all(value, axis, split_axis=0, concat_axis=0, tiled=True)  23.8 us
    ppermute x13, starting transfers between devices, shift(): lax.ppermute(value, axis, [(i, (i + by) % size) for i in range(size)])  20.9 us
    all_to_all x3, waiting for transfers between devices, swap(): return lax.all_to_all(value, axis, split_axis=0, concat_axis=0, tiled=True)  15.9 us
    pallas_call x1, Pallas kernels, base_parts(): pl.pallas_call(base_kernel, out_shape=[jax.ShapeDtypeStruct((ny * nz * ro...  7.15 us
    unnamed x17, local copies, waits for them, and re-layouts  7.14 us
    pallas_call x1, Pallas kernels, local_parts(): pl.pallas_call(local_kernel, out_shape=[jax.ShapeDtypeStruct((ny * nz, ro...  4.63 us
    pallas_call x1, Pallas kernels, cut_parts(): pl.pallas_call(cut_kernel, out_shape=jax.ShapeDtypeStruct((count, len(poo...  3.69 us
  transfers between devices with their start and end apart: 18, of which 10 were waited for; matrix products, arithmetic and copies ran while one was open for 1% of the time, Pallas kernels for 11%

profile of v4, /device:TPU:1, one launch (start us, length us, event | category | flops | bytes accessed | tf_op | source)
XLA Modules:
  0.0 149.3 jit_solution(14480332029202275882)
XLA Ops:
  6.5 0.0 copy-start
  6.5 0.0 all-gather.2.cloned.1.call-start
  6.5 0.7 compare_select_fusion
  7.3 0.0 copy-start.3
  7.3 1.0 copy-done.3
  8.3 0.6 send_parts.1
  8.9 2.2 %collective-permute-start = (bf16[32,2048]{1,0:T(8,128)(2,1)S(1)}, bf16[32,2048]{1,0:T(8,128)(2,1)S(1)}, u32[]{:S(2)}, u32[]{:S(2)}) collective-permute-start(bf16[32,2048]{1,0:T(8,128)(2,1)S(1)} %get-tuple-element.23), channel_id=1, source_target_pairs={{0,8},{8,16},{16,24},{24,0},{1,9},{9,17},{17,25},{25,1},{2,10},{10... | collective-permute-start | bytes 393224 | tf_op jit(solution)/shard_map/ppermute | solution.py:23
  11.1 2.6 %collective-permute-start.1 = (bf16[32,2048]{1,0:T(8,128)(2,1)S(1)}, bf16[32,2048]{1,0:T(8,128)(2,1)S(1)}, u32[]{:S(2)}, u32[]{:S(2)}) collective-permute-start(bf16[32,2048]{1,0:T(8,128)(2,1)S(1)} %get-tuple-element.26), channel_id=1, source_target_pairs={{0,16},{8,24},{16,0},{24,8},{1,17},{9,25},{17,1},{25,9},{2,18},{10... | collective-permute-start | bytes 393224 | tf_op jit(solution)/shard_map/ppermute | solution.py:23
  13.7 1.1 collective-permute-start.2
  14.8 3.7 %cut_parts.1 = bf16[4,4,64,2048]{3,2,1,0:T(8,128)(2,1)} custom-call(bf16[2,64,8192]{2,1,0:T(8,128)(2,1)} %refs_0_.1, bf16[2,64,8192]{2,1,0:T(8,128)(2,1)} %refs_1_), custom_call_target="tpu_custom_call" | custom-call | bytes 8388608 | tf_op jit(solution)/shard_map/cut_parts/pallas_call | solution.py:74
  18.5 0.0 collective-permute-done
  18.6 0.9 collective-permute-done.1
  19.5 0.0 collective-permute-done.2
  19.5 0.0 copy-start.5
  19.5 0.8 copy-done.5
  20.3 0.0 all-gather.2.cloned.1.call-update
  20.4 1.1 dynamic-slice_bitcast_fusion
  21.5 0.1 collective-permute-start.3
  21.6 2.1 %collective-permute-start.4 = (bf16[256,256]{1,0:T(8,128)(2,1)S(1)}, bf16[256,256]{1,0:T(8,128)(2,1)S(1)}, u32[]{:S(2)}, u32[]{:S(2)}) collective-permute-start(bf16[256,256]{1,0:T(8,128)(2,1)S(1)} %get-tuple-element.29), channel_id=1, source_target_pairs={{0,16},{8,24},{16,0},{24,8},{1,17},{9,25},{17,1},{25,9},{2,18},{10... | collective-permute-start | bytes 393224 | tf_op jit(solution)/shard_map/ppermute | solution.py:23
  23.7 1.7 %collective-permute-start.5 = (bf16[256,256]{1,0:T(8,128)(2,1)S(1)}, bf16[256,256]{1,0:T(8,128)(2,1)S(1)}, u32[]{:S(2)}, u32[]{:S(2)}) collective-permute-start(bf16[256,256]{1,0:T(8,128)(2,1)S(1)} %get-tuple-element.30), channel_id=1, source_target_pairs={{0,24},{8,0},{16,8},{24,16},{1,25},{9,1},{17,9},{25,17},{2,26},{10... | collective-permute-start | bytes 393224 | tf_op jit(solution)/shard_map/ppermute | solution.py:23
  25.4 3.4 %collective-permute-done.3 = bf16[256,256]{1,0:T(8,128)(2,1)S(1)} collective-permute-done((bf16[256,256]{1,0:T(8,128)(2,1)S(1)}, bf16[256,256]{1,0:T(8,128)(2,1)S(1)}, u32[]{:S(2)}, u32[]{:S(2)}) %collective-permute-start.3) | collective-permute-done | bytes 131104 | tf_op jit(solution)/shard_map/ppermute | solution.py:23
  28.7 0.0 collective-permute-done.4
  28.7 0.4 collective-permute-done.5
  29.1 4.9 %all-to-all-start = ((bf16[4,4,64,2048]{3,2,1,0:T(8,128)(2,1)}), bf16[4,4,64,2048]{3,2,1,0:T(8,128)(2,1)}, u32[]{:S(2)}, u32[]{:S(2)}) async-start(bf16[4,4,64,2048]{3,2,1,0:T(8,128)(2,1)} %cut_parts.1), calls=%async_computation | async-start | bytes 8388608 | tf_op jit(solution)/shard_map/all_to_all | solution.py:15
  34.0 0.0 reduce-scatter.2.cloned.1.call-start
  34.1 0.1 pad_maximum_fusion.refs_0_
  34.1 1.9 %collective-permute-start.6 = (bf16[256,1024]{1,0:T(8,128)(2,1)S(1)}, bf16[256,1024]{1,0:T(8,128)(2,1)S(1)}, u32[]{:S(2)}, u32[]{:S(2)}) collective-permute-start(bf16[256,1024]{1,0:T(8,128)(2,1)S(1)} %pad_maximum_fusion.refs_0_), channel_id=1, source_target_pairs={{0,64},{64,128},{128,192},{192,0},{1,65},{65,129},{129,193},{193,1... | collective-permute-start | bytes 1572872 | tf_op jit(solution)/shard_map/ppermute | solution.py:23
  36.0 2.5 %collective-permute-start.7 = (bf16[256,1024]{1,0:T(8,128)(2,1)S(1)}, bf16[256,1024]{1,0:T(8,128)(2,1)S(1)}, u32[]{:S(2)}, u32[]{:S(2)}) collective-permute-start(bf16[256,1024]{1,0:T(8,128)(2,1)S(1)} %pad_maximum_fusion.refs_0_), channel_id=1, source_target_pairs={{0,128},{64,192},{128,0},{192,64},{1,129},{65,193},{129,1},{193,65... | collective-permute-start | bytes 1572872 | tf_op jit(solution)/shard_map/ppermute | solution.py:23
  38.5 1.2 collective-permute-start.8
  39.6 7.1 %collective-permute-done.6.refs_1_ = bf16[256,1024]{1,0:T(8,128)(2,1)S(1)} collective-permute-done((bf16[256,1024]{1,0:T(8,128)(2,1)S(1)}, bf16[256,1024]{1,0:T(8,128)(2,1)S(1)}, u32[]{:S(2)}, u32[]{:S(2)}) %collective-permute-start.6) | collective-permute-done | bytes 524320 | tf_op jit(solution)/shard_map/ppermute | solution.py:23
  46.7 12.4 %collective-permute-done.7.refs_2_ = bf16[256,1024]{1,0:T(8,128)(2,1)S(1)} collective-permute-done((bf16[256,1024]{1,0:T(8,128)(2,1)S(1)}, bf16[256,1024]{1,0:T(8,128)(2,1)S(1)}, u32[]{:S(2)}, u32[]{:S(2)}) %collective-permute-start.7) | collective-permute-done | bytes 524320 | tf_op jit(solution)/shard_map/ppermute | solution.py:23
  59.1 1.4 collective-permute-done.8.refs_3_
  60.6 0.7 order_parts.1.mine_ref
  61.2 2.1 %collective-permute-start.9 = (bf16[1024,1024]{1,0:T(8,128)(2,1)S(1)}, bf16[1024,1024]{1,0:T(8,128)(2,1)}, u32[]{:S(2)}, u32[]{:S(2)}) collective-permute-start(bf16[1024,1024]{1,0:T(8,128)(2,1)S(1)} %order_parts.1.mine_ref), channel_id=1, source_target_pairs={{0,32},{32,0},{1,33},{33,1},{2,34},{34,2},{3,35},{35,3},{4,36},{36... | collective-permute-start | bytes 6291464 | tf_op jit(solution)/shard_map/ppermute | solution.py:23
  63.4 0.0 copy-done
  63.4 0.6 gather_fusion
  64.0 0.1 pad_add_fusion.1.slot_ref
  64.1 15.7 %all-to-all-done = bf16[4,4,64,2048]{3,2,1,0:T(8,128)(2,1)} async-done(((bf16[4,4,64,2048]{3,2,1,0:T(8,128)(2,1)}), bf16[4,4,64,2048]{3,2,1,0:T(8,128)(2,1)}, u32[]{:S(2)}, u32[]{:S(2)}) %all-to-all-start) | async-done | bytes 4194336 | tf_op jit(solution)/shard_map/all_to_all | solution.py:15
  79.8 0.0 all-gather.2.cloned.1.call-done
  79.8 0.0 copy-start.1
  79.8 2.2 %copy-done.1 = bf16[1024,2048]{1,0:T(8,128)(2,1)S(1)} copy-done((bf16[1024,2048]{1,0:T(8,128)(2,1)S(1)}, bf16[1024,2048]{1,0:T(8,128)(2,1)}, u32[]{:S(2)}) %copy-start.1) | copy-done | bytes 4194328
  82.0 4.6 %local_parts.1 = (bf16[32,32,256]{2,1,0:T(8,128)(2,1)}, bf16[8,4,64,256]{3,2,1,0:T(8,128)(2,1)}) custom-call(s32[4]{0:T(128)S(1)} %get-tuple-element.34.place_ref, s32[4]{0:T(128)S(1)} %compare_convert_fusion.wanted_ref, s32[8]{0:T(128)S(1)} %pad_add_fusion.1.slot_ref, bf16[8,4,32,2048]{3,2,1,0:T(8,128)(2,1)S(1)} %bitcast.20, ...), custom_call_target="tpu_custom_call" | custom-call | flops 1073741824 | bytes 8388608 | tf_op jit(solution)/shard_map/local_parts/pallas_call | solution.py:165
  86.7 0.0 reduce-scatter.2.cloned.1.call-update
  86.7 10.3 %all-to-all-start.1 = ((bf16[32,32,256]{2,1,0:T(8,128)(2,1)}), bf16[32,32,256]{2,1,0:T(8,128)(2,1)S(1)}, u32[]{:S(2)}, u32[]{:S(2)}) async-start(bf16[32,32,256]{2,1,0:T(8,128)(2,1)} %get-tuple-element.32), calls=%async_computation.1 | async-start | bytes 1048576 | tf_op jit(solution)/shard_map/all_to_all | solution.py:15
  97.0 0.0 collective-permute-done.9.other_ref
  97.0 0.0 copy-start.2
  97.1 2.2 %copy-done.2 = bf16[1024,2048]{1,0:T(8,128)(2,1)S(1)} copy-done((bf16[1024,2048]{1,0:T(8,128)(2,1)S(1)}, bf16[1024,2048]{1,0:T(8,128)(2,1)}, u32[]{:S(2)}) %copy-start.2) | copy-done | bytes 4194328
  99.2 0.0 copy-start.6
  99.2 7.2 %base_parts.1 = (bf16[1024,256]{1,0:T(8,128)(2,1)S(1)}, bf16[1024,256]{1,0:T(8,128)(2,1)}, bf16[1024,256]{1,0:T(8,128)(2,1)}, bf16[1024,256]{1,0:T(8,128)(2,1)}) custom-call(s32[4]{0:T(128)S(1)} %get-tuple-element.34.place_ref, bf16[8,4,32,2048]{3,2,1,0:T(8,128)(2,1)S(1)} %bitcast.21, bf16[1024,1024]{1,0:T(8,128)(2,1)S(1)} %order_parts.1.mine_ref, ...), custom_call_target="tpu_custom_call" | custom-call | flops 4294967296 | bytes 10485760 | tf_op jit(solution)/shard_map/base_parts/pallas_call | solution.py:207
  106.4 2.5 %collective-permute-start.10 = (bf16[1024,256]{1,0:T(8,128)(2,1)}, bf16[1024,256]{1,0:T(8,128)(2,1)S(1)}, u32[]{:S(2)}, u32[]{:S(2)}) collective-permute-start(bf16[1024,256]{1,0:T(8,128)(2,1)} %get-tuple-element.36), channel_id=1, source_target_pairs={{0,24},{8,0},{16,8},{24,16},{1,25},{9,1},{17,9},{25,17},{2,26},{10... | collective-permute-start | bytes 1572872 | tf_op jit(solution)/shard_map/ppermute | solution.py:23
  108.9 0.5 collective-permute-start.11
  109.4 0.6 collective-permute-start.12
  110.0 0.0 all-to-all-done.1.parts_ref
  110.0 0.0 copy-done.6
  110.0 0.1 broadcast_in_dim.10.ids_ref
  110.1 0.9 lower_parts.1
  111.0 8.6 %all-to-all-start.2 = ((bf16[32,32,128]{2,1,0:T(8,128)(2,1)}), bf16[32,32,128]{2,1,0:T(8,128)(2,1)S(1)}, u32[]{:S(2)}, u32[]{:S(2)}) async-start(bf16[32,32,128]{2,1,0:T(8,128)(2,1)} %lower_parts.1), calls=%async_computation.2 | async-start | bytes 524288 | tf_op jit(solution)/shard_map/all_to_all | solution.py:15
  119.5 0.0 collective-permute-done.10
  119.5 2.5 %collective-permute-done.11 = bf16[1024,256]{1,0:T(8,128)(2,1)S(1)} collective-permute-done((bf16[1024,256]{1,0:T(8,128)(2,1)}, bf16[1024,256]{1,0:T(8,128)(2,1)S(1)}, u32[]{:S(2)}, u32[]{:S(2)}) %collective-permute-start.11) | collective-permute-done | bytes 524320 | tf_op jit(solution)/shard_map/ppermute | solution.py:23
  122.0 17.4 %collective-permute-done.12 = bf16[1024,256]{1,0:T(8,128)(2,1)S(1)} collective-permute-done((bf16[1024,256]{1,0:T(8,128)(2,1)}, bf16[1024,256]{1,0:T(8,128)(2,1)S(1)}, u32[]{:S(2)}, u32[]{:S(2)}) %collective-permute-start.12) | collective-permute-done | bytes 524320 | tf_op jit(solution)/shard_map/ppermute | solution.py:23
  139.5 0.2 all-to-all-done.2.low_ref
  139.7 0.0 reduce-scatter.2.cloned.1.call-done
  139.7 0.9 copy-done.4
  140.6 1.9 %final_rows.1 = bf16[1024,256]{1,0:T(8,128)(2,1)} custom-call(s32[4]{0:T(128)S(1)} %get-tuple-element.34.place_ref, bf16[32,32,128]{2,1,0:T(8,128)(2,1)S(1)} %all-to-all-done.2.low_ref, bf16[4,64,256]{2,1,0:T(8,128)(2,1)S(1)} %bitcast.26, bf16[8,4,32,256]{3,2,1,0:T(8,128)(2,1)S(1)} %bitcast.22, bf16[8,4,32,256]{3,2,1,0:T(8,128)(2,1)S(1)} %bitcast.23, ...), custom_call_target="tpu_custom_call" | custom-call | flops 134217728 | bytes 4194304 | tf_op jit(solution)/shard_map/final_rows/pallas_call | solution.py:275
  (8 shorter events, 0.1 us)
Async XLA Ops:
  6.5 56.8 %copy-start = (s32[64]{0:T(128)S(1)}, s32[64]{0:T(128)}, u32[]{:S(2)}) copy-start(s32[64]{0:T(128)} %param.11) | copy-start | bytes 772
  6.5 73.3 %all-gather.2.cloned.1.call-start = ((), (), s32[]{:S(2)}) async-start(), calls=%async_computation.4 | async-start | bytes 4718592 | tf_op jit(solution)/shard_map/all_gather | solution.py:303
  7.3 1.0 copy-start.3
  8.9 9.6 %collective-permute-start = (bf16[32,2048]{1,0:T(8,128)(2,1)S(1)}, bf16[32,2048]{1,0:T(8,128)(2,1)S(1)}, u32[]{:S(2)}, u32[]{:S(2)}) collective-permute-start(bf16[32,2048]{1,0:T(8,128)(2,1)S(1)} %get-tuple-element.23), channel_id=1, source_target_pairs={{0,8},{8,16},{16,24},{24,0},{1,9},{9,17},{17,25},{25,1},{2,10},{10... | collective-permute-start | bytes 393224 | tf_op jit(solution)/shard_map/ppermute | solution.py:23
  11.1 8.3 %collective-permute-start.1 = (bf16[32,2048]{1,0:T(8,128)(2,1)S(1)}, bf16[32,2048]{1,0:T(8,128)(2,1)S(1)}, u32[]{:S(2)}, u32[]{:S(2)}) collective-permute-start(bf16[32,2048]{1,0:T(8,128)(2,1)S(1)} %get-tuple-element.26), channel_id=1, source_target_pairs={{0,16},{8,24},{16,0},{24,8},{1,17},{9,25},{17,1},{25,9},{2,18},{10... | collective-permute-start | bytes 393224 | tf_op jit(solution)/shard_map/ppermute | solution.py:23
  13.7 5.7 %collective-permute-start.2 = (bf16[32,2048]{1,0:T(8,128)(2,1)S(1)}, bf16[32,2048]{1,0:T(8,128)(2,1)S(1)}, u32[]{:S(2)}, u32[]{:S(2)}) collective-permute-start(bf16[32,2048]{1,0:T(8,128)(2,1)S(1)} %get-tuple-element.27), channel_id=1, source_target_pairs={{0,24},{8,0},{16,8},{24,16},{1,25},{9,1},{17,9},{25,17},{2,26},{10... | collective-permute-start | bytes 393224 | tf_op jit(solution)/shard_map/ppermute | solution.py:23
  19.5 0.8 copy-start.5
  21.5 7.2 %collective-permute-start.3 = (bf16[256,256]{1,0:T(8,128)(2,1)S(1)}, bf16[256,256]{1,0:T(8,128)(2,1)S(1)}, u32[]{:S(2)}, u32[]{:S(2)}) collective-permute-start(bf16[256,256]{1,0:T(8,128)(2,1)S(1)} %get-tuple-element.28), channel_id=1, source_target_pairs={{0,8},{8,16},{16,24},{24,0},{1,9},{9,17},{17,25},{25,1},{2,10},{10... | collective-permute-start | bytes 393224 | tf_op jit(solution)/shard_map/ppermute | solution.py:23
  21.6 7.1 %collective-permute-start.4 = (bf16[256,256]{1,0:T(8,128)(2,1)S(1)}, bf16[256,256]{1,0:T(8,128)(2,1)S(1)}, u32[]{:S(2)}, u32[]{:S(2)}) collective-permute-start(bf16[256,256]{1,0:T(8,128)(2,1)S(1)} %get-tuple-element.29), channel_id=1, source_target_pairs={{0,16},{8,24},{16,0},{24,8},{1,17},{9,25},{17,1},{25,9},{2,18},{10... | collective-permute-start | bytes 393224 | tf_op jit(solution)/shard_map/ppermute | solution.py:23
  23.7 5.4 %collective-permute-start.5 = (bf16[256,256]{1,0:T(8,128)(2,1)S(1)}, bf16[256,256]{1,0:T(8,128)(2,1)S(1)}, u32[]{:S(2)}, u32[]{:S(2)}) collective-permute-start(bf16[256,256]{1,0:T(8,128)(2,1)S(1)} %get-tuple-element.30), channel_id=1, source_target_pairs={{0,24},{8,0},{16,8},{24,16},{1,25},{9,1},{17,9},{25,17},{2,26},{10... | collective-permute-start | bytes 393224 | tf_op jit(solution)/shard_map/ppermute | solution.py:23
  29.1 50.7 %all-to-all-start = ((bf16[4,4,64,2048]{3,2,1,0:T(8,128)(2,1)}), bf16[4,4,64,2048]{3,2,1,0:T(8,128)(2,1)}, u32[]{:S(2)}, u32[]{:S(2)}) async-start(bf16[4,4,64,2048]{3,2,1,0:T(8,128)(2,1)} %cut_parts.1), calls=%async_computation | async-start | bytes 8388608 | tf_op jit(solution)/shard_map/all_to_all | solution.py:15
  34.0 105.7 %reduce-scatter.2.cloned.1.call-start = ((), (), s32[]{:S(2)}) async-start(), calls=%async_computation.5 | async-start | bytes 1179648 | tf_op jit(solution)/shard_map/reduce_scatter | solution.py:326
  34.1 12.6 %collective-permute-start.6 = (bf16[256,1024]{1,0:T(8,128)(2,1)S(1)}, bf16[256,1024]{1,0:T(8,128)(2,1)S(1)}, u32[]{:S(2)}, u32[]{:S(2)}) collective-permute-start(bf16[256,1024]{1,0:T(8,128)(2,1)S(1)} %pad_maximum_fusion.refs_0_), channel_id=1, source_target_pairs={{0,64},{64,128},{128,192},{192,0},{1,65},{65,129},{129,193},{193,1... | collective-permute-start | bytes 1572872 | tf_op jit(solution)/shard_map/ppermute | solution.py:23
  36.0 23.1 %collective-permute-start.7 = (bf16[256,1024]{1,0:T(8,128)(2,1)S(1)}, bf16[256,1024]{1,0:T(8,128)(2,1)S(1)}, u32[]{:S(2)}, u32[]{:S(2)}) collective-permute-start(bf16[256,1024]{1,0:T(8,128)(2,1)S(1)} %pad_maximum_fusion.refs_0_), channel_id=1, source_target_pairs={{0,128},{64,192},{128,0},{192,64},{1,129},{65,193},{129,1},{193,65... | collective-permute-start | bytes 1572872 | tf_op jit(solution)/shard_map/ppermute | solution.py:23
  38.5 22.1 %collective-permute-start.8 = (bf16[256,1024]{1,0:T(8,128)(2,1)S(1)}, bf16[256,1024]{1,0:T(8,128)(2,1)S(1)}, u32[]{:S(2)}, u32[]{:S(2)}) collective-permute-start(bf16[256,1024]{1,0:T(8,128)(2,1)S(1)} %pad_maximum_fusion.refs_0_), channel_id=1, source_target_pairs={{0,192},{64,0},{128,64},{192,128},{1,193},{65,1},{129,65},{193,129... | collective-permute-start | bytes 1572872 | tf_op jit(solution)/shard_map/ppermute | solution.py:23
  61.2 35.8 %collective-permute-start.9 = (bf16[1024,1024]{1,0:T(8,128)(2,1)S(1)}, bf16[1024,1024]{1,0:T(8,128)(2,1)}, u32[]{:S(2)}, u32[]{:S(2)}) collective-permute-start(bf16[1024,1024]{1,0:T(8,128)(2,1)S(1)} %order_parts.1.mine_ref), channel_id=1, source_target_pairs={{0,32},{32,0},{1,33},{33,1},{2,34},{34,2},{3,35},{35,3},{4,36},{36... | collective-permute-start | bytes 6291464 | tf_op jit(solution)/shard_map/ppermute | solution.py:23
  79.8 2.2 %copy-start.1 = (bf16[1024,2048]{1,0:T(8,128)(2,1)S(1)}, bf16[1024,2048]{1,0:T(8,128)(2,1)}, u32[]{:S(2)}) copy-start(bf16[1024,2048]{1,0:T(8,128)(2,1)} %all-gather.2.cloned.1.call-done) | copy-start | bytes 12582916
  86.7 23.3 %all-to-all-start.1 = ((bf16[32,32,256]{2,1,0:T(8,128)(2,1)}), bf16[32,32,256]{2,1,0:T(8,128)(2,1)S(1)}, u32[]{:S(2)}, u32[]{:S(2)}) async-start(bf16[32,32,256]{2,1,0:T(8,128)(2,1)} %get-tuple-element.32), calls=%async_computation.1 | async-start | bytes 1048576 | tf_op jit(solution)/shard_map/all_to_all | solution.py:15
  97.0 2.2 %copy-start.2 = (bf16[1024,2048]{1,0:T(8,128)(2,1)S(1)}, bf16[1024,2048]{1,0:T(8,128)(2,1)}, u32[]{:S(2)}) copy-start(bf16[1024,2048]{1,0:T(8,128)(2,1)} %all-gather.2.cloned.1.call-done) | copy-start | bytes 12582916
  99.2 10.8 %copy-start.6 = (s32[32]{0:T(128)S(1)}, s32[32]{0:T(128)}, u32[]{:S(2)}) copy-start(s32[32]{0:T(128)} %param.13) | copy-start | bytes 388
  106.4 13.1 %collective-permute-start.10 = (bf16[1024,256]{1,0:T(8,128)(2,1)}, bf16[1024,256]{1,0:T(8,128)(2,1)S(1)}, u32[]{:S(2)}, u32[]{:S(2)}) collective-permute-start(bf16[1024,256]{1,0:T(8,128)(2,1)} %get-tuple-element.36), channel_id=1, source_target_pairs={{0,24},{8,0},{16,8},{24,16},{1,25},{9,1},{17,9},{25,17},{2,26},{10... | collective-permute-start | bytes 1572872 | tf_op jit(solution)/shard_map/ppermute | solution.py:23
  108.9 13.2 %collective-permute-start.11 = (bf16[1024,256]{1,0:T(8,128)(2,1)}, bf16[1024,256]{1,0:T(8,128)(2,1)S(1)}, u32[]{:S(2)}, u32[]{:S(2)}) collective-permute-start(bf16[1024,256]{1,0:T(8,128)(2,1)} %get-tuple-element.37), channel_id=1, source_target_pairs={{0,16},{8,24},{16,0},{24,8},{1,17},{9,25},{17,1},{25,9},{2,18},{10... | collective-permute-start | bytes 1572872 | tf_op jit(solution)/shard_map/ppermute | solution.py:23
  109.4 30.1 %collective-permute-start.12 = (bf16[1024,256]{1,0:T(8,128)(2,1)}, bf16[1024,256]{1,0:T(8,128)(2,1)S(1)}, u32[]{:S(2)}, u32[]{:S(2)}) collective-permute-start(bf16[1024,256]{1,0:T(8,128)(2,1)} %get-tuple-element.38), channel_id=1, source_target_pairs={{0,8},{8,16},{16,24},{24,0},{1,9},{9,17},{17,25},{25,1},{2,10},{10... | collective-permute-start | bytes 1572872 | tf_op jit(solution)/shard_map/ppermute | solution.py:23
  111.0 28.7 %all-to-all-start.2 = ((bf16[32,32,128]{2,1,0:T(8,128)(2,1)}), bf16[32,32,128]{2,1,0:T(8,128)(2,1)S(1)}, u32[]{:S(2)}, u32[]{:S(2)}) async-start(bf16[32,32,128]{2,1,0:T(8,128)(2,1)} %lower_parts.1), calls=%async_computation.2 | async-start | bytes 524288 | tf_op jit(solution)/shard_map/all_to_all | solution.py:15
  139.7 0.9 copy-start.4
Sparse Core Ops, SparseCore 0:
  20.4 58.0 all-gather.1
  86.8 42.7 reduce-scatter.1

commit v5 on v4

--- a/solution.py
+++ b/solution.py
@@ -244,7 +244,10 @@
 
 
 def final_kernel(place_ref, low_ref, up_ref, *rest):
-    base, out_ref = rest[:-1], rest[-1]
+    base, (out_ref, own_ref, arrived) = rest[:-3], rest[-3:]
+    copy = pltpu.make_async_copy(base[0], own_ref, arrived)
+    copy.start()
+    base = (own_ref,) + base[1:]
     ny = len(base)
     nz, _, rows, width = base[0].shape
     count, rank, _ = up_ref.shape
@@ -260,6 +263,7 @@
     ]
     up = up_ref[...].reshape(count * rank, width)
     update = jnp.dot(jnp.concatenate(kept, axis=1), up, preferred_element_type=jnp.float32)
+    copy.wait()
     for owner in range(ny):
         total = adapter_scale * update[owner * block : (owner + 1) * block]
         for d, ref in enumerate(base):
@@ -275,8 +279,14 @@
     return pl.pallas_call(
         final_kernel,
         out_shape=jax.ShapeDtypeStruct((tall, width_out), jnp.bfloat16),
-        in_specs=[pl.BlockSpec(memory_space=pltpu.SMEM)] + [near] * (2 + len(base)),
+        in_specs=[pl.BlockSpec(memory_space=pltpu.SMEM)] + [near] * 2
+        + [pl.BlockSpec(memory_space=pl.ANY)]
+        + [near] * (len(base) - 1),
         out_specs=near,
+        scratch_shapes=[
+            pltpu.VMEM((nz, ny, tall // (ny * nz), width_out), base[0].dtype),
+            pltpu.SemaphoreType.DMA,
+        ],
         compiler_params=pltpu.CompilerParams(vmem_limit_bytes=16 * mebibyte),
         cost_estimate=pl.CostEstimate(
             flops=2 * tall * count * rank * width_out, bytes_accessed=4 * mebibyte, transcendentals=0

time: 150 us -> 150 us (level)
  no operation moved by 1% of the time
where the time goes in v5:
time: 150 us
  waiting for transfers between devices  61.4 us (41%)
  starting transfers between devices  44.8 us (30%)
  Pallas kernels  19.7 us (13%)
  between operations  13.7 us (9%)
  local copies, waits for them, and re-layouts  9 us (6%)
    ppermute x13, waiting for transfers between devices, shift(): lax.ppermute(value, axis, [(i, (i + by) % size) for i in range(size)])  45.5 us
    all_to_all x3, starting transfers between devices, swap(): return lax.all_to_all(value, axis, split_axis=0, concat_axis=0, tiled=True)  23.8 us
    ppermute x13, starting transfers between devices, shift(): lax.ppermute(value, axis, [(i, (i + by) % size) for i in range(size)])  20.9 us
    all_to_all x3, waiting for transfers between devices, swap(): return lax.all_to_all(value, axis, split_axis=0, concat_axis=0, tiled=True)  15.9 us
    pallas_call x1, Pallas kernels, base_parts(): pl.pallas_call(base_kernel, out_shape=[jax.ShapeDtypeStruct((ny * nz * ro...  7.15 us
    unnamed x17, local copies, waits for them, and re-layouts  7.14 us
    pallas_call x1, Pallas kernels, local_parts(): pl.pallas_call(local_kernel, out_shape=[jax.ShapeDtypeStruct((ny * nz, ro...  4.63 us
    pallas_call x1, Pallas kernels, cut_parts(): pl.pallas_call(cut_kernel, out_shape=jax.ShapeDtypeStruct((count, len(poo...  3.69 us
  transfers between devices with their start and end apart: 18, of which 10 were waited for; matrix products, arithmetic and copies ran while one was open for 1% of the time, Pallas kernels for 11%

profile of v5, /device:TPU:1, one launch (start us, length us, event | category | flops | bytes accessed | tf_op | source)
XLA Modules:
  0.0 149.5 jit_solution(11181762307608951708)
XLA Ops:
  6.5 0.0 copy-start
  6.5 0.0 all-gather.2.cloned.1.call-start
  6.5 0.7 compare_select_fusion
  7.3 0.0 copy-start.3
  7.3 1.0 copy-done.3
  8.3 0.6 send_parts.1
  8.9 2.2 %collective-permute-start = (bf16[32,2048]{1,0:T(8,128)(2,1)S(1)}, bf16[32,2048]{1,0:T(8,128)(2,1)S(1)}, u32[]{:S(2)}, u32[]{:S(2)}) collective-permute-start(bf16[32,2048]{1,0:T(8,128)(2,1)S(1)} %get-tuple-element.23), channel_id=1, source_target_pairs={{0,8},{8,16},{16,24},{24,0},{1,9},{9,17},{17,25},{25,1},{2,10},{10... | collective-permute-start | bytes 393224 | tf_op jit(solution)/shard_map/ppermute | solution.py:23
  11.1 2.6 %collective-permute-start.1 = (bf16[32,2048]{1,0:T(8,128)(2,1)S(1)}, bf16[32,2048]{1,0:T(8,128)(2,1)S(1)}, u32[]{:S(2)}, u32[]{:S(2)}) collective-permute-start(bf16[32,2048]{1,0:T(8,128)(2,1)S(1)} %get-tuple-element.26), channel_id=1, source_target_pairs={{0,16},{8,24},{16,0},{24,8},{1,17},{9,25},{17,1},{25,9},{2,18},{10... | collective-permute-start | bytes 393224 | tf_op jit(solution)/shard_map/ppermute | solution.py:23
  13.7 1.1 collective-permute-start.2
  14.8 3.7 %cut_parts.1 = bf16[4,4,64,2048]{3,2,1,0:T(8,128)(2,1)} custom-call(bf16[2,64,8192]{2,1,0:T(8,128)(2,1)} %refs_0_.1, bf16[2,64,8192]{2,1,0:T(8,128)(2,1)} %refs_1_), custom_call_target="tpu_custom_call" | custom-call | bytes 8388608 | tf_op jit(solution)/shard_map/cut_parts/pallas_call | solution.py:74
  18.5 0.0 collective-permute-done
  18.6 0.9 collective-permute-done.1
  19.5 0.0 collective-permute-done.2
  19.5 0.0 copy-start.5
  19.5 0.8 copy-done.5
  20.3 0.0 all-gather.2.cloned.1.call-update
  20.4 1.1 dynamic-slice_bitcast_fusion
  21.5 0.1 collective-permute-start.3
  21.6 2.1 %collective-permute-start.4 = (bf16[256,256]{1,0:T(8,128)(2,1)S(1)}, bf16[256,256]{1,0:T(8,128)(2,1)S(1)}, u32[]{:S(2)}, u32[]{:S(2)}) collective-permute-start(bf16[256,256]{1,0:T(8,128)(2,1)S(1)} %get-tuple-element.29), channel_id=1, source_target_pairs={{0,16},{8,24},{16,0},{24,8},{1,17},{9,25},{17,1},{25,9},{2,18},{10... | collective-permute-start | bytes 393224 | tf_op jit(solution)/shard_map/ppermute | solution.py:23
  23.7 1.7 %collective-permute-start.5 = (bf16[256,256]{1,0:T(8,128)(2,1)S(1)}, bf16[256,256]{1,0:T(8,128)(2,1)S(1)}, u32[]{:S(2)}, u32[]{:S(2)}) collective-permute-start(bf16[256,256]{1,0:T(8,128)(2,1)S(1)} %get-tuple-element.30), channel_id=1, source_target_pairs={{0,24},{8,0},{16,8},{24,16},{1,25},{9,1},{17,9},{25,17},{2,26},{10... | collective-permute-start | bytes 393224 | tf_op jit(solution)/shard_map/ppermute | solution.py:23
  25.4 3.4 %collective-permute-done.3 = bf16[256,256]{1,0:T(8,128)(2,1)S(1)} collective-permute-done((bf16[256,256]{1,0:T(8,128)(2,1)S(1)}, bf16[256,256]{1,0:T(8,128)(2,1)S(1)}, u32[]{:S(2)}, u32[]{:S(2)}) %collective-permute-start.3) | collective-permute-done | bytes 131104 | tf_op jit(solution)/shard_map/ppermute | solution.py:23
  28.7 0.0 collective-permute-done.4
  28.7 0.4 collective-permute-done.5
  29.1 4.9 %all-to-all-start = ((bf16[4,4,64,2048]{3,2,1,0:T(8,128)(2,1)}), bf16[4,4,64,2048]{3,2,1,0:T(8,128)(2,1)}, u32[]{:S(2)}, u32[]{:S(2)}) async-start(bf16[4,4,64,2048]{3,2,1,0:T(8,128)(2,1)} %cut_parts.1), calls=%async_computation | async-start | bytes 8388608 | tf_op jit(solution)/shard_map/all_to_all | solution.py:15
  34.0 0.0 reduce-scatter.2.cloned.1.call-start
  34.1 0.1 pad_maximum_fusion.refs_0_
  34.1 1.9 %collective-permute-start.6 = (bf16[256,1024]{1,0:T(8,128)(2,1)S(1)}, bf16[256,1024]{1,0:T(8,128)(2,1)S(1)}, u32[]{:S(2)}, u32[]{:S(2)}) collective-permute-start(bf16[256,1024]{1,0:T(8,128)(2,1)S(1)} %pad_maximum_fusion.refs_0_), channel_id=1, source_target_pairs={{0,64},{64,128},{128,192},{192,0},{1,65},{65,129},{129,193},{193,1... | collective-permute-start | bytes 1572872 | tf_op jit(solution)/shard_map/ppermute | solution.py:23
  36.0 2.5 %collective-permute-start.7 = (bf16[256,1024]{1,0:T(8,128)(2,1)S(1)}, bf16[256,1024]{1,0:T(8,128)(2,1)S(1)}, u32[]{:S(2)}, u32[]{:S(2)}) collective-permute-start(bf16[256,1024]{1,0:T(8,128)(2,1)S(1)} %pad_maximum_fusion.refs_0_), channel_id=1, source_target_pairs={{0,128},{64,192},{128,0},{192,64},{1,129},{65,193},{129,1},{193,65... | collective-permute-start | bytes 1572872 | tf_op jit(solution)/shard_map/ppermute | solution.py:23
  38.5 1.2 collective-permute-start.8
  39.6 7.1 %collective-permute-done.6.refs_1_ = bf16[256,1024]{1,0:T(8,128)(2,1)S(1)} collective-permute-done((bf16[256,1024]{1,0:T(8,128)(2,1)S(1)}, bf16[256,1024]{1,0:T(8,128)(2,1)S(1)}, u32[]{:S(2)}, u32[]{:S(2)}) %collective-permute-start.6) | collective-permute-done | bytes 524320 | tf_op jit(solution)/shard_map/ppermute | solution.py:23
  46.7 12.4 %collective-permute-done.7.refs_2_ = bf16[256,1024]{1,0:T(8,128)(2,1)S(1)} collective-permute-done((bf16[256,1024]{1,0:T(8,128)(2,1)S(1)}, bf16[256,1024]{1,0:T(8,128)(2,1)S(1)}, u32[]{:S(2)}, u32[]{:S(2)}) %collective-permute-start.7) | collective-permute-done | bytes 524320 | tf_op jit(solution)/shard_map/ppermute | solution.py:23
  59.1 1.4 collective-permute-done.8.refs_3_
  60.6 0.7 order_parts.1.mine_ref
  61.2 2.1 %collective-permute-start.9 = (bf16[1024,1024]{1,0:T(8,128)(2,1)S(1)}, bf16[1024,1024]{1,0:T(8,128)(2,1)}, u32[]{:S(2)}, u32[]{:S(2)}) collective-permute-start(bf16[1024,1024]{1,0:T(8,128)(2,1)S(1)} %order_parts.1.mine_ref), channel_id=1, source_target_pairs={{0,32},{32,0},{1,33},{33,1},{2,34},{34,2},{3,35},{35,3},{4,36},{36... | collective-permute-start | bytes 6291464 | tf_op jit(solution)/shard_map/ppermute | solution.py:23
  63.4 0.0 copy-done
  63.4 0.6 gather_fusion
  64.0 0.1 pad_add_fusion.1.slot_ref
  64.1 15.7 %all-to-all-done = bf16[4,4,64,2048]{3,2,1,0:T(8,128)(2,1)} async-done(((bf16[4,4,64,2048]{3,2,1,0:T(8,128)(2,1)}), bf16[4,4,64,2048]{3,2,1,0:T(8,128)(2,1)}, u32[]{:S(2)}, u32[]{:S(2)}) %all-to-all-start) | async-done | bytes 4194336 | tf_op jit(solution)/shard_map/all_to_all | solution.py:15
  79.8 0.0 all-gather.2.cloned.1.call-done
  79.8 0.0 copy-start.1
  79.8 2.2 %copy-done.1 = bf16[1024,2048]{1,0:T(8,128)(2,1)S(1)} copy-done((bf16[1024,2048]{1,0:T(8,128)(2,1)S(1)}, bf16[1024,2048]{1,0:T(8,128)(2,1)}, u32[]{:S(2)}) %copy-start.1) | copy-done | bytes 4194328
  82.0 4.6 %local_parts.1 = (bf16[32,32,256]{2,1,0:T(8,128)(2,1)}, bf16[8,4,64,256]{3,2,1,0:T(8,128)(2,1)}) custom-call(s32[4]{0:T(128)S(1)} %get-tuple-element.34.place_ref, s32[4]{0:T(128)S(1)} %compare_convert_fusion.wanted_ref, s32[8]{0:T(128)S(1)} %pad_add_fusion.1.slot_ref, bf16[8,4,32,2048]{3,2,1,0:T(8,128)(2,1)S(1)} %bitcast.20, ...), custom_call_target="tpu_custom_call" | custom-call | flops 1073741824 | bytes 8388608 | tf_op jit(solution)/shard_map/local_parts/pallas_call | solution.py:165
  86.7 0.0 reduce-scatter.2.cloned.1.call-update
  86.7 10.3 %all-to-all-start.1 = ((bf16[32,32,256]{2,1,0:T(8,128)(2,1)}), bf16[32,32,256]{2,1,0:T(8,128)(2,1)S(1)}, u32[]{:S(2)}, u32[]{:S(2)}) async-start(bf16[32,32,256]{2,1,0:T(8,128)(2,1)} %get-tuple-element.32), calls=%async_computation.1 | async-start | bytes 1048576 | tf_op jit(solution)/shard_map/all_to_all | solution.py:15
  97.0 0.0 collective-permute-done.9.other_ref
  97.0 0.0 copy-start.2
  97.1 2.2 %copy-done.2 = bf16[1024,2048]{1,0:T(8,128)(2,1)S(1)} copy-done((bf16[1024,2048]{1,0:T(8,128)(2,1)S(1)}, bf16[1024,2048]{1,0:T(8,128)(2,1)}, u32[]{:S(2)}) %copy-start.2) | copy-done | bytes 4194328
  99.2 0.0 copy-start.6
  99.2 7.2 %base_parts.1 = (bf16[1024,256]{1,0:T(8,128)(2,1)S(1)}, bf16[1024,256]{1,0:T(8,128)(2,1)}, bf16[1024,256]{1,0:T(8,128)(2,1)}, bf16[1024,256]{1,0:T(8,128)(2,1)}) custom-call(s32[4]{0:T(128)S(1)} %get-tuple-element.34.place_ref, bf16[8,4,32,2048]{3,2,1,0:T(8,128)(2,1)S(1)} %bitcast.21, bf16[1024,1024]{1,0:T(8,128)(2,1)S(1)} %order_parts.1.mine_ref, ...), custom_call_target="tpu_custom_call" | custom-call | flops 4294967296 | bytes 10485760 | tf_op jit(solution)/shard_map/base_parts/pallas_call | solution.py:207
  106.4 2.5 %collective-permute-start.10 = (bf16[1024,256]{1,0:T(8,128)(2,1)}, bf16[1024,256]{1,0:T(8,128)(2,1)S(1)}, u32[]{:S(2)}, u32[]{:S(2)}) collective-permute-start(bf16[1024,256]{1,0:T(8,128)(2,1)} %get-tuple-element.36), channel_id=1, source_target_pairs={{0,24},{8,0},{16,8},{24,16},{1,25},{9,1},{17,9},{25,17},{2,26},{10... | collective-permute-start | bytes 1572872 | tf_op jit(solution)/shard_map/ppermute | solution.py:23
  108.9 0.5 collective-permute-start.11
  109.4 0.6 collective-permute-start.12
  110.0 0.0 all-to-all-done.1.parts_ref
  110.0 0.0 copy-done.6
  110.0 0.1 broadcast_in_dim.10.ids_ref
  110.1 0.9 lower_parts.1
  111.0 8.6 %all-to-all-start.2 = ((bf16[32,32,128]{2,1,0:T(8,128)(2,1)}), bf16[32,32,128]{2,1,0:T(8,128)(2,1)S(1)}, u32[]{:S(2)}, u32[]{:S(2)}) async-start(bf16[32,32,128]{2,1,0:T(8,128)(2,1)} %lower_parts.1), calls=%async_computation.2 | async-start | bytes 524288 | tf_op jit(solution)/shard_map/all_to_all | solution.py:15
  119.5 0.0 collective-permute-done.10
  119.5 2.6 %collective-permute-done.11 = bf16[1024,256]{1,0:T(8,128)(2,1)S(1)} collective-permute-done((bf16[1024,256]{1,0:T(8,128)(2,1)}, bf16[1024,256]{1,0:T(8,128)(2,1)S(1)}, u32[]{:S(2)}, u32[]{:S(2)}) %collective-permute-start.11) | collective-permute-done | bytes 524320 | tf_op jit(solution)/shard_map/ppermute | solution.py:23
  122.1 17.3 %collective-permute-done.12 = bf16[1024,256]{1,0:T(8,128)(2,1)S(1)} collective-permute-done((bf16[1024,256]{1,0:T(8,128)(2,1)}, bf16[1024,256]{1,0:T(8,128)(2,1)S(1)}, u32[]{:S(2)}, u32[]{:S(2)}) %collective-permute-start.12) | collective-permute-done | bytes 524320 | tf_op jit(solution)/shard_map/ppermute | solution.py:23
  139.5 0.2 all-to-all-done.2.low_ref
  139.7 0.0 reduce-scatter.2.cloned.1.call-done
  139.7 0.9 copy-done.4
  140.6 2.1 %final_rows.1 = bf16[1024,256]{1,0:T(8,128)(2,1)} custom-call(s32[4]{0:T(128)S(1)} %get-tuple-element.34.place_ref, bf16[32,32,128]{2,1,0:T(8,128)(2,1)S(1)} %all-to-all-done.2.low_ref, bf16[4,64,256]{2,1,0:T(8,128)(2,1)S(1)} %bitcast.26, bf16[8,4,32,256]{3,2,1,0:T(8,128)(2,1)S(1)} %bitcast.22, bf16[8,4,32,256]{3,2,1,0:T(8,128)(2,1)S(1)} %bitcast.23, ...), custom_call_target="tpu_custom_call" | custom-call | flops 134217728 | bytes 4194304 | tf_op jit(solution)/shard_map/final_rows/pallas_call | solution.py:279
  (8 shorter events, 0.1 us)
Async XLA Ops:
  6.5 56.8 %copy-start = (s32[64]{0:T(128)S(1)}, s32[64]{0:T(128)}, u32[]{:S(2)}) copy-start(s32[64]{0:T(128)} %param.11) | copy-start | bytes 772
  6.5 73.3 %all-gather.2.cloned.1.call-start = ((), (), s32[]{:S(2)}) async-start(), calls=%async_computation.4 | async-start | bytes 4718592 | tf_op jit(solution)/shard_map/all_gather | solution.py:313
  7.3 1.0 copy-start.3
  8.9 9.6 %collective-permute-start = (bf16[32,2048]{1,0:T(8,128)(2,1)S(1)}, bf16[32,2048]{1,0:T(8,128)(2,1)S(1)}, u32[]{:S(2)}, u32[]{:S(2)}) collective-permute-start(bf16[32,2048]{1,0:T(8,128)(2,1)S(1)} %get-tuple-element.23), channel_id=1, source_target_pairs={{0,8},{8,16},{16,24},{24,0},{1,9},{9,17},{17,25},{25,1},{2,10},{10... | collective-permute-start | bytes 393224 | tf_op jit(solution)/shard_map/ppermute | solution.py:23
  11.1 8.3 %collective-permute-start.1 = (bf16[32,2048]{1,0:T(8,128)(2,1)S(1)}, bf16[32,2048]{1,0:T(8,128)(2,1)S(1)}, u32[]{:S(2)}, u32[]{:S(2)}) collective-permute-start(bf16[32,2048]{1,0:T(8,128)(2,1)S(1)} %get-tuple-element.26), channel_id=1, source_target_pairs={{0,16},{8,24},{16,0},{24,8},{1,17},{9,25},{17,1},{25,9},{2,18},{10... | collective-permute-start | bytes 393224 | tf_op jit(solution)/shard_map/ppermute | solution.py:23
  13.7 5.7 %collective-permute-start.2 = (bf16[32,2048]{1,0:T(8,128)(2,1)S(1)}, bf16[32,2048]{1,0:T(8,128)(2,1)S(1)}, u32[]{:S(2)}, u32[]{:S(2)}) collective-permute-start(bf16[32,2048]{1,0:T(8,128)(2,1)S(1)} %get-tuple-element.27), channel_id=1, source_target_pairs={{0,24},{8,0},{16,8},{24,16},{1,25},{9,1},{17,9},{25,17},{2,26},{10... | collective-permute-start | bytes 393224 | tf_op jit(solution)/shard_map/ppermute | solution.py:23
  19.5 0.8 copy-start.5
  21.5 7.2 %collective-permute-start.3 = (bf16[256,256]{1,0:T(8,128)(2,1)S(1)}, bf16[256,256]{1,0:T(8,128)(2,1)S(1)}, u32[]{:S(2)}, u32[]{:S(2)}) collective-permute-start(bf16[256,256]{1,0:T(8,128)(2,1)S(1)} %get-tuple-element.28), channel_id=1, source_target_pairs={{0,8},{8,16},{16,24},{24,0},{1,9},{9,17},{17,25},{25,1},{2,10},{10... | collective-permute-start | bytes 393224 | tf_op jit(solution)/shard_map/ppermute | solution.py:23
  21.6 7.1 %collective-permute-start.4 = (bf16[256,256]{1,0:T(8,128)(2,1)S(1)}, bf16[256,256]{1,0:T(8,128)(2,1)S(1)}, u32[]{:S(2)}, u32[]{:S(2)}) collective-permute-start(bf16[256,256]{1,0:T(8,128)(2,1)S(1)} %get-tuple-element.29), channel_id=1, source_target_pairs={{0,16},{8,24},{16,0},{24,8},{1,17},{9,25},{17,1},{25,9},{2,18},{10... | collective-permute-start | bytes 393224 | tf_op jit(solution)/shard_map/ppermute | solution.py:23
  23.7 5.4 %collective-permute-start.5 = (bf16[256,256]{1,0:T(8,128)(2,1)S(1)}, bf16[256,256]{1,0:T(8,128)(2,1)S(1)}, u32[]{:S(2)}, u32[]{:S(2)}) collective-permute-start(bf16[256,256]{1,0:T(8,128)(2,1)S(1)} %get-tuple-element.30), channel_id=1, source_target_pairs={{0,24},{8,0},{16,8},{24,16},{1,25},{9,1},{17,9},{25,17},{2,26},{10... | collective-permute-start | bytes 393224 | tf_op jit(solution)/shard_map/ppermute | solution.py:23
  29.1 50.7 %all-to-all-start = ((bf16[4,4,64,2048]{3,2,1,0:T(8,128)(2,1)}), bf16[4,4,64,2048]{3,2,1,0:T(8,128)(2,1)}, u32[]{:S(2)}, u32[]{:S(2)}) async-start(bf16[4,4,64,2048]{3,2,1,0:T(8,128)(2,1)} %cut_parts.1), calls=%async_computation | async-start | bytes 8388608 | tf_op jit(solution)/shard_map/all_to_all | solution.py:15
  34.0 105.7 %reduce-scatter.2.cloned.1.call-start = ((), (), s32[]{:S(2)}) async-start(), calls=%async_computation.5 | async-start | bytes 1179648 | tf_op jit(solution)/shard_map/reduce_scatter | solution.py:336
  34.1 12.6 %collective-permute-start.6 = (bf16[256,1024]{1,0:T(8,128)(2,1)S(1)}, bf16[256,1024]{1,0:T(8,128)(2,1)S(1)}, u32[]{:S(2)}, u32[]{:S(2)}) collective-permute-start(bf16[256,1024]{1,0:T(8,128)(2,1)S(1)} %pad_maximum_fusion.refs_0_), channel_id=1, source_target_pairs={{0,64},{64,128},{128,192},{192,0},{1,65},{65,129},{129,193},{193,1... | collective-permute-start | bytes 1572872 | tf_op jit(solution)/shard_map/ppermute | solution.py:23
  36.0 23.1 %collective-permute-start.7 = (bf16[256,1024]{1,0:T(8,128)(2,1)S(1)}, bf16[256,1024]{1,0:T(8,128)(2,1)S(1)}, u32[]{:S(2)}, u32[]{:S(2)}) collective-permute-start(bf16[256,1024]{1,0:T(8,128)(2,1)S(1)} %pad_maximum_fusion.refs_0_), channel_id=1, source_target_pairs={{0,128},{64,192},{128,0},{192,64},{1,129},{65,193},{129,1},{193,65... | collective-permute-start | bytes 1572872 | tf_op jit(solution)/shard_map/ppermute | solution.py:23
  38.5 22.1 %collective-permute-start.8 = (bf16[256,1024]{1,0:T(8,128)(2,1)S(1)}, bf16[256,1024]{1,0:T(8,128)(2,1)S(1)}, u32[]{:S(2)}, u32[]{:S(2)}) collective-permute-start(bf16[256,1024]{1,0:T(8,128)(2,1)S(1)} %pad_maximum_fusion.refs_0_), channel_id=1, source_target_pairs={{0,192},{64,0},{128,64},{192,128},{1,193},{65,1},{129,65},{193,129... | collective-permute-start | bytes 1572872 | tf_op jit(solution)/shard_map/ppermute | solution.py:23
  61.2 35.8 %collective-permute-start.9 = (bf16[1024,1024]{1,0:T(8,128)(2,1)S(1)}, bf16[1024,1024]{1,0:T(8,128)(2,1)}, u32[]{:S(2)}, u32[]{:S(2)}) collective-permute-start(bf16[1024,1024]{1,0:T(8,128)(2,1)S(1)} %order_parts.1.mine_ref), channel_id=1, source_target_pairs={{0,32},{32,0},{1,33},{33,1},{2,34},{34,2},{3,35},{35,3},{4,36},{36... | collective-permute-start | bytes 6291464 | tf_op jit(solution)/shard_map/ppermute | solution.py:23
  79.8 2.2 %copy-start.1 = (bf16[1024,2048]{1,0:T(8,128)(2,1)S(1)}, bf16[1024,2048]{1,0:T(8,128)(2,1)}, u32[]{:S(2)}) copy-start(bf16[1024,2048]{1,0:T(8,128)(2,1)} %all-gather.2.cloned.1.call-done) | copy-start | bytes 12582916
  86.7 23.3 %all-to-all-start.1 = ((bf16[32,32,256]{2,1,0:T(8,128)(2,1)}), bf16[32,32,256]{2,1,0:T(8,128)(2,1)S(1)}, u32[]{:S(2)}, u32[]{:S(2)}) async-start(bf16[32,32,256]{2,1,0:T(8,128)(2,1)} %get-tuple-element.32), calls=%async_computation.1 | async-start | bytes 1048576 | tf_op jit(solution)/shard_map/all_to_all | solution.py:15
  97.0 2.2 %copy-start.2 = (bf16[1024,2048]{1,0:T(8,128)(2,1)S(1)}, bf16[1024,2048]{1,0:T(8,128)(2,1)}, u32[]{:S(2)}) copy-start(bf16[1024,2048]{1,0:T(8,128)(2,1)} %all-gather.2.cloned.1.call-done) | copy-start | bytes 12582916
  99.2 10.8 %copy-start.6 = (s32[32]{0:T(128)S(1)}, s32[32]{0:T(128)}, u32[]{:S(2)}) copy-start(s32[32]{0:T(128)} %param.13) | copy-start | bytes 388
  106.4 13.1 %collective-permute-start.10 = (bf16[1024,256]{1,0:T(8,128)(2,1)}, bf16[1024,256]{1,0:T(8,128)(2,1)S(1)}, u32[]{:S(2)}, u32[]{:S(2)}) collective-permute-start(bf16[1024,256]{1,0:T(8,128)(2,1)} %get-tuple-element.36), channel_id=1, source_target_pairs={{0,24},{8,0},{16,8},{24,16},{1,25},{9,1},{17,9},{25,17},{2,26},{10... | collective-permute-start | bytes 1572872 | tf_op jit(solution)/shard_map/ppermute | solution.py:23
  108.9 13.3 %collective-permute-start.11 = (bf16[1024,256]{1,0:T(8,128)(2,1)}, bf16[1024,256]{1,0:T(8,128)(2,1)S(1)}, u32[]{:S(2)}, u32[]{:S(2)}) collective-permute-start(bf16[1024,256]{1,0:T(8,128)(2,1)} %get-tuple-element.37), channel_id=1, source_target_pairs={{0,16},{8,24},{16,0},{24,8},{1,17},{9,25},{17,1},{25,9},{2,18},{10... | collective-permute-start | bytes 1572872 | tf_op jit(solution)/shard_map/ppermute | solution.py:23
  109.4 30.1 %collective-permute-start.12 = (bf16[1024,256]{1,0:T(8,128)(2,1)}, bf16[1024,256]{1,0:T(8,128)(2,1)S(1)}, u32[]{:S(2)}, u32[]{:S(2)}) collective-permute-start(bf16[1024,256]{1,0:T(8,128)(2,1)} %get-tuple-element.38), channel_id=1, source_target_pairs={{0,8},{8,16},{16,24},{24,0},{1,9},{9,17},{17,25},{25,1},{2,10},{10... | collective-permute-start | bytes 1572872 | tf_op jit(solution)/shard_map/ppermute | solution.py:23
  111.0 28.7 %all-to-all-start.2 = ((bf16[32,32,128]{2,1,0:T(8,128)(2,1)}), bf16[32,32,128]{2,1,0:T(8,128)(2,1)S(1)}, u32[]{:S(2)}, u32[]{:S(2)}) async-start(bf16[32,32,128]{2,1,0:T(8,128)(2,1)} %lower_parts.1), calls=%async_computation.2 | async-start | bytes 524288 | tf_op jit(solution)/shard_map/all_to_all | solution.py:15
  139.7 0.9 copy-start.4
Sparse Core Ops, SparseCore 0:
  20.4 58.0 all-gather.1
  86.8 42.7 reduce-scatter.1

commit v6 on v4

--- a/solution.py
+++ b/solution.py
@@ -309,7 +309,7 @@
     ]
     piece = [shift(after(block, sent[1]), "y", ny, d) if d else block for d, block in enumerate(piece)]
 
-    pools = swap(after(pools, far, *piece), "y").reshape(ny * 2 * held, rank, part)
+    pools = swap(after(pools, far, piece[1]), "y").reshape(ny * 2 * held, rank, part)
     piece = jnp.concatenate(piece, axis=1)
 
     pool_rows = slot_of[requested]

time: 150 us -> 182 us (1.21)
  waiting for transfers between devices: 61.4 us -> 93.4 us
    ppermute x13, waiting for transfers between devices: 45.5 us -> 87.8 us  [shift(): lax.ppermute(value, axis, [(i, (i + by) % size) for i in range(size)])]
    all_to_all x3, waiting for transfers between devices: 15.9 us -> 5.5 us  [swap(): return lax.all_to_all(value, axis, split_axis=0, concat_axis=0, tiled=True)]
  transfers between devices with their start and end apart: 18 -> 18, of which waited for: 10 -> 11; matrix products, arithmetic and copies ran while one was open for 1% -> 1% of each run, Pallas kernels for 11% -> 9%
where the time goes in v6:
time: 182 us; the launch traced here: 181 us
  waiting for transfers between devices  93.4 us (51%)
  starting transfers between devices  44.8 us (25%)
  Pallas kernels  19.7 us (11%)
  between operations  13.7 us (8%)
  local copies, waits for them, and re-layouts  9 us (5%)
    ppermute x13, waiting for transfers between devices, shift(): lax.ppermute(value, axis, [(i, (i + by) % size) for i in range(size)])  87.8 us
    all_to_all x3, starting transfers between devices, swap(): return lax.all_to_all(value, axis, split_axis=0, concat_axis=0, tiled=True)  24.8 us
    ppermute x13, starting transfers between devices, shift(): lax.ppermute(value, axis, [(i, (i + by) % size) for i in range(size)])  20 us
    pallas_call x1, Pallas kernels, base_parts(): pl.pallas_call(base_kernel, out_shape=[jax.ShapeDtypeStruct((ny * nz * ro...  7.16 us
    unnamed x17, local copies, waits for them, and re-layouts  7.14 us
    all_to_all x3, waiting for transfers between devices, swap(): return lax.all_to_all(value, axis, split_axis=0, concat_axis=0, tiled=True)  5.5 us
    pallas_call x1, Pallas kernels, local_parts(): pl.pallas_call(local_kernel, out_shape=[jax.ShapeDtypeStruct((ny * nz, ro...  4.78 us
    pallas_call x1, Pallas kernels, cut_parts(): pl.pallas_call(cut_kernel, out_shape=jax.ShapeDtypeStruct((count, len(poo...  3.69 us
  transfers between devices with their start and end apart: 18, of which 11 were waited for; matrix products, arithmetic and copies ran while one was open for 1% of the time, Pallas kernels for 9%

profile of v6, /device:TPU:1, one launch (start us, length us, event | category | flops | bytes accessed | tf_op | source)
XLA Modules:
  0.0 181.5 jit_solution(243736302328498237)
XLA Ops:
  6.5 0.0 copy-start
  6.5 0.0 all-gather.2.cloned.1.call-start
  6.5 0.7 compare_select_fusion
  7.3 0.0 copy-start.3
  7.3 1.0 copy-done.3
  8.3 0.6 send_parts.1
  8.9 2.2 %collective-permute-start = (bf16[32,2048]{1,0:T(8,128)(2,1)S(1)}, bf16[32,2048]{1,0:T(8,128)(2,1)S(1)}, u32[]{:S(2)}, u32[]{:S(2)}) collective-permute-start(bf16[32,2048]{1,0:T(8,128)(2,1)S(1)} %get-tuple-element.23), channel_id=1, source_target_pairs={{0,8},{8,16},{16,24},{24,0},{1,9},{9,17},{17,25},{25,1},{2,10},{10... | collective-permute-start | bytes 393224 | tf_op jit(solution)/shard_map/ppermute | solution.py:23
  11.1 2.6 %collective-permute-start.1 = (bf16[32,2048]{1,0:T(8,128)(2,1)S(1)}, bf16[32,2048]{1,0:T(8,128)(2,1)S(1)}, u32[]{:S(2)}, u32[]{:S(2)}) collective-permute-start(bf16[32,2048]{1,0:T(8,128)(2,1)S(1)} %get-tuple-element.26), channel_id=1, source_target_pairs={{0,16},{8,24},{16,0},{24,8},{1,17},{9,25},{17,1},{25,9},{2,18},{10... | collective-permute-start | bytes 393224 | tf_op jit(solution)/shard_map/ppermute | solution.py:23
  13.7 1.1 collective-permute-start.2
  14.8 3.7 %cut_parts.1 = bf16[4,4,64,2048]{3,2,1,0:T(8,128)(2,1)} custom-call(bf16[2,64,8192]{2,1,0:T(8,128)(2,1)} %refs_0_.1, bf16[2,64,8192]{2,1,0:T(8,128)(2,1)} %refs_1_), custom_call_target="tpu_custom_call" | custom-call | bytes 8388608 | tf_op jit(solution)/shard_map/cut_parts/pallas_call | solution.py:74
  18.5 0.0 collective-permute-done
  18.6 0.9 collective-permute-done.1
  19.5 0.0 collective-permute-done.2
  19.5 0.0 copy-start.5
  19.5 0.8 copy-done.5
  20.3 0.0 all-gather.2.cloned.1.call-update
  20.4 1.1 dynamic-slice_bitcast_fusion.2
  21.5 0.1 collective-permute-start.3
  21.6 5.0 %collective-permute-done.3 = bf16[256,256]{1,0:T(8,128)(2,1)S(1)} collective-permute-done((bf16[256,256]{1,0:T(8,128)(2,1)S(1)}, bf16[256,256]{1,0:T(8,128)(2,1)S(1)}, u32[]{:S(2)}, u32[]{:S(2)}) %collective-permute-start.3) | collective-permute-done | bytes 131104 | tf_op jit(solution)/shard_map/ppermute | solution.py:23
  26.6 4.9 %all-to-all-start = ((bf16[4,4,64,2048]{3,2,1,0:T(8,128)(2,1)}), bf16[4,4,64,2048]{3,2,1,0:T(8,128)(2,1)}, u32[]{:S(2)}, u32[]{:S(2)}) async-start(bf16[4,4,64,2048]{3,2,1,0:T(8,128)(2,1)} %cut_parts.1), calls=%async_computation | async-start | bytes 8388608 | tf_op jit(solution)/shard_map/all_to_all | solution.py:15
  31.5 0.0 reduce-scatter.2.cloned.1.call-start
  31.6 2.6 %collective-permute-start.5 = (bf16[256,256]{1,0:T(8,128)(2,1)S(1)}, bf16[256,256]{1,0:T(8,128)(2,1)S(1)}, u32[]{:S(2)}, u32[]{:S(2)}) collective-permute-start(bf16[256,256]{1,0:T(8,128)(2,1)S(1)} %get-tuple-element.34), channel_id=1, source_target_pairs={{0,24},{8,0},{16,8},{24,16},{1,25},{9,1},{17,9},{25,17},{2,26},{10... | collective-permute-start | bytes 393224 | tf_op jit(solution)/shard_map/ppermute | solution.py:23
  34.2 0.6 collective-permute-start.4
  34.7 44.1 %collective-permute-done.5 = bf16[256,256]{1,0:T(8,128)(2,1)S(1)} collective-permute-done((bf16[256,256]{1,0:T(8,128)(2,1)S(1)}, bf16[256,256]{1,0:T(8,128)(2,1)S(1)}, u32[]{:S(2)}, u32[]{:S(2)}) %collective-permute-start.5) | collective-permute-done | bytes 131104 | tf_op jit(solution)/shard_map/ppermute | solution.py:23
  78.8 1.5 collective-permute-done.4
  80.3 0.1 pad_maximum_fusion.refs_0_
  80.3 1.5 collective-permute-start.6
  81.9 2.5 %collective-permute-start.7 = (bf16[256,1024]{1,0:T(8,128)(2,1)S(1)}, bf16[256,1024]{1,0:T(8,128)(2,1)S(1)}, u32[]{:S(2)}, u32[]{:S(2)}) collective-permute-start(bf16[256,1024]{1,0:T(8,128)(2,1)S(1)} %pad_maximum_fusion.refs_0_), channel_id=1, source_target_pairs={{0,128},{64,192},{128,0},{192,64},{1,129},{65,193},{129,1},{193,65... | collective-permute-start | bytes 1572872 | tf_op jit(solution)/shard_map/ppermute | solution.py:23
  84.3 1.2 collective-permute-start.8
  85.5 5.9 %collective-permute-done.6.refs_1_ = bf16[256,1024]{1,0:T(8,128)(2,1)S(1)} collective-permute-done((bf16[256,1024]{1,0:T(8,128)(2,1)S(1)}, bf16[256,1024]{1,0:T(8,128)(2,1)S(1)}, u32[]{:S(2)}, u32[]{:S(2)}) %collective-permute-start.6) | collective-permute-done | bytes 524320 | tf_op jit(solution)/shard_map/ppermute | solution.py:23
  91.4 12.6 %collective-permute-done.7.refs_2_ = bf16[256,1024]{1,0:T(8,128)(2,1)S(1)} collective-permute-done((bf16[256,1024]{1,0:T(8,128)(2,1)S(1)}, bf16[256,1024]{1,0:T(8,128)(2,1)S(1)}, u32[]{:S(2)}, u32[]{:S(2)}) %collective-permute-start.7) | collective-permute-done | bytes 524320 | tf_op jit(solution)/shard_map/ppermute | solution.py:23
  104.0 2.4 %collective-permute-done.8.refs_3_ = bf16[256,1024]{1,0:T(8,128)(2,1)S(1)} collective-permute-done((bf16[256,1024]{1,0:T(8,128)(2,1)S(1)}, bf16[256,1024]{1,0:T(8,128)(2,1)S(1)}, u32[]{:S(2)}, u32[]{:S(2)}) %collective-permute-start.8) | collective-permute-done | bytes 524320 | tf_op jit(solution)/shard_map/ppermute | solution.py:23
  106.4 0.7 order_parts.1.mine_ref
  107.1 2.1 %collective-permute-start.9 = (bf16[1024,1024]{1,0:T(8,128)(2,1)S(1)}, bf16[1024,1024]{1,0:T(8,128)(2,1)}, u32[]{:S(2)}, u32[]{:S(2)}) collective-permute-start(bf16[1024,1024]{1,0:T(8,128)(2,1)S(1)} %order_parts.1.mine_ref), channel_id=1, source_target_pairs={{0,32},{32,0},{1,33},{33,1},{2,34},{34,2},{3,35},{35,3},{4,36},{36... | collective-permute-start | bytes 6291464 | tf_op jit(solution)/shard_map/ppermute | solution.py:23
  109.2 0.0 copy-done
  109.2 0.6 gather_fusion
  109.9 0.1 pad_add_fusion.1.slot_ref
  110.0 0.0 all-to-all-done
  110.0 0.0 all-gather.2.cloned.1.call-done
  110.0 0.0 copy-start.1
  110.0 2.2 %copy-done.1 = bf16[1024,2048]{1,0:T(8,128)(2,1)S(1)} copy-done((bf16[1024,2048]{1,0:T(8,128)(2,1)S(1)}, bf16[1024,2048]{1,0:T(8,128)(2,1)}, u32[]{:S(2)}) %copy-start.1) | copy-done | bytes 4194328
  112.2 4.8 %local_parts.1 = (bf16[32,32,256]{2,1,0:T(8,128)(2,1)}, bf16[8,4,64,256]{3,2,1,0:T(8,128)(2,1)}) custom-call(s32[4]{0:T(128)S(1)} %get-tuple-element.32.place_ref, s32[4]{0:T(128)S(1)} %compare_convert_fusion.wanted_ref, s32[8]{0:T(128)S(1)} %pad_add_fusion.1.slot_ref, bf16[8,4,32,2048]{3,2,1,0:T(8,128)(2,1)S(1)} %bitcast.20, ...), custom_call_target="tpu_custom_call" | custom-call | flops 1073741824 | bytes 8388608 | tf_op jit(solution)/shard_map/local_parts/pallas_call | solution.py:165
  117.0 0.0 reduce-scatter.2.cloned.1.call-update
  117.0 12.0 %all-to-all-start.1 = ((bf16[32,32,256]{2,1,0:T(8,128)(2,1)}), bf16[32,32,256]{2,1,0:T(8,128)(2,1)S(1)}, u32[]{:S(2)}, u32[]{:S(2)}) async-start(bf16[32,32,256]{2,1,0:T(8,128)(2,1)} %get-tuple-element.30), calls=%async_computation.1 | async-start | bytes 1048576 | tf_op jit(solution)/shard_map/all_to_all | solution.py:15
  129.1 0.0 collective-permute-done.9.other_ref
  129.1 0.0 copy-start.2
  129.1 2.2 %copy-done.2 = bf16[1024,2048]{1,0:T(8,128)(2,1)S(1)} copy-done((bf16[1024,2048]{1,0:T(8,128)(2,1)S(1)}, bf16[1024,2048]{1,0:T(8,128)(2,1)}, u32[]{:S(2)}) %copy-start.2) | copy-done | bytes 4194328
  131.3 0.0 copy-start.6
  131.3 7.2 %base_parts.1 = (bf16[1024,256]{1,0:T(8,128)(2,1)S(1)}, bf16[1024,256]{1,0:T(8,128)(2,1)}, bf16[1024,256]{1,0:T(8,128)(2,1)}, bf16[1024,256]{1,0:T(8,128)(2,1)}) custom-call(s32[4]{0:T(128)S(1)} %get-tuple-element.32.place_ref, bf16[8,4,32,2048]{3,2,1,0:T(8,128)(2,1)S(1)} %bitcast.21, bf16[1024,1024]{1,0:T(8,128)(2,1)S(1)} %order_parts.1.mine_ref, ...), custom_call_target="tpu_custom_call" | custom-call | flops 4294967296 | bytes 10485760 | tf_op jit(solution)/shard_map/base_parts/pallas_call | solution.py:207
  138.4 2.5 %collective-permute-start.10 = (bf16[1024,256]{1,0:T(8,128)(2,1)}, bf16[1024,256]{1,0:T(8,128)(2,1)S(1)}, u32[]{:S(2)}, u32[]{:S(2)}) collective-permute-start(bf16[1024,256]{1,0:T(8,128)(2,1)} %get-tuple-element.36), channel_id=1, source_target_pairs={{0,24},{8,0},{16,8},{24,16},{1,25},{9,1},{17,9},{25,17},{2,26},{10... | collective-permute-start | bytes 1572872 | tf_op jit(solution)/shard_map/ppermute | solution.py:23
  140.9 0.5 collective-permute-start.11
  141.5 0.6 collective-permute-start.12
  142.1 5.3 %all-to-all-done.1.parts_ref = bf16[32,32,256]{2,1,0:T(8,128)(2,1)S(1)} async-done(((bf16[32,32,256]{2,1,0:T(8,128)(2,1)}), bf16[32,32,256]{2,1,0:T(8,128)(2,1)S(1)}, u32[]{:S(2)}, u32[]{:S(2)}) %all-to-all-start.1) | async-done | bytes 524320 | tf_op jit(solution)/shard_map/all_to_all | solution.py:15
  147.4 0.0 copy-done.6
  147.4 0.1 broadcast_in_dim.10.ids_ref
  147.5 0.9 lower_parts.1
  148.3 7.9 %all-to-all-start.2 = ((bf16[32,32,128]{2,1,0:T(8,128)(2,1)}), bf16[32,32,128]{2,1,0:T(8,128)(2,1)S(1)}, u32[]{:S(2)}, u32[]{:S(2)}) async-start(bf16[32,32,128]{2,1,0:T(8,128)(2,1)} %lower_parts.1), calls=%async_computation.2 | async-start | bytes 524288 | tf_op jit(solution)/shard_map/all_to_all | solution.py:15
  156.2 11.8 %collective-permute-done.10 = bf16[1024,256]{1,0:T(8,128)(2,1)S(1)} collective-permute-done((bf16[1024,256]{1,0:T(8,128)(2,1)}, bf16[1024,256]{1,0:T(8,128)(2,1)S(1)}, u32[]{:S(2)}, u32[]{:S(2)}) %collective-permute-start.10) | collective-permute-done | bytes 524320 | tf_op jit(solution)/shard_map/ppermute | solution.py:23
  168.1 0.0 collective-permute-done.11
  168.1 3.6 %collective-permute-done.12 = bf16[1024,256]{1,0:T(8,128)(2,1)S(1)} collective-permute-done((bf16[1024,256]{1,0:T(8,128)(2,1)}, bf16[1024,256]{1,0:T(8,128)(2,1)S(1)}, u32[]{:S(2)}, u32[]{:S(2)}) %collective-permute-start.12) | collective-permute-done | bytes 524320 | tf_op jit(solution)/shard_map/ppermute | solution.py:23
  171.7 0.2 all-to-all-done.2.low_ref
  171.8 0.0 reduce-scatter.2.cloned.1.call-done
  171.8 0.9 copy-done.4
  172.7 1.9 %final_rows.1 = bf16[1024,256]{1,0:T(8,128)(2,1)} custom-call(s32[4]{0:T(128)S(1)} %get-tuple-element.32.place_ref, bf16[32,32,128]{2,1,0:T(8,128)(2,1)S(1)} %all-to-all-done.2.low_ref, bf16[4,64,256]{2,1,0:T(8,128)(2,1)S(1)} %bitcast.26, bf16[8,4,32,256]{3,2,1,0:T(8,128)(2,1)S(1)} %bitcast.22, bf16[8,4,32,256]{3,2,1,0:T(8,128)(2,1)S(1)} %bitcast.23, ...), custom_call_target="tpu_custom_call" | custom-call | flops 134217728 | bytes 4194304 | tf_op jit(solution)/shard_map/final_rows/pallas_call | solution.py:275
  (8 shorter events, 0.1 us)
Async XLA Ops:
  6.5 102.7 %copy-start = (s32[64]{0:T(128)S(1)}, s32[64]{0:T(128)}, u32[]{:S(2)}) copy-start(s32[64]{0:T(128)} %param.11) | copy-start | bytes 772
  6.5 103.5 %all-gather.2.cloned.1.call-start = ((), (), s32[]{:S(2)}) async-start(), calls=%async_computation.4 | async-start | bytes 4718592 | tf_op jit(solution)/shard_map/all_gather | solution.py:303
  7.3 1.0 copy-start.3
  8.9 9.6 %collective-permute-start = (bf16[32,2048]{1,0:T(8,128)(2,1)S(1)}, bf16[32,2048]{1,0:T(8,128)(2,1)S(1)}, u32[]{:S(2)}, u32[]{:S(2)}) collective-permute-start(bf16[32,2048]{1,0:T(8,128)(2,1)S(1)} %get-tuple-element.23), channel_id=1, source_target_pairs={{0,8},{8,16},{16,24},{24,0},{1,9},{9,17},{17,25},{25,1},{2,10},{10... | collective-permute-start | bytes 393224 | tf_op jit(solution)/shard_map/ppermute | solution.py:23
  11.1 8.3 %collective-permute-start.1 = (bf16[32,2048]{1,0:T(8,128)(2,1)S(1)}, bf16[32,2048]{1,0:T(8,128)(2,1)S(1)}, u32[]{:S(2)}, u32[]{:S(2)}) collective-permute-start(bf16[32,2048]{1,0:T(8,128)(2,1)S(1)} %get-tuple-element.26), channel_id=1, source_target_pairs={{0,16},{8,24},{16,0},{24,8},{1,17},{9,25},{17,1},{25,9},{2,18},{10... | collective-permute-start | bytes 393224 | tf_op jit(solution)/shard_map/ppermute | solution.py:23
  13.7 5.7 %collective-permute-start.2 = (bf16[32,2048]{1,0:T(8,128)(2,1)S(1)}, bf16[32,2048]{1,0:T(8,128)(2,1)S(1)}, u32[]{:S(2)}, u32[]{:S(2)}) collective-permute-start(bf16[32,2048]{1,0:T(8,128)(2,1)S(1)} %get-tuple-element.27), channel_id=1, source_target_pairs={{0,24},{8,0},{16,8},{24,16},{1,25},{9,1},{17,9},{25,17},{2,26},{10... | collective-permute-start | bytes 393224 | tf_op jit(solution)/shard_map/ppermute | solution.py:23
  19.5 0.8 copy-start.5
  21.5 5.1 %collective-permute-start.3 = (bf16[256,256]{1,0:T(8,128)(2,1)S(1)}, bf16[256,256]{1,0:T(8,128)(2,1)S(1)}, u32[]{:S(2)}, u32[]{:S(2)}) collective-permute-start(bf16[256,256]{1,0:T(8,128)(2,1)S(1)} %get-tuple-element.28), channel_id=1, source_target_pairs={{0,8},{8,16},{16,24},{24,0},{1,9},{9,17},{17,25},{25,1},{2,10},{10... | collective-permute-start | bytes 393224 | tf_op jit(solution)/shard_map/ppermute | solution.py:23
  26.6 83.4 %all-to-all-start = ((bf16[4,4,64,2048]{3,2,1,0:T(8,128)(2,1)}), bf16[4,4,64,2048]{3,2,1,0:T(8,128)(2,1)}, u32[]{:S(2)}, u32[]{:S(2)}) async-start(bf16[4,4,64,2048]{3,2,1,0:T(8,128)(2,1)} %cut_parts.1), calls=%async_computation | async-start | bytes 8388608 | tf_op jit(solution)/shard_map/all_to_all | solution.py:15
  31.5 140.3 %reduce-scatter.2.cloned.1.call-start = ((), (), s32[]{:S(2)}) async-start(), calls=%async_computation.5 | async-start | bytes 1179648 | tf_op jit(solution)/shard_map/reduce_scatter | solution.py:326
  31.6 47.2 %collective-permute-start.5 = (bf16[256,256]{1,0:T(8,128)(2,1)S(1)}, bf16[256,256]{1,0:T(8,128)(2,1)S(1)}, u32[]{:S(2)}, u32[]{:S(2)}) collective-permute-start(bf16[256,256]{1,0:T(8,128)(2,1)S(1)} %get-tuple-element.34), channel_id=1, source_target_pairs={{0,24},{8,0},{16,8},{24,16},{1,25},{9,1},{17,9},{25,17},{2,26},{10... | collective-permute-start | bytes 393224 | tf_op jit(solution)/shard_map/ppermute | solution.py:23
  34.2 46.1 %collective-permute-start.4 = (bf16[256,256]{1,0:T(8,128)(2,1)S(1)}, bf16[256,256]{1,0:T(8,128)(2,1)S(1)}, u32[]{:S(2)}, u32[]{:S(2)}) collective-permute-start(bf16[256,256]{1,0:T(8,128)(2,1)S(1)} %get-tuple-element.33), channel_id=1, source_target_pairs={{0,16},{8,24},{16,0},{24,8},{1,17},{9,25},{17,1},{25,9},{2,18},{10... | collective-permute-start | bytes 393224 | tf_op jit(solution)/shard_map/ppermute | solution.py:23
  80.3 11.1 %collective-permute-start.6 = (bf16[256,1024]{1,0:T(8,128)(2,1)S(1)}, bf16[256,1024]{1,0:T(8,128)(2,1)S(1)}, u32[]{:S(2)}, u32[]{:S(2)}) collective-permute-start(bf16[256,1024]{1,0:T(8,128)(2,1)S(1)} %pad_maximum_fusion.refs_0_), channel_id=1, source_target_pairs={{0,64},{64,128},{128,192},{192,0},{1,65},{65,129},{129,193},{193,1... | collective-permute-start | bytes 1572872 | tf_op jit(solution)/shard_map/ppermute | solution.py:23
  81.9 22.1 %collective-permute-start.7 = (bf16[256,1024]{1,0:T(8,128)(2,1)S(1)}, bf16[256,1024]{1,0:T(8,128)(2,1)S(1)}, u32[]{:S(2)}, u32[]{:S(2)}) collective-permute-start(bf16[256,1024]{1,0:T(8,128)(2,1)S(1)} %pad_maximum_fusion.refs_0_), channel_id=1, source_target_pairs={{0,128},{64,192},{128,0},{192,64},{1,129},{65,193},{129,1},{193,65... | collective-permute-start | bytes 1572872 | tf_op jit(solution)/shard_map/ppermute | solution.py:23
  84.3 22.1 %collective-permute-start.8 = (bf16[256,1024]{1,0:T(8,128)(2,1)S(1)}, bf16[256,1024]{1,0:T(8,128)(2,1)S(1)}, u32[]{:S(2)}, u32[]{:S(2)}) collective-permute-start(bf16[256,1024]{1,0:T(8,128)(2,1)S(1)} %pad_maximum_fusion.refs_0_), channel_id=1, source_target_pairs={{0,192},{64,0},{128,64},{192,128},{1,193},{65,1},{129,65},{193,129... | collective-permute-start | bytes 1572872 | tf_op jit(solution)/shard_map/ppermute | solution.py:23
  107.1 22.0 %collective-permute-start.9 = (bf16[1024,1024]{1,0:T(8,128)(2,1)S(1)}, bf16[1024,1024]{1,0:T(8,128)(2,1)}, u32[]{:S(2)}, u32[]{:S(2)}) collective-permute-start(bf16[1024,1024]{1,0:T(8,128)(2,1)S(1)} %order_parts.1.mine_ref), channel_id=1, source_target_pairs={{0,32},{32,0},{1,33},{33,1},{2,34},{34,2},{3,35},{35,3},{4,36},{36... | collective-permute-start | bytes 6291464 | tf_op jit(solution)/shard_map/ppermute | solution.py:23
  110.0 2.2 %copy-start.1 = (bf16[1024,2048]{1,0:T(8,128)(2,1)S(1)}, bf16[1024,2048]{1,0:T(8,128)(2,1)}, u32[]{:S(2)}) copy-start(bf16[1024,2048]{1,0:T(8,128)(2,1)} %all-gather.2.cloned.1.call-done) | copy-start | bytes 12582916
  117.0 30.4 %all-to-all-start.1 = ((bf16[32,32,256]{2,1,0:T(8,128)(2,1)}), bf16[32,32,256]{2,1,0:T(8,128)(2,1)S(1)}, u32[]{:S(2)}, u32[]{:S(2)}) async-start(bf16[32,32,256]{2,1,0:T(8,128)(2,1)} %get-tuple-element.30), calls=%async_computation.1 | async-start | bytes 1048576 | tf_op jit(solution)/shard_map/all_to_all | solution.py:15
  129.1 2.2 %copy-start.2 = (bf16[1024,2048]{1,0:T(8,128)(2,1)S(1)}, bf16[1024,2048]{1,0:T(8,128)(2,1)}, u32[]{:S(2)}) copy-start(bf16[1024,2048]{1,0:T(8,128)(2,1)} %all-gather.2.cloned.1.call-done) | copy-start | bytes 12582916
  131.3 16.1 %copy-start.6 = (s32[32]{0:T(128)S(1)}, s32[32]{0:T(128)}, u32[]{:S(2)}) copy-start(s32[32]{0:T(128)} %param.13) | copy-start | bytes 388
  138.4 29.6 %collective-permute-start.10 = (bf16[1024,256]{1,0:T(8,128)(2,1)}, bf16[1024,256]{1,0:T(8,128)(2,1)S(1)}, u32[]{:S(2)}, u32[]{:S(2)}) collective-permute-start(bf16[1024,256]{1,0:T(8,128)(2,1)} %get-tuple-element.36), channel_id=1, source_target_pairs={{0,24},{8,0},{16,8},{24,16},{1,25},{9,1},{17,9},{25,17},{2,26},{10... | collective-permute-start | bytes 1572872 | tf_op jit(solution)/shard_map/ppermute | solution.py:23
  140.9 27.1 %collective-permute-start.11 = (bf16[1024,256]{1,0:T(8,128)(2,1)}, bf16[1024,256]{1,0:T(8,128)(2,1)S(1)}, u32[]{:S(2)}, u32[]{:S(2)}) collective-permute-start(bf16[1024,256]{1,0:T(8,128)(2,1)} %get-tuple-element.37), channel_id=1, source_target_pairs={{0,16},{8,24},{16,0},{24,8},{1,17},{9,25},{17,1},{25,9},{2,18},{10... | collective-permute-start | bytes 1572872 | tf_op jit(solution)/shard_map/ppermute | solution.py:23
  141.5 30.2 %collective-permute-start.12 = (bf16[1024,256]{1,0:T(8,128)(2,1)}, bf16[1024,256]{1,0:T(8,128)(2,1)S(1)}, u32[]{:S(2)}, u32[]{:S(2)}) collective-permute-start(bf16[1024,256]{1,0:T(8,128)(2,1)} %get-tuple-element.38), channel_id=1, source_target_pairs={{0,8},{8,16},{16,24},{24,0},{1,9},{9,17},{17,25},{25,1},{2,10},{10... | collective-permute-start | bytes 1572872 | tf_op jit(solution)/shard_map/ppermute | solution.py:23
  148.3 23.5 %all-to-all-start.2 = ((bf16[32,32,128]{2,1,0:T(8,128)(2,1)}), bf16[32,32,128]{2,1,0:T(8,128)(2,1)S(1)}, u32[]{:S(2)}, u32[]{:S(2)}) async-start(bf16[32,32,128]{2,1,0:T(8,128)(2,1)} %lower_parts.1), calls=%async_computation.2 | async-start | bytes 524288 | tf_op jit(solution)/shard_map/all_to_all | solution.py:15
  171.8 0.9 copy-start.4
Sparse Core Ops, SparseCore 0:
  20.4 58.0 all-gather.1
  117.1 43.9 reduce-scatter.1
